TPU v7x, 32 devices: a whole 2x2x4 slice. The times are simulated.
32 devices in a mesh: frame: 4 (over x, core), clip: 8 (over z, y).
Axes of the slice: x: 2, y: 2, z: 4, core: 2. Of those that a mesh axis runs over, the one named last changes fastest.
Arguments:
- tokens: bfloat16 [96, 320, 768], P('clip', 'frame'), may hold values from -6 to 6
- cotangent: bfloat16 [96, 320, 768], P('clip', 'frame'), may hold values from -6 to 6
- frame_count: int32 [96], P('clip'), may hold values from 1 to 8, as said below
- image_group: int32 [96, 8], P('clip', 'frame'), may hold values from 0 to 3
- keep_mask: int32 [96, 320], P('clip', 'frame'), may hold values from 0 to 1, as said below
- attn_norm_gain: bfloat16 [768], P(('frame', 'clip')), may hold values from 0.5 to 1.5
- attn_norm_bias: bfloat16 [768], P(('frame', 'clip')), may hold values from -1.5 to 1.5
- w_qkv: bfloat16 [768, 2304], P(('frame', 'clip')), may hold values from -0.21875 to 0.21875
- query_bias: bfloat16 [768], P(('frame', 'clip')), may hold values from -1.5 to 1.5
- value_bias: bfloat16 [768], P(('frame', 'clip')), may hold values from -1.5 to 1.5
- w_out: bfloat16 [768, 768], P(('frame', 'clip')), may hold values from -0.625 to 0.625
- out_bias: bfloat16 [768], P(('frame', 'clip')), may hold values from -1.5 to 1.5
- mlp_norm_gain: bfloat16 [768], P(('frame', 'clip')), may hold values from 0.5 to 1.5
- mlp_norm_bias: bfloat16 [768], P(('frame', 'clip')), may hold values from -1.5 to 1.5
- w_up: bfloat16 [768, 3072], P(('frame', 'clip')), may hold values from -0.21875 to 0.21875
- up_bias: bfloat16 [3072], P(('frame', 'clip')), may hold values from -1.5 to 1.5
- w_down: bfloat16 [3072, 768], P(('frame', 'clip')), may hold values from -0.109375 to 0.109375
- down_bias: bfloat16 [768], P(('frame', 'clip')), may hold values from -1.5 to 1.5
Outputs:
- output: bfloat16 [96, 320, 768], P('clip', 'frame')
- input_grad: float32 [96, 320, 768], P('clip', 'frame')
- grad_attn_norm_gain: float32 [768], P(('frame', 'clip'))
- grad_attn_norm_bias: float32 [768], P(('frame', 'clip'))
- grad_w_qkv: float32 [768, 2304], P(('frame', 'clip'))
- grad_query_bias: float32 [768], P(('frame', 'clip'))
- grad_value_bias: float32 [768], P(('frame', 'clip'))
- grad_w_out: float32 [768, 768], P(('frame', 'clip'))
- grad_out_bias: float32 [768], P(('frame', 'clip'))
- grad_mlp_norm_gain: float32 [768], P(('frame', 'clip'))
- grad_mlp_norm_bias: float32 [768], P(('frame', 'clip'))
- grad_w_up: float32 [768, 3072], P(('frame', 'clip'))
- grad_up_bias: float32 [3072], P(('frame', 'clip'))
- grad_w_down: float32 [3072, 768], P(('frame', 'clip'))
- grad_down_bias: float32 [768], P(('frame', 'clip'))
Inputs may be any that keep to these rules, and one draw needn't show every extreme that they name: The first frame_count frames of a slot are one clip, the others single images; in each aligned run of 12 slots one slot holds a clip of all 8 frames. `image_group`: entries of frames that belong to the clip are unused. `keep_mask`: every frame of every slot keeps at least one of its 40 positions.
All inputs are finite; a program needn't handle non-finite values.
Results may differ from a plain program's by a relative error of at most 0.012.
Values may be sent and summed in bfloat16 or wider, within the bound.
No kernel may reach another device: no remote copies, remote signals or barrier semaphores. Data moves between devices by JAX's collectives and lax.ppermute only.
A program may use at most 256 MiB of HBM per device.

v0:
```python
import jax
import jax.numpy as jnp
from jax import lax
from jax.experimental import pallas as pl
from jax.experimental.pallas import tpu as pltpu
from jax.sharding import Mesh
from jax.sharding import PartitionSpec as P

HEADS = 12
EPSILON = 1e-06
AXES = ("x", "core", "z", "y")
FRAME = ("x", "core")
ANY = pl.BlockSpec(memory_space=pl.ANY)


def index_of(sizes, at):
    value = 0
    for name, size in zip(AXES, sizes):
        value = value * size + at[name]
    return value


def swap(sizes, value, choose):
    pairs = []
    for x in range(sizes[0]):
        for core in range(sizes[1]):
            for z in range(sizes[2]):
                for y in range(sizes[3]):
                    at = {"x": x, "core": core, "z": z, "y": y}
                    pairs.append((index_of(sizes, at), index_of(sizes, choose(dict(at)))))
    return lax.ppermute(value, AXES, pairs)


def near_peer(at):
    at["y" if at["core"] else "x"] ^= 1
    return at


def far_peer(at):
    at["x" if at["core"] else "y"] ^= 1
    return at


def line_peer(bits):
    def choose(at):
        at["z"] ^= bits
        return at

    return choose


def core_peer(at):
    at["core"] ^= 1
    return at


def cell(core, x, y, near, far):
    return jnp.where(core == 0, x ^ near, x ^ far), jnp.where(core == 0, y ^ far, y ^ near)


def hold(values, after):
    def body(*refs):
        pass

    return pl.pallas_call(
        body,
        in_specs=[ANY] * (len(values) + len(after)),
        out_specs=[ANY] * len(values),
        out_shape=[jax.ShapeDtypeStruct(value.shape, value.dtype) for value in values],
        input_output_aliases={index: index for index in range(len(values))},
    )(*values, *after)


def copy_after(value, after):
    def body(in_ref, *refs):
        refs[-1][...] = in_ref[...]

    return pl.pallas_call(
        body,
        in_specs=[pl.BlockSpec(memory_space=pltpu.VMEM)] + [ANY] * len(after),
        out_specs=pl.BlockSpec(memory_space=pltpu.VMEM),
        out_shape=jax.ShapeDtypeStruct(value.shape, value.dtype),
    )(value, *after)


def columns_of(vectors, tail):
    rows = tail.shape[0]

    def body(*refs):
        out = refs[-1]
        lines = jnp.concatenate([ref[...].astype(jnp.float32) for ref in refs[:-2]], axis=0)
        lines = jnp.pad(lines, ((0, 0), (0, 128 - rows)))
        turned = jnp.pad(lines, ((0, 128 - lines.shape[0]), (0, 0))).T[:rows]
        out[...] = turned.astype(jnp.bfloat16)
        out[:, len(vectors) : len(vectors) + tail.shape[1]] = refs[-2][...]

    return pl.pallas_call(
        body, out_shape=jax.ShapeDtypeStruct((rows, 128), jnp.bfloat16)
    )(*[v.reshape(1, rows) for v in vectors], tail)


class Gather:
    def __init__(self, sizes, here, shard):
        self.sizes, self.here = sizes, here
        self.parts = [shard] + [swap(sizes, shard, line_peer(bits)) for bits in range(1, sizes[2])]

    def stack(self, after=()):
        parts = self.parts[:1] + list(hold(self.parts[1:], after)) if after else self.parts
        self.pieces = {(0, 0): jnp.stack(parts)}
        return [self.pieces[0, 0]]

    def second(self):
        column = self.pieces[0, 0]
        self.pieces[1, 0] = swap(self.sizes, column, near_peer)
        self.pieces[0, 1] = swap(self.sizes, column, far_peer)
        return [self.pieces[1, 0], self.pieces[0, 1]]

    def third(self, after=()):
        (self.pieces[1, 0],) = hold([self.pieces[1, 0]], [self.pieces[0, 1]] + list(after))
        self.pieces[1, 1] = swap(self.sizes, self.pieces[1, 0], far_peer)
        return [self.pieces[1, 1]]

    def whole(self, lines=0, after=()):
        if after:
            (self.pieces[1, 1],) = hold([self.pieces[1, 1]], after)
        keys = sorted(self.pieces)
        mine = [self.pieces[key] for key in keys]
        theirs = [swap(self.sizes, piece, core_peer) for piece in mine]
        count, rows, width = mine[0].shape
        total = 2 * len(keys)
        devices = self.sizes[0] * self.sizes[1] * self.sizes[2] * self.sizes[3]

        def body(here_ref, *refs):
            out, sems = refs[total], refs[-1]
            copies = []
            for side in range(2):
                core = here_ref[1] ^ side
                for index, (near, far) in enumerate(keys):
                    x, y = cell(core, here_ref[0], here_ref[3], near, far)
                    slot = side * len(keys) + index
                    for bits in range(count):
                        to = out.at[x, core, here_ref[2] ^ bits, y]
                        copies.append(pltpu.make_async_copy(refs[slot].at[bits], to, sems.at[slot * count + bits]))
            for copy in copies:
                copy.start()
            for copy in copies:
                copy.wait()
            if lines:
                tail = out[..., width - 128 :].astype(jnp.float32).reshape(devices * rows, 128)
                refs[total + 1][...] = tail.T[:lines]

        vmem = pl.BlockSpec(memory_space=pltpu.VMEM)
        shapes = [jax.ShapeDtypeStruct((self.sizes[0], 2, count, 2, rows, width), mine[0].dtype)]
        if lines:
            shapes.append(jax.ShapeDtypeStruct((lines, devices * rows), jnp.float32))
        results = pl.pallas_call(
            body,
            in_specs=[pl.BlockSpec(memory_space=pltpu.SMEM)] + [ANY] * total,
            out_specs=[vmem] * len(shapes),
            out_shape=shapes,
            scratch_shapes=[pltpu.SemaphoreType.DMA((total * count,))],
        )(self.here, *mine, *theirs)
        full = results[0].reshape(-1, width)
        return (full, results[1]) if lines else full


class Scatter:
    def __init__(self, sizes, here, sent, kept):
        self.sizes, self.here = sizes, here
        rows = kept.shape[1] // (sizes[2] * 2)
        shape = (sizes[0], sizes[2], 2, rows, kept.shape[2])
        self.terms = [kept.reshape(shape), swap(sizes, sent.reshape(shape), core_peer)]

    def hold(self, after):
        self.terms[0] = hold(self.terms[:1], after)[0]

    def add(self, cells):
        _, count, _, rows, width = self.terms[0].shape
        steps = len(cells)
        used = len(self.terms)
        near, first = cells[0]

        def body(here_ref, *refs):
            for bit in range(2):
                z = (here_ref[2] & 1) ^ bit
                value = refs[0][0, z, 0].astype(jnp.float32) + refs[1][0, z, 0].astype(jnp.float32)
                for ref in refs[2:used]:
                    value += ref[0, bit].astype(jnp.float32)
                refs[used][0, bit] = value.astype(jnp.bfloat16)

        def place(step, pair, here_ref):
            far = first if steps == 1 else step
            x, y = cell(here_ref[1], here_ref[0], here_ref[3], near, far)
            return x, (here_ref[2] >> 1) ^ pair, y, 0, 0

        plain = (1, 2, rows, width)
        specs = [pl.BlockSpec((1, 2, 1, rows, width), place)] * 2
        for term in self.terms[2:]:
            many = term.shape[0] > 1
            specs.append(
                pl.BlockSpec(plain, lambda i, b, h, m=many: ((first if steps == 1 else i) if m else 0, b, 0, 0))
            )
        return pl.pallas_call(
            body,
            grid_spec=pltpu.PrefetchScalarGridSpec(
                num_scalar_prefetch=1,
                grid=(steps, count // 2),
                in_specs=specs,
                out_specs=pl.BlockSpec(plain, lambda i, b, h: (i, b, 0, 0)),
            ),
            out_shape=jax.ShapeDtypeStruct((steps, count, rows, width), jnp.bfloat16),
            cost_estimate=pl.CostEstimate(
                flops=0, bytes_accessed=2 * steps * count * rows * width * (used + 1), transcendentals=0
            ),
        )(self.here, *self.terms)

    def second(self):
        self.sent = self.add([(1, 0), (1, 1)])
        self.terms.append(swap(self.sizes, self.sent, near_peer))

    def third(self):
        self.sent = self.add([(0, 1)])
        self.terms.append(swap(self.sizes, self.sent, far_peer))

    def fourth(self):
        value = self.add([(0, 0)])[0]
        self.sent = value
        self.parts = [value[0]]
        for bits in range(1, self.sizes[2]):
            self.parts.append(swap(self.sizes, value[bits], line_peer(bits)))

    def last(self):
        return sum(part.astype(jnp.float32) for part in self.parts)


ROOT_HALF = 0.7071067811865476
DENSITY = 0.3989422804014327
NT = (((1,), (1,)), ((), ()))
NN = (((1,), (0,)), ((), ()))
TN = (((0,), (0,)), ((), ()))


def dot(left, right, dims=NN):
    return lax.dot_general(left, right, dims, preferred_element_type=jnp.float32)


def normalize(values):
    center = values - jnp.mean(values, axis=-1, keepdims=True)
    spread = jnp.mean(center * center, axis=-1, keepdims=True)
    scale = lax.rsqrt(spread + EPSILON)
    return center * scale, scale


def gelu_parts(u):
    size = jnp.abs(u)
    bell = jnp.exp(-0.5 * (u * u))
    t = 1.0 / (1.0 + (0.3275911 * ROOT_HALF) * size)
    poly = t * (
        0.5 * 0.254829592
        + t * (0.5 * -0.284496736 + t * (0.5 * 1.421413741 + t * (0.5 * -1.453152027 + t * (0.5 * 1.061405429))))
    )
    tail = poly * bell
    value = jnp.maximum(u, 0.0) - size * tail
    slope = jnp.where(u > 0, 1.0 - tail, tail) + DENSITY * (u * bell)
    return value, slope


def add_rows(ref, values):
    total = jnp.sum(values, axis=0, keepdims=True)

    @pl.when(pl.program_id(0) == 0)
    def _():
        ref[...] = total

    @pl.when(pl.program_id(0) != 0)
    def _():
        ref[...] += total


def rows_of(refs):
    return jnp.concatenate([ref[0, : ref.shape[1] - 8] for ref in refs], axis=0)


def tags_of(refs):
    width = refs[0].shape[1] - 8
    rows = width * len(refs)
    column, line = None, None
    for index, ref in enumerate(refs):
        tags = ref[0, width:, :128]
        row = lax.broadcasted_iota(jnp.int32, (rows, 128), 0)
        place = lax.broadcasted_iota(jnp.int32, (rows, 128), 1) + index * width
        chosen = jnp.where(row == place, 1.0, 0.0).astype(jnp.bfloat16)
        one, other = dot(chosen, tags, NT), dot(tags, chosen, NT)
        column = one if column is None else column + one
        line = other if line is None else line + other
    return column[:, :1].astype(jnp.int32), line[:1].astype(jnp.int32)


def spread(refs, rows):
    width = refs[0].shape[1]
    for index, ref in enumerate(refs):
        ref[0] = rows[index * width : (index + 1) * width]


def attend_kernel(x_ref, w_ref, vec_ref, h_ref, qkv_ref, o_ref, p_ref, tag_ref):
    model = x_ref[0].shape[-1]
    head = model // HEADS
    n, _ = normalize(rows_of(x_ref).astype(jnp.float32))
    low = (n * vec_ref[0:1] + vec_ref[1:2]).astype(jnp.bfloat16)
    h_ref[0] = low
    q = dot(low, w_ref[:, :model]) + vec_ref[2:3]
    qkv_ref[0, :, :model] = q.astype(jnp.bfloat16) * jnp.bfloat16(head**-0.5)
    qkv_ref[0, :, model : 2 * model] = dot(low, w_ref[:, model : 2 * model]).astype(jnp.bfloat16)
    v = dot(low, w_ref[:, 2 * model : 3 * model]) + vec_ref[3:4]
    qkv_ref[0, :, 2 * model :] = v.astype(jnp.bfloat16)
    column, line = tags_of(x_ref)
    tag_ref[0] = column
    code = jnp.where(line & 1 == 1, line >> 1, -1)
    bias = jnp.where(column >> 1 == code, 0.0, -1e30)
    for i in range(HEADS):
        at = slice(i * head, (i + 1) * head)
        k_at = slice(model + i * head, model + (i + 1) * head)
        v_at = slice(2 * model + i * head, 2 * model + (i + 1) * head)
        s = dot(qkv_ref[0, :, at], qkv_ref[0, :, k_at], NT) + bias
        e = jnp.exp(s - jnp.max(s, axis=-1, keepdims=True))
        p = (e * (1.0 / jnp.sum(e, axis=-1, keepdims=True))).astype(jnp.bfloat16)
        p_ref[0, i] = p
        o_ref[0, :, at] = dot(p, qkv_ref[0, :, v_at]).astype(jnp.bfloat16)


def project_kernel(x_ref, o_ref, wo_ref, vec_ref, x2_ref, h2_ref):
    x2 = rows_of(x_ref).astype(jnp.float32) + (dot(o_ref[0], wo_ref[...]) + vec_ref[4:5])
    x2_ref[0] = x2
    n, _ = normalize(x2)
    h2_ref[0] = (n * vec_ref[5:6] + vec_ref[6:7]).astype(jnp.bfloat16)


def mlp(here, h2, cot, tags, rest, up_bias, shard):
    slots, length, model = h2.shape
    rows = slots * length
    hidden = up_bias.shape[1]
    steps = hidden // model
    peers = len(cot)
    chunk = model // peers
    bf, f32 = jnp.bfloat16, jnp.float32

    def body(here_ref, h2_ref, tag_ref, u_ref, b_ref, *refs):
        cot_refs = refs[:peers]
        down_refs = refs[peers : peers + steps]
        y_ref, gh_ref, gm_ref, sent_ref, kept_ref, gub_ref, gdb_ref, y_acc, gh_acc, ups, downs, sems = refs[
            peers + steps :
        ]
        step = pl.program_id(0)
        core = here_ref[1]

        @pl.when(step == 0)
        def _():
            total = jnp.zeros((1, model), f32)
            for slot in range(slots):
                keep = (tag_ref[slot] & 1).astype(f32)
                gy = keep * jnp.concatenate([ref[slot] for ref in cot_refs], axis=0).astype(f32)
                gm_ref[slot] = gy.astype(bf)
                total += jnp.sum(gy, axis=0, keepdims=True)
            gdb_ref[...] = total

        h2 = h2_ref[...].reshape(rows, model)
        gm = gm_ref[...].reshape(rows, model)
        up = u_ref[...]
        parts = [ref[...].astype(f32).reshape(-1, 1, shard, model) for ref in down_refs]
        down = jnp.concatenate(parts, axis=1).reshape(model, model).astype(bf)
        value, slope = gelu_parts(dot(h2, up) + b_ref[...])
        a = value.astype(bf)
        y = dot(a, down)
        gu32 = dot(gm, down, NT) * slope
        gu = gu32.astype(bf)
        gub_ref[...] = jnp.sum(gu.astype(f32), axis=0, keepdims=True)
        gh = dot(gu, up, NT)

        @pl.when(step == 0)
        def _():
            y_acc[...] = y
            gh_acc[...] = gh

        @pl.when(step != 0)
        def _():
            y_acc[...] += y
            gh_acc[...] += gh

        g_down = dot(a, gm, TN).reshape(-1, steps, shard, model)
        g_up = dot(h2, gu, TN).astype(bf).reshape(ups.shape)
        up_at = pl.ds(pl.multiple_of(at(step, here_ref) * model, 128), model)

        def up_copies():
            found = []
            for x in range(2):
                found.append(pltpu.make_async_copy(ups.at[2 * x + (1 - core)], sent_ref.at[x, :, up_at], sems.at[2 * x]))
                found.append(pltpu.make_async_copy(ups.at[2 * x + core], kept_ref.at[x, :, up_at], sems.at[2 * x + 1]))
            return found

        def down_copies(to_ref):
            return [
                pltpu.make_async_copy(
                    downs.at[part],
                    to_ref.at[step % 2, :, pl.ds(hidden + part * model, model)],
                    sems.at[4 + part],
                )
                for part in range(steps)
            ]

        @pl.when(step != 0)
        def _():
            for copy in up_copies() + down_copies(kept_ref):
                copy.wait()

        ups[...] = g_up
        for part in range(steps):
            downs[part] = g_down[:, part].reshape(chunk, model).astype(bf)
        for copy in up_copies():
            copy.start()

        @pl.when(step < steps // 2)
        def _():
            for copy in down_copies(sent_ref):
                copy.start()

        @pl.when(step >= steps // 2)
        def _():
            for copy in down_copies(kept_ref):
                copy.start()

        @pl.when(step == steps - 1)
        def _():
            y_ref[...] = y_acc[...].reshape(y_ref.shape)
            gh_ref[...] = gh_acc[...].reshape(gh_ref.shape)
            for copy in up_copies() + down_copies(kept_ref):
                copy.wait()

    def at(step, here_ref):
        return 2 * (step % 2) + (here_ref[1] ^ (1 - step // 2))

    full = pl.BlockSpec((slots, length, model), lambda i, h: (0, 0, 0))
    shape = (slots, length, model)
    side = jax.ShapeDtypeStruct((2, chunk, 2 * hidden), bf)
    line = jax.ShapeDtypeStruct((1, model), f32)
    return pl.pallas_call(
        body,
        grid_spec=pltpu.PrefetchScalarGridSpec(
            num_scalar_prefetch=1,
            grid=(steps,),
            in_specs=[
                full,
                pl.BlockSpec(tags.shape, lambda i, h: (0, 0, 0)),
                pl.BlockSpec((model, model), lambda i, h: (0, 1 + at(i, h))),
                pl.BlockSpec((1, model), lambda i, h: (0, at(i, h))),
            ]
            + [pl.BlockSpec(cot[0].shape, lambda i, h: (0, 0, 0))] * peers
            + [
                pl.BlockSpec((chunk, model), lambda i, h, c=1 + steps + step: (at(i, h), c))
                for step in range(steps)
            ],
            out_specs=[
                full,
                full,
                full,
                ANY,
                ANY,
                pl.BlockSpec((1, model), lambda i, h: (0, at(i, h))),
                pl.BlockSpec((1, model), lambda i, h: (0, 0)),
            ],
            scratch_shapes=[
                pltpu.VMEM((rows, model), f32),
                pltpu.VMEM((rows, model), f32),
                pltpu.VMEM((4, chunk, model), bf),
                pltpu.VMEM((steps, chunk, model), bf),
                pltpu.SemaphoreType.DMA((4 + steps,)),
            ],
        ),
        out_shape=[
            jax.ShapeDtypeStruct(shape, f32),
            jax.ShapeDtypeStruct(shape, f32),
            jax.ShapeDtypeStruct(shape, bf),
            side,
            side,
            jax.ShapeDtypeStruct((1, hidden), f32),
            line,
        ],
        compiler_params=pltpu.CompilerParams(vmem_limit_bytes=58 * 1024 * 1024),
        cost_estimate=pl.CostEstimate(
            flops=12 * rows * model * hidden, bytes_accessed=30 * rows * model, transcendentals=rows * hidden
        ),
    )(here, h2, tags, rest, up_bias, *cot, *([rest] * steps))


def norm_back(grad, n, scale, gain):
    gn = grad * gain
    mean = jnp.mean(gn, axis=-1, keepdims=True)
    cross = jnp.mean(gn * n, axis=-1, keepdims=True)
    return (gn - mean - n * cross) * scale


def middle_kernel(y_ref, gh_ref, wo_ref, x2_ref, gm_ref, tag_ref, vec_ref, out_ref, gx_ref, ga_ref, go_ref, gg_ref, gb_ref, gob_ref):
    x2 = x2_ref[0]
    keep = (tag_ref[0] & 1).astype(jnp.float32)
    spread(out_ref, (keep * (x2 + (y_ref[0] + vec_ref[7:8]))).astype(jnp.bfloat16))
    gh = gh_ref[0]
    n, scale = normalize(x2)
    add_rows(gg_ref, gh * n)
    add_rows(gb_ref, gh)
    gx = gm_ref[0].astype(jnp.float32) + norm_back(gh, n, scale, vec_ref[5:6])
    gx_ref[0] = gx
    low = gx.astype(jnp.bfloat16)
    ga_ref[0] = low
    add_rows(gob_ref, low.astype(jnp.float32))
    go_ref[0] = dot(low, wo_ref[...], NT).astype(jnp.bfloat16)


def attend_back_kernel(qkv_ref, go_ref, p_ref, g_ref, gqb_ref, gvb_ref):
    model = go_ref.shape[-1]
    head = model // HEADS
    for i in range(HEADS):
        at = slice(i * head, (i + 1) * head)
        k_at = slice(model + i * head, model + (i + 1) * head)
        v_at = slice(2 * model + i * head, 2 * model + (i + 1) * head)
        go = go_ref[0, :, at]
        p = p_ref[0, i]
        dp = dot(go, qkv_ref[0, :, v_at], NT)
        pf = p.astype(jnp.float32)
        delta = jnp.sum(pf * dp, axis=-1, keepdims=True)
        ds = (pf * (dp - delta)).astype(jnp.bfloat16)
        g_ref[0, :, at] = (dot(ds, qkv_ref[0, :, k_at]) * head**-0.5).astype(jnp.bfloat16)
        g_ref[0, :, k_at] = dot(ds, qkv_ref[0, :, at], TN).astype(jnp.bfloat16)
        g_ref[0, :, v_at] = dot(p, go, TN).astype(jnp.bfloat16)
    add_rows(gqb_ref, g_ref[0, :, :model].astype(jnp.float32))
    add_rows(gvb_ref, g_ref[0, :, 2 * model :].astype(jnp.float32))


def input_kernel(g_ref, w_ref, x_ref, gx_ref, vec_ref, out_ref, gg_ref, gb_ref):
    model = x_ref[0].shape[-1]
    gh = dot(g_ref[0], w_ref[:, : 3 * model], NT)
    n, scale = normalize(rows_of(x_ref).astype(jnp.float32))
    add_rows(gg_ref, gh * n)
    add_rows(gb_ref, gh)
    grad = gx_ref[0] + norm_back(gh, n, scale, vec_ref[0:1])
    spread(out_ref, grad.astype(jnp.bfloat16))


def call(kernel, inputs, outputs, slots, flops, first=0, carry=None, after=(), limit=56):
    specs = []
    arrays = []
    groups = []

    def slot_spec(shape):
        return pl.BlockSpec((1,) + shape[1:], lambda i, n=len(shape) - 1: (i + first,) + (0,) * n)

    for array, kind in inputs:
        if kind == "frames":
            groups.append(len(array))
            arrays += array
            specs += [slot_spec(piece.shape) for piece in array]
            continue
        groups.append(0)
        arrays.append(array)
        if kind == "slot":
            specs.append(slot_spec(array.shape))
        elif kind == "whole":
            specs.append(pl.BlockSpec(array.shape, lambda i, n=array.ndim: (0,) * n))
        else:
            rows = array.shape[0]
            specs.append(pl.BlockSpec((rows, rows), lambda i, j=kind: (0, j)))
    used = len(arrays)
    extra = list(after)
    shapes = []
    places = []
    aliases = {}
    for output in outputs:
        parts = output if isinstance(output, list) else [output]
        groups.append(len(parts) if isinstance(output, list) else 0)
        for shape, dtype in parts:
            shapes.append(jax.ShapeDtypeStruct(shape, dtype))
            if len(shape) > 2:
                places.append(slot_spec(shape))
                if carry is not None:
                    aliases[used + len(extra)] = len(shapes) - 1
                    extra.append(carry[len(shapes) - 1])
            else:
                places.append(pl.BlockSpec(shape, lambda i: (0, 0)))
    moved = sum(s.size * s.dtype.itemsize for s in arrays + shapes)
    skip = used + len(extra)

    def run(*refs):
        refs = list(refs[:used]) + list(refs[skip:])
        arguments = []
        for size in groups:
            arguments.append(refs[:size] if size else refs[0])
            refs = refs[size or 1 :]
        kernel(*arguments)

    results = pl.pallas_call(
        run,
        grid=(slots,),
        in_specs=specs + [ANY] * len(extra),
        out_specs=places,
        out_shape=shapes,
        input_output_aliases=aliases,
        compiler_params=pltpu.CompilerParams(vmem_limit_bytes=limit * 1024 * 1024),
        cost_estimate=pl.CostEstimate(flops=flops, bytes_accessed=moved, transcendentals=0),
    )(*arrays, *extra)
    final = []
    for output in outputs:
        size = len(output) if isinstance(output, list) else 0
        final.append(list(results[:size]) if size else results[0])
        results = results[size or 1 :]
    return final


def row_grad(here, products, after):
    slots, length, model = products[0][0].shape
    steps = []
    for index, (_, right) in enumerate(products):
        steps += [index] * (right.shape[2] // model)
    starts = [steps.index(index) for index in range(len(products))]
    chunk = model // 4
    used = 2 * len(products)

    def body(here_ref, *refs):
        sent_ref, kept_ref, value_ref = refs[-3:]
        core = here_ref[1]
        step = pl.program_id(0)
        for index in range(len(products)):
            end = starts[index] + steps.count(index)

            @pl.when((step >= starts[index]) & (step < end))
            def _():
                left, right = refs[2 * index], refs[2 * index + 1]
                value = dot(left[...].reshape(-1, model), right[...].reshape(-1, model), TN)
                value_ref[...] = value.astype(jnp.bfloat16).reshape(value_ref.shape)

        for x in range(2):
            sent_ref[x] = value_ref[2 * x + (1 - core)]
            kept_ref[x] = value_ref[2 * x + core]

    specs = []
    for index, (left, right) in enumerate(products):
        most = right.shape[2] // model - 1
        specs.append(pl.BlockSpec((slots, length, model), lambda i, h: (0, 0, 0)))
        specs.append(
            pl.BlockSpec(
                (slots, length, model),
                lambda i, h, s=starts[index], m=most: (0, 0, jnp.clip(i - s, 0, m)),
            )
        )
    shape = jax.ShapeDtypeStruct((2, chunk, len(steps) * model), jnp.bfloat16)
    out = pl.BlockSpec((2, chunk, model), lambda i, h: (0, 0, i))
    return pl.pallas_call(
        body,
        grid_spec=pltpu.PrefetchScalarGridSpec(
            num_scalar_prefetch=1,
            grid=(len(steps),),
            in_specs=specs + [ANY] * len(after),
            out_specs=[out, out],
            scratch_shapes=[pltpu.VMEM((4, chunk, model), jnp.bfloat16)],
        ),
        out_shape=[shape, shape],
        compiler_params=pltpu.CompilerParams(vmem_limit_bytes=56 * 1024 * 1024),
        cost_estimate=pl.CostEstimate(
            flops=2 * slots * length * model * model * len(steps),
            bytes_accessed=2 * sum(r.size for _, r in products),
            transcendentals=0,
        ),
    )(here, *[array for pair in products for array in pair], *after)


def turned(lines, tail, after):
    width = lines[0].shape[1]
    used = len(lines)

    def body(*refs):
        out = refs[-1]
        value = jnp.concatenate([ref[...] for ref in refs[:used]], axis=0)
        value = jnp.pad(value, ((0, 128 - value.shape[0]), (0, 0))).T
        out[...] = value.astype(jnp.bfloat16)
        out[:, used : used + tail.shape[1]] = refs[used][...].astype(jnp.bfloat16)

    vmem = pl.BlockSpec(memory_space=pltpu.VMEM)
    return pl.pallas_call(
        body,
        in_specs=[vmem] * (used + 1) + [ANY] * len(after),
        out_specs=vmem,
        out_shape=jax.ShapeDtypeStruct((width, 128), jnp.bfloat16),
    )(*lines, tail, *after)


def join(here, pieces, dtype):
    slots, width, model = pieces[0].shape
    count = len(pieces)

    def body(here_ref, *refs):
        for step in range(count):

            @pl.when(pl.program_id(0) == step)
            def _():
                refs[-1][...] = refs[step][...].astype(dtype)

    whole = pl.BlockSpec((slots, width, model), lambda i, h: (0, 0, 0))
    return pl.pallas_call(
        body,
        grid_spec=pltpu.PrefetchScalarGridSpec(
            num_scalar_prefetch=1,
            grid=(count,),
            in_specs=[whole] * count,
            out_specs=pl.BlockSpec((slots, width, model), lambda i, h: ((2 * h[0] + h[1]) ^ i, 0, 0)),
        ),
        out_shape=jax.ShapeDtypeStruct((slots * count, width, model), dtype),
    )(here, *pieces)


def side_by_side(out, up, down):
    rows, width = out.shape
    blocks = down.shape[0] // rows

    def body(out_ref, up_ref, down_ref, to_ref):
        to_ref[:, :width] = out_ref[...]
        to_ref[:, width : width + up.shape[1]] = up_ref[...]
        value = down_ref[...].astype(jnp.float32).reshape(blocks, rows, width)
        for step in range(blocks):
            at = width + up.shape[1] + step * width
            to_ref[:, at : at + width] = value[step].astype(down.dtype)

    total = width + up.shape[1] + blocks * width
    return pl.pallas_call(body, out_shape=jax.ShapeDtypeStruct((rows, total), down.dtype))(out, up, down)


def body(
    sizes,
    tokens,
    cotangent,
    frame_count,
    image_group,
    keep_mask,
    attn_norm_gain,
    attn_norm_bias,
    w_qkv,
    query_bias,
    value_bias,
    w_out,
    out_bias,
    mlp_norm_gain,
    mlp_norm_bias,
    w_up,
    up_bias,
    w_down,
    down_bias,
):
    bf, f32 = jnp.bfloat16, jnp.float32
    here = jnp.stack([lax.axis_index(name) for name in AXES]).astype(jnp.int32)
    peers = sizes[0] * sizes[1]
    frames_here = image_group.shape[1]
    block_width = keep_mask.shape[1] // frames_here
    frame_index = lax.axis_index(FRAME) * frames_here + jnp.arange(frames_here, dtype=jnp.int32)
    segment = jnp.where(frame_index[None, :] < frame_count[:, None], 0, 1 + image_group)
    tags = jnp.repeat(segment, block_width, axis=1) * 2 + keep_mask

    def frame_peer(bits):
        def choose(at):
            at["x"] ^= bits // 2
            at["core"] ^= bits % 2
            return at

        return choose

    def exchange(pieces):
        return list(pieces[:1]) + [swap(sizes, pieces[bits], frame_peer(bits)) for bits in range(1, peers)]

    def slots_for(value):
        own = value.shape[0] // peers
        frame = lax.axis_index(FRAME)
        return [lax.dynamic_slice_in_dim(value, (frame ^ bits) * own, own, 0) for bits in range(peers)]

    rows, model = w_out.shape
    hidden = w_up.shape[1]
    ratio = hidden // model
    vectors = [
        attn_norm_gain, attn_norm_bias, query_bias, value_bias, out_bias, mlp_norm_gain, mlp_norm_bias, down_bias
    ]
    small = columns_of(vectors, up_bias.reshape(rows, ratio))
    slots = tokens.shape[0] // peers
    length = peers * tokens.shape[1]
    here_rows = slots * length
    framed = [((slots, tokens.shape[1], model), bf)] * peers
    full = (slots, length, model)
    wide = (slots, length, hidden)
    scores = 2 * here_rows * length * model
    each = (1,) * slots

    rest = lax.all_gather(side_by_side(w_out, w_up, w_down), AXES, axis=0, tiled=True)
    tags = jnp.pad(tags.astype(bf)[:, None, :], ((0, 0), (0, 7), (0, model - tags.shape[1])))
    x = exchange(slots_for(jnp.concatenate([tokens, tags], axis=1)))
    get_mixed = Gather(sizes, here, jnp.concatenate([w_qkv, small], axis=1))
    get_mixed.stack(x[1:])
    get_mixed.second()
    get_mixed.third()
    mixed, vec = get_mixed.whole(16)
    up_bias_row = vec[8 : 8 + ratio].T.reshape(1, -1)

    attend = (
        attend_kernel,
        [(x, "frames"), (mixed, "whole"), (vec, "whole")],
        [
            (full, bf), ((slots, length, 3 * model), bf), (full, bf), ((slots, HEADS, length, length), bf),
            ((slots, length, 1), jnp.int32),
        ],
    )
    cost = (6 * here_rows * model * model + 8 * scores) // slots
    h1, qkv, o, p, tag_columns = call(*attend, slots, cost * slots)
    cot = exchange(slots_for(copy_after(cotangent, [mixed])))
    x2, h2 = call(
        project_kernel,
        [(x, "frames"), (o, "slot"), (rest, 0), (vec, "whole")],
        [(full, f32), (full, bf)],
        slots,
        2 * here_rows * model * model,
    )
    y, gh, gm, sent, kept, gub, gdb = mlp(here, h2, cot, tag_columns, rest, up_bias_row, rows)
    put_rest = Scatter(sizes, here, sent, kept)
    out, gx, ga, go, gmg, gmb, gob = call(
        middle_kernel,
        [(y, "slot"), (gh, "slot"), (rest, 0), (x2, "slot"), (gm, "slot"), (tag_columns, "slot"), (vec, "whole")],
        [framed, (full, f32), (full, bf), (full, bf)] + [((1, model), f32)] * 3,
        slots,
        2 * here_rows * model * model,
    )
    put_rest.hold([go])
    put_rest.second()
    g_mix, gqb, gvb = call(
        attend_back_kernel,
        [(qkv, "slot"), (go, "slot"), (p, "slot")],
        [((slots, length, 3 * model), bf)] + [((1, model), f32)] * 2,
        slots,
        16 * scores,
        after=[put_rest.sent],
    )
    put_rest.hold([g_mix])
    put_rest.third()
    in_grad, gag, gab = call(
        input_kernel,
        [(g_mix, "slot"), (mixed, "whole"), (x, "frames"), (gx, "slot"), (vec, "whole")],
        [framed] + [((1, model), f32)] * 2,
        slots,
        6 * here_rows * model * model,
        after=[put_rest.sent],
    )
    out = exchange(hold(out, [g_mix]))
    in_grad = exchange(in_grad)
    put_rest.hold([gag])
    put_rest.fourth()
    sent, kept = row_grad(here, [(h1, g_mix), (o, ga)], [gag, put_rest.sent] + out[1:])
    put_mixed = Scatter(sizes, here, hold([sent], in_grad[1:])[0], kept)
    put_mixed.second()
    sums = [gag, gab, gqb, gvb, gob, gmg, gmb, gdb]
    pack = turned(sums, gub.reshape(-1, ratio), [])
    pack = lax.all_to_all(pack.reshape(-1, rows, 128), AXES, 0, 0, tiled=True)
    last = jnp.sum(pack.astype(f32), axis=0)
    put_mixed.third()
    put_mixed.hold([pack])
    put_mixed.fourth()
    rest_rows = put_rest.last()
    g_up = rest_rows[:, :hidden]
    g_down = rest_rows[:, hidden:].reshape(rows, ratio, model).transpose(1, 0, 2).reshape(ratio * rows, model)
    mixed_rows = put_mixed.last()
    g_qkv, g_out = mixed_rows[:, : 3 * model], mixed_rows[:, 3 * model :]
    v = [last[:, i] for i in range(8)]
    return (
        join(here, out, bf), join(here, in_grad, f32), v[0], v[1], g_qkv, v[2], v[3], g_out, v[4], v[5], v[6],
        g_up, last[:, 8 : 8 + ratio].reshape(-1), g_down, v[7],
    )


def solution(mesh):
    frames, clips = mesh.shape["frame"], mesh.shape["clip"]
    sizes = (frames // 2, 2, clips // 2, 2)
    mesh = Mesh(mesh.devices.reshape(sizes), AXES)

    def run(*arguments):
        return body(sizes, *arguments)

    placed = (
        P(("z", "y"), FRAME, None),
        P(("z", "y"), FRAME, None),
        P(("z", "y")),
        P(("z", "y"), FRAME),
        P(("z", "y"), FRAME),
        P(AXES),
        P(AXES),
        P(AXES, None),
        P(AXES),
        P(AXES),
        P(AXES, None),
        P(AXES),
        P(AXES),
        P(AXES),
        P(AXES, None),
        P(AXES),
        P(AXES, None),
        P(AXES),
    )
    return jax.shard_map(
        run,
        mesh=mesh,
        in_specs=placed,
        out_specs=(
            P(("z", "y"), FRAME, None),
            P(("z", "y"), FRAME, None),
            P(AXES),
            P(AXES),
            P(AXES, None),
            P(AXES),
            P(AXES),
            P(AXES, None),
            P(AXES),
            P(AXES),
            P(AXES),
            P(AXES, None),
            P(AXES),
            P(AXES, None),
            P(AXES),
        ),
        check_vma=False,
    )
```

profile of v0, /device:TPU:0, one launch (start us, length us, event | category | flops | bytes accessed | tf_op | source)
XLA Modules:
  0.0 357.2 jit_solution(6676805825392921469)
XLA Ops:
  21.1 2.6 collective-permute-start.4
  23.7 2.8 collective-permute-done.3.refs_0_
  26.5 5.9 %collective-permute-start.5 = (bf16[24,2432]{1,0:T(8,128)(2,1)S(1)}, bf16[24,2432]{1,0:T(8,128)(2,1)S(1)}, u32[]{:S(2)}, u32[]{:S(2)}) collective-permute-start(bf16[24,2432]{1,0:T(8,128)(2,1)S(1)} %get-tuple-element.128), channel_id=1, source_target_pairs={{0,6},{1,7},{2,4},{3,5},{4,2},{5,3},{6,0},{7,1},{8,14},{9,15},{10,... | collective-permute-start | bytes 350216 | tf_op jit(solution)/shard_map/ppermute | solution.py:31
  32.4 5.4 %collective-permute-done.4.refs_1_ = bf16[24,2432]{1,0:T(8,128)(2,1)S(1)} collective-permute-done((bf16[24,2432]{1,0:T(8,128)(2,1)S(1)}, bf16[24,2432]{1,0:T(8,128)(2,1)S(1)}, u32[]{:S(2)}, u32[]{:S(2)}) %collective-permute-start.4) | collective-permute-done | bytes 116768 | tf_op jit(solution)/shard_map/ppermute | solution.py:31
  43.6 14.6 %collective-permute-done.6.refs_1_ = bf16[4,24,2432]{2,1,0:T(8,128)(2,1)S(1)} collective-permute-done((bf16[4,24,2432]{2,1,0:T(8,128)(2,1)S(1)}, bf16[4,24,2432]{2,1,0:T(8,128)(2,1)S(1)}, u32[]{:S(2)}, u32[]{:S(2)}) %collective-permute-start.6) | collective-permute-done | bytes 466976 | tf_op jit(solution)/shard_map/ppermute | solution.py:31
  61.9 7.5 %collective-permute-done.8.refs_3_ = bf16[4,24,2432]{2,1,0:T(8,128)(2,1)S(1)} collective-permute-done((bf16[4,24,2432]{2,1,0:T(8,128)(2,1)}, bf16[4,24,2432]{2,1,0:T(8,128)(2,1)S(1)}, u32[]{:S(2)}, u32[]{:S(2)}) %collective-permute-start.8) | collective-permute-done | bytes 466976 | tf_op jit(solution)/shard_map/ppermute | solution.py:31
  72.0 4.9 %shard_map.292 = (bf16[2,2,4,2,24,2432]{5,4,3,2,1,0:T(8,128)(2,1)}, f32[16,768]{1,0:T(8,128)}) custom-call(s32[4]{0:T(128)} %pad_add_fusion.here_ref, bf16[4,24,2432]{2,1,0:T(8,128)(2,1)} %copy-done.7, bf16[4,24,2432]{2,1,0:T(8,128)(2,1)} %copy-done.8, bf16[4,24,2432]{2,1,0:T(8,128)(2,1)} %shard_map.291.refs_2_, bf16[4,24,2432]{2,1,0:T(8,128)(2,1)} %copy-done.18, ...), custom_call_target="tpu_custom_call" | custom-call | tf_op jit(solution)/shard_map/pallas_call | solution.py:156
  77.0 2.6 shard_map.296
  84.9 25.1 %shard_map.293 = (bf16[3,320,768]{2,1,0:T(8,128)(2,1)}, bf16[3,320,2304]{2,1,0:T(8,128)(2,1)}, bf16[3,320,768]{2,1,0:T(8,128)(2,1)}, bf16[3,12,320,320]{3,2,1,0:T(8,128)(2,1)}, s32[3,320,1]{2,1,0:T(8,128)}) custom-call(bf16[3,88,768]{2,1,0:T(8,128)(2,1)} %get-tuple-element.114.refs_0_.refs_2_, bf16[3,88,768]{2,1,0:T(8,128)(2,1)} %copy-done.4, ...), custom_call_target="tpu_custom_call" | custom-call | flops 7172259840 | bytes 20156160 | tf_op jit(solution)/shard_map/pallas_call | solution.py:598
  111.8 12.1 %all-gather.2.cloned.1.call-done.refs_5_.u_ref.refs_4_.refs_6_.refs_7_.refs_2_ = bf16[768,6912]{1,0:T(8,128)(2,1)} async-done(((bf16[24,6912]{1,0:T(8,128)(2,1)}), bf16[768,6912]{1,0:T(8,128)(2,1)}) %all-gather.2.cloned.1.call-update) | async-done | bytes 10616848 | tf_op jit(solution)/shard_map/all_gather | solution.py:795
  123.9 6.0 %shard_map.295 = (f32[3,320,768]{2,1,0:T(8,128)}, bf16[3,320,768]{2,1,0:T(8,128)(2,1)}) custom-call(bf16[3,88,768]{2,1,0:T(8,128)(2,1)} %get-tuple-element.114.refs_0_.refs_2_, bf16[3,88,768]{2,1,0:T(8,128)(2,1)} %copy-done.4, bf16[3,88,768]{2,1,0:T(8,128)(2,1)} %copy-done.5, bf16[3,88,768]{2,1,0:T(8,128)(2,1)} %copy-done.6, ...), custom_call_target="tpu_custom_call" | custom-call | flops 1132462080 | bytes 18186240 | tf_op jit(solution)/shard_map/pallas_call | solution.py:598
  130.9 47.6 %shard_map.297 = (f32[3,320,768]{2,1,0:T(8,128)}, f32[3,320,768]{2,1,0:T(8,128)}, bf16[3,320,768]{2,1,0:T(8,128)(2,1)}, bf16[2,192,6144]{2,1,0:T(8,128)(2,1)}, b...) custom-call(s32[4]{0:T(128)} %pad_add_fusion.here_ref, ...), custom_call_target="tpu_custom_call" | custom-call | flops 27179089920 | bytes 22118400 | tf_op jit(solution)/shard_map/pallas_call | solution.py:445
  178.5 9.8 %shard_map.298 = (bf16[3,80,768]{2,1,0:T(8,128)(2,1)}, bf16[3,80,768]{2,1,0:T(8,128)(2,1)}, bf16[3,80,768]{2,1,0:T(8,128)(2,1)}, bf16[3,80,768]{2,1,0:T(8,128)(2...) custom-call(f32[3,320,768]{2,1,0:T(8,128)} %get-tuple-element.67.ref, ...), custom_call_target="tpu_custom_call" | custom-call | flops 1132462080 | bytes 28373760 | tf_op jit(solution)/shard_map/pallas_call | solution.py:598
  188.4 5.2 %shard_map.300.refs_3_ = bf16[2,4,24,6144]{3,2,1,0:T(8,128)(2,1)} custom-call(s32[4]{0:T(128)} %pad_add_fusion.here_ref, bf16[2,4,2,24,6144]{4,3,2,1,0:T(8,128)(2,1)} %shard_map.299.refs_0_, bf16[2,4,2,24,6144]{4,3,2,1,0:T(8,128)(2,1)} %collective-permute-done.16.refs_1_), custom_call_target="tpu_custom_call" | custom-call | bytes 7077888 | tf_op jit(solution)/shard_map/pallas_call | solution.py:203
  193.5 24.2 %shard_map.301 = (bf16[3,320,2304]{2,1,0:T(8,128)(2,1)}, f32[1,768]{1,0:T(1,128)}, f32[1,768]{1,0:T(1,128)}) custom-call(bf16[3,320,2304]{2,1,0:T(8,128)(2,1)} %get-tuple-element.75.refs_0_, bf16[3,320,768]{2,1,0:T(8,128)(2,1)} %get-tuple-element.76.refs_1_, bf16[3,12,320,320]{3,2,1,0:T(8,128)(2,1)} %get-tuple-element.77.refs_2_, ...), custom_call_target="tpu_custom_call" | custom-call | flops 7549747200 | bytes 17700864 | tf_op jit(solution)/shard_map/pallas_call | solution.py:598
  217.8 4.8 %collective-permute-done.20.refs_2_ = bf16[2,4,24,6144]{3,2,1,0:T(8,128)(2,1)S(1)} collective-permute-done((bf16[2,4,24,6144]{3,2,1,0:T(8,128)(2,1)}, bf16[2,4,24,6144]{3,2,1,0:T(8,128)(2,1)S(1)}, u32[]{:S(2)}, u32[]{:S(2)}) %collective-permute-start.20) | collective-permute-done | bytes 2359328 | tf_op jit(solution)/shard_map/ppermute | solution.py:31
  224.0 3.7 %shard_map.305.refs_8_ = bf16[1,4,24,6144]{3,2,1,0:T(8,128)(2,1)} custom-call(s32[4]{0:T(128)} %pad_add_fusion.here_ref, bf16[2,4,2,24,6144]{4,3,2,1,0:T(8,128)(2,1)} %shard_map.304.refs_0_, bf16[2,4,2,24,6144]{4,3,2,1,0:T(8,128)(2,1)} %collective-permute-done.16.refs_1_, bf16[2,4,24,6144]{3,2,1,0:T(8,128)(2,1)} %copy-done.1), custom_call_target="tpu_custom_call" | custom-call | bytes 4718592 | tf_op jit(solution)/shard_map/pallas_call | solution.py:203
  232.2 9.4 %shard_map.306 = (bf16[3,80,768]{2,1,0:T(8,128)(2,1)}, bf16[3,80,768]{2,1,0:T(8,128)(2,1)}, bf16[3,80,768]{2,1,0:T(8,128)(2,1)}, bf16[3,80,768]{2,1,0:T(8,128)(2...) custom-call(bf16[3,320,2304]{2,1,0:T(8,128)(2,1)} %get-tuple-element.80.refs_4_.refs_1_.refs_0_, bf16[768,2432]{1,0:T(8,128)(2,1)} %bitcast.58, ...), custom_call_target="tpu_custom_call" | custom-call | flops 3397386240 | bytes 14260224 | tf_op jit(solution)/shard_map/pallas_call | solution.py:598
  242.0 2.7 collective-permute-done.24.refs_3_
  245.7 4.1 %shard_map.310 = bf16[1,4,24,6144]{3,2,1,0:T(8,128)(2,1)} custom-call(s32[4]{0:T(128)} %pad_add_fusion.here_ref, bf16[2,4,2,24,6144]{4,3,2,1,0:T(8,128)(2,1)} %shard_map.309.refs_0_, bf16[2,4,2,24,6144]{4,3,2,1,0:T(8,128)(2,1)} %collective-permute-done.16.refs_1_, bf16[2,4,24,6144]{3,2,1,0:T(8,128)(2,1)} %copy-done.1, bf16[1,4,24,6144]{3,2,1,0:T(8,128)(2,1)} %copy-done.13), custom_call_target="tpu_custom_call" | custom-call | bytes 5898240 | tf_op jit(solution)/shard_map/pallas_call | solution.py:203
  249.9 8.3 %collective-permute-start.23 = (bf16[3,80,768]{2,1,0:T(8,128)(2,1)S(1)}, bf16[3,80,768]{2,1,0:T(8,128)(2,1)S(1)}, u32[]{:S(2)}, u32[]{:S(2)}) collective-permute-start(bf16[3,80,768]{2,1,0:T(8,128)(2,1)S(1)} %copy-done.29), channel_id=1, source_target_pairs={{0,24},{1,25},{2,26},{3,27},{4,28},{5,29},{6,30},{7,31},{8,16},{9,... | collective-permute-start | bytes 1105928 | tf_op jit(solution)/shard_map/ppermute | solution.py:31
  258.2 6.8 %collective-permute-done.19.refs_3_.refs_8_ = bf16[3,80,768]{2,1,0:T(8,128)(2,1)S(1)} collective-permute-done((bf16[3,80,768]{2,1,0:T(8,128)(2,1)}, bf16[3,80,768]{2,1,0:T(8,128)(2,1)S(1)}, u32[]{:S(2)}, u32[]{:S(2)}) %collective-permute-start.19) | collective-permute-done | bytes 368672 | tf_op jit(solution)/shard_map/ppermute | solution.py:31
  265.8 10.9 %shard_map.311 = (bf16[2,192,3072]{2,1,0:T(8,128)(2,1)}, bf16[2,192,3072]{2,1,0:T(8,128)(2,1)}) custom-call(s32[4]{0:T(128)} %pad_add_fusion.here_ref, bf16[3,320,768]{2,1,0:T(8,128)(2,1)} %get-tuple-element.99.refs_0_, bf16[3,320,2304]{2,1,0:T(8,128)(2,1)} %get-tuple-element.80.refs_4_.refs_1_.refs_0_, ...), custom_call_target="tpu_custom_call" | custom-call | flops 4529848320 | bytes 5898240 | tf_op jit(solution)/shard_map/pallas_call | solution.py:654
  282.2 7.7 %all-to-all-start = ((bf16[32,24,128]{2,1,0:T(8,128)(2,1)}), bf16[32,24,128]{2,1,0:T(8,128)(2,1)}, u32[]{:S(2)}, u32[]{:S(2)}) async-start(bf16[32,24,128]{2,1,0:T(8,128)(2,1)} %bitcast.62), calls=%async_computation | async-start | bytes 393216 | tf_op jit(solution)/shard_map/all_to_all | solution.py:861
  291.4 4.5 %shard_map.314 = bf16[2,4,24,3072]{3,2,1,0:T(8,128)(2,1)} custom-call(s32[4]{0:T(128)} %pad_add_fusion.here_ref, bf16[2,4,2,24,3072]{4,3,2,1,0:T(8,128)(2,1)} %bitcast.53, bf16[2,4,2,24,3072]{4,3,2,1,0:T(8,128)(2,1)} %copy-done), custom_call_target="tpu_custom_call" | custom-call | bytes 3538944 | tf_op jit(solution)/shard_map/pallas_call | solution.py:203
  302.6 3.7 %shard_map.303 = bf16[12,80,768]{2,1,0:T(8,128)(2,1)} custom-call(s32[4]{0:T(128)} %pad_add_fusion.here_ref, bf16[3,80,768]{2,1,0:T(8,128)(2,1)} %get-tuple-element.81.refs_0_, bf16[3,80,768]{2,1,0:T(8,128)(2,1)} %copy-done.23, bf16[3,80,768]{2,1,0:T(8,128)(2,1)} %copy-done.24, bf16[3,80,768]{2,1,0:T(8,128)(2,1)} %copy-done.25), custom_call_target="tpu_custom_call" | custom-call | tf_op jit(solution)/shard_map/pallas_call | solution.py:705
  306.3 4.1 %shard_map.307 = f32[12,80,768]{2,1,0:T(8,128)} custom-call(s32[4]{0:T(128)} %pad_add_fusion.here_ref, bf16[3,80,768]{2,1,0:T(8,128)(2,1)} %get-tuple-element.86.refs_0_, bf16[3,80,768]{2,1,0:T(8,128)(2,1)} %copy-done.10, bf16[3,80,768]{2,1,0:T(8,128)(2,1)} %copy-done.11, bf16[3,80,768]{2,1,0:T(8,128)(2,1)} %copy-done.12), custom_call_target="tpu_custom_call" | custom-call | tf_op jit(solution)/shard_map/pallas_call | solution.py:705
  315.2 2.9 shard_map.315
  319.6 3.5 collective-permute-done.32
  324.2 4.0 %collective-permute-done.27.refs_3_ = bf16[1,4,24,3072]{3,2,1,0:T(8,128)(2,1)S(1)} collective-permute-done((bf16[1,4,24,3072]{3,2,1,0:T(8,128)(2,1)}, bf16[1,4,24,3072]{3,2,1,0:T(8,128)(2,1)S(1)}, u32[]{:S(2)}, u32[]{:S(2)}) %collective-permute-start.27) | collective-permute-done | bytes 589856 | tf_op jit(solution)/shard_map/ppermute | solution.py:31
  329.0 3.2 shard_map.316
  340.2 7.8 %collective-permute-done.29 = bf16[24,3072]{1,0:T(8,128)(2,1)S(1)} collective-permute-done((bf16[24,3072]{1,0:T(8,128)(2,1)S(1)}, bf16[24,3072]{1,0:T(8,128)(2,1)S(1)}, u32[]{:S(2)}, u32[]{:S(2)}) %collective-permute-start.29) | collective-permute-done | bytes 147488 | tf_op jit(solution)/shard_map/ppermute | solution.py:31
  (168 shorter events, 74.1 us)
Async XLA Ops:
  7.2 116.7 %all-gather.2.cloned.1.call-start = ((), (), s32[]{:S(2)}) async-start(), calls=%async_computation.1 | async-start | bytes 10948608 | tf_op jit(solution)/shard_map/all_gather | solution.py:795
  13.2 24.5 %collective-permute-start = (bf16[3,88,768]{2,1,0:T(8,128)(2,1)S(1)}, bf16[3,88,768]{2,1,0:T(8,128)(2,1)S(1)}, u32[]{:S(2)}, u32[]{:S(2)}) collective-permute-start(bf16[3,88,768]{2,1,0:T(8,128)(2,1)S(1)} %get-tuple-element.113), channel_id=1, source_target_pairs={{0,8},{1,9},{2,10},{3,11},{4,12},{5,13},{6,14},{7,15},{8,0},{9,1},... | collective-permute-start | bytes 1216520 | tf_op jit(solution)/shard_map/ppermute | solution.py:31
  13.6 24.1 %collective-permute-start.1 = (bf16[3,88,768]{2,1,0:T(8,128)(2,1)S(1)}, bf16[3,88,768]{2,1,0:T(8,128)(2,1)S(1)}, u32[]{:S(2)}, u32[]{:S(2)}) collective-permute-start(bf16[3,88,768]{2,1,0:T(8,128)(2,1)S(1)} %get-tuple-element.112), channel_id=1, source_target_pairs={{0,16},{1,17},{2,18},{3,19},{4,20},{5,21},{6,22},{7,23},{8,24},{9,... | collective-permute-start | bytes 1216520 | tf_op jit(solution)/shard_map/ppermute | solution.py:31
  16.2 21.6 %collective-permute-start.2 = (bf16[3,88,768]{2,1,0:T(8,128)(2,1)S(1)}, bf16[3,88,768]{2,1,0:T(8,128)(2,1)S(1)}, u32[]{:S(2)}, u32[]{:S(2)}) collective-permute-start(bf16[3,88,768]{2,1,0:T(8,128)(2,1)S(1)} %get-tuple-element.111), channel_id=1, source_target_pairs={{0,24},{1,25},{2,26},{3,27},{4,28},{5,29},{6,30},{7,31},{8,16},{9,... | collective-permute-start | bytes 1216520 | tf_op jit(solution)/shard_map/ppermute | solution.py:31
  21.1 16.6 %collective-permute-start.4 = (bf16[24,2432]{1,0:T(8,128)(2,1)S(1)}, bf16[24,2432]{1,0:T(8,128)(2,1)S(1)}, u32[]{:S(2)}, u32[]{:S(2)}) collective-permute-start(bf16[24,2432]{1,0:T(8,128)(2,1)S(1)} %get-tuple-element.128), channel_id=1, source_target_pairs={{0,4},{1,5},{2,6},{3,7},{4,0},{5,1},{6,2},{7,3},{8,12},{9,13},{10,... | collective-permute-start | bytes 350216 | tf_op jit(solution)/shard_map/ppermute | solution.py:31
  26.5 11.3 %collective-permute-start.5 = (bf16[24,2432]{1,0:T(8,128)(2,1)S(1)}, bf16[24,2432]{1,0:T(8,128)(2,1)S(1)}, u32[]{:S(2)}, u32[]{:S(2)}) collective-permute-start(bf16[24,2432]{1,0:T(8,128)(2,1)S(1)} %get-tuple-element.128), channel_id=1, source_target_pairs={{0,6},{1,7},{2,4},{3,5},{4,2},{5,3},{6,0},{7,1},{8,14},{9,15},{10,... | collective-permute-start | bytes 350216 | tf_op jit(solution)/shard_map/ppermute | solution.py:31
  40.6 17.7 %collective-permute-start.6 = (bf16[4,24,2432]{2,1,0:T(8,128)(2,1)S(1)}, bf16[4,24,2432]{2,1,0:T(8,128)(2,1)S(1)}, u32[]{:S(2)}, u32[]{:S(2)}) collective-permute-start(bf16[4,24,2432]{2,1,0:T(8,128)(2,1)S(1)} %pad_maximum_fusion.refs_0_), channel_id=1, source_target_pairs={{0,1},{1,0},{2,3},{3,2},{4,5},{5,4},{6,7},{7,6},{8,24},{9,25},{10,... | collective-permute-start | bytes 1400840 | tf_op jit(solution)/shard_map/ppermute | solution.py:31
  42.2 17.6 %collective-permute-start.7 = (bf16[4,24,2432]{2,1,0:T(8,128)(2,1)S(1)}, bf16[4,24,2432]{2,1,0:T(8,128)(2,1)S(1)}, u32[]{:S(2)}, u32[]{:S(2)}) collective-permute-start(bf16[4,24,2432]{2,1,0:T(8,128)(2,1)S(1)} %pad_maximum_fusion.refs_0_), channel_id=1, source_target_pairs={{0,16},{1,17},{2,18},{3,19},{4,20},{5,21},{6,22},{7,23},{8,9},{9,8... | collective-permute-start | bytes 1400840 | tf_op jit(solution)/shard_map/ppermute | solution.py:31
  60.6 8.8 %collective-permute-start.8 = (bf16[4,24,2432]{2,1,0:T(8,128)(2,1)}, bf16[4,24,2432]{2,1,0:T(8,128)(2,1)S(1)}, u32[]{:S(2)}, u32[]{:S(2)}) collective-permute-start(bf16[4,24,2432]{2,1,0:T(8,128)(2,1)} %shard_map.291.refs_2_), channel_id=1, source_target_pairs={{0,1},{1,0},{2,3},{3,2},{4,5},{5,4},{6,7},{7,6},{8,24},{9,25},{10,... | collective-permute-start | bytes 1400840 | tf_op jit(solution)/shard_map/ppermute | solution.py:31
  61.3 8.7 %collective-permute-start.9 = (bf16[4,24,2432]{2,1,0:T(8,128)(2,1)S(1)}, bf16[4,24,2432]{2,1,0:T(8,128)(2,1)S(1)}, u32[]{:S(2)}, u32[]{:S(2)}) collective-permute-start(bf16[4,24,2432]{2,1,0:T(8,128)(2,1)S(1)} %pad_maximum_fusion.refs_0_), channel_id=1, source_target_pairs={{0,8},{1,9},{2,10},{3,11},{4,12},{5,13},{6,14},{7,15},{8,0},{9,1},... | collective-permute-start | bytes 1400840 | tf_op jit(solution)/shard_map/ppermute | solution.py:31
  61.3 8.7 %collective-permute-start.11 = (bf16[4,24,2432]{2,1,0:T(8,128)(2,1)}, bf16[4,24,2432]{2,1,0:T(8,128)(2,1)S(1)}, u32[]{:S(2)}, u32[]{:S(2)}) collective-permute-start(bf16[4,24,2432]{2,1,0:T(8,128)(2,1)} %shard_map.291.refs_2_), channel_id=1, source_target_pairs={{0,8},{1,9},{2,10},{3,11},{4,12},{5,13},{6,14},{7,15},{8,0},{9,1},... | collective-permute-start | bytes 1400840 | tf_op jit(solution)/shard_map/ppermute | solution.py:31
  82.1 47.8 %collective-permute-start.13 = (bf16[3,80,768]{2,1,0:T(8,128)(2,1)S(1)}, bf16[3,80,768]{2,1,0:T(8,128)(2,1)S(1)}, u32[]{:S(2)}, u32[]{:S(2)}) collective-permute-start(bf16[3,80,768]{2,1,0:T(8,128)(2,1)S(1)} %get-tuple-element.117), channel_id=1, source_target_pairs={{0,8},{1,9},{2,10},{3,11},{4,12},{5,13},{6,14},{7,15},{8,0},{9,1},... | collective-permute-start | bytes 1105928 | tf_op jit(solution)/shard_map/ppermute | solution.py:31
  82.4 47.5 %collective-permute-start.14 = (bf16[3,80,768]{2,1,0:T(8,128)(2,1)S(1)}, bf16[3,80,768]{2,1,0:T(8,128)(2,1)S(1)}, u32[]{:S(2)}, u32[]{:S(2)}) collective-permute-start(bf16[3,80,768]{2,1,0:T(8,128)(2,1)S(1)} %get-tuple-element.116), channel_id=1, source_target_pairs={{0,16},{1,17},{2,18},{3,19},{4,20},{5,21},{6,22},{7,23},{8,24},{9,... | collective-permute-start | bytes 1105928 | tf_op jit(solution)/shard_map/ppermute | solution.py:31
  84.9 45.0 %collective-permute-start.15 = (bf16[3,80,768]{2,1,0:T(8,128)(2,1)S(1)}, bf16[3,80,768]{2,1,0:T(8,128)(2,1)S(1)}, u32[]{:S(2)}, u32[]{:S(2)}) collective-permute-start(bf16[3,80,768]{2,1,0:T(8,128)(2,1)S(1)} %get-tuple-element.115), channel_id=1, source_target_pairs={{0,24},{1,25},{2,26},{3,27},{4,28},{5,29},{6,30},{7,31},{8,16},{9,... | collective-permute-start | bytes 1105928 | tf_op jit(solution)/shard_map/ppermute | solution.py:31
  178.4 9.9 %collective-permute-start.16 = (bf16[2,4,2,24,6144]{4,3,2,1,0:T(8,128)(2,1)}, bf16[2,4,2,24,6144]{4,3,2,1,0:T(8,128)(2,1)}, u32[]{:S(2)}, u32[]{:S(2)}) collective-permute-start(bf16[2,4,2,24,6144]{4,3,2,1,0:T(8,128)(2,1)} %bitcast.75), channel_id=1, source_target_pairs={{0,8},{1,9},{2,10},{3,11},{4,12},{5,13},{6,14},{7,15},{8,0},{9,1},... | collective-permute-start | bytes 14155784 | tf_op jit(solution)/shard_map/ppermute | solution.py:31
  193.5 29.1 %collective-permute-start.20 = (bf16[2,4,24,6144]{3,2,1,0:T(8,128)(2,1)}, bf16[2,4,24,6144]{3,2,1,0:T(8,128)(2,1)S(1)}, u32[]{:S(2)}, u32[]{:S(2)}) collective-permute-start(bf16[2,4,24,6144]{3,2,1,0:T(8,128)(2,1)} %shard_map.300.refs_3_), channel_id=1, source_target_pairs={{0,16},{1,17},{2,18},{3,19},{4,20},{5,21},{6,22},{7,23},{8,9},{9,8... | collective-permute-start | bytes 7077896 | tf_op jit(solution)/shard_map/ppermute | solution.py:31
  227.7 17.0 %collective-permute-start.24 = (bf16[1,4,24,6144]{3,2,1,0:T(8,128)(2,1)}, bf16[1,4,24,6144]{3,2,1,0:T(8,128)(2,1)S(1)}, u32[]{:S(2)}, u32[]{:S(2)}) collective-permute-start(bf16[1,4,24,6144]{3,2,1,0:T(8,128)(2,1)} %shard_map.305.refs_8_), channel_id=1, source_target_pairs={{0,1},{1,0},{2,3},{3,2},{4,5},{5,4},{6,7},{7,6},{8,24},{9,25},{10,... | collective-permute-start | bytes 3538952 | tf_op jit(solution)/shard_map/ppermute | solution.py:31
  230.3 19.6 %collective-permute-start.17 = (bf16[3,80,768]{2,1,0:T(8,128)(2,1)}, bf16[3,80,768]{2,1,0:T(8,128)(2,1)S(1)}, u32[]{:S(2)}, u32[]{:S(2)}) collective-permute-start(bf16[3,80,768]{2,1,0:T(8,128)(2,1)} %get-tuple-element.82), channel_id=1, source_target_pairs={{0,8},{1,9},{2,10},{3,11},{4,12},{5,13},{6,14},{7,15},{8,0},{9,1},... | collective-permute-start | bytes 1105928 | tf_op jit(solution)/shard_map/ppermute | solution.py:31
  230.3 27.9 %collective-permute-start.18 = (bf16[3,80,768]{2,1,0:T(8,128)(2,1)}, bf16[3,80,768]{2,1,0:T(8,128)(2,1)S(1)}, u32[]{:S(2)}, u32[]{:S(2)}) collective-permute-start(bf16[3,80,768]{2,1,0:T(8,128)(2,1)} %get-tuple-element.83), channel_id=1, source_target_pairs={{0,16},{1,17},{2,18},{3,19},{4,20},{5,21},{6,22},{7,23},{8,24},{9,... | collective-permute-start | bytes 1105928 | tf_op jit(solution)/shard_map/ppermute | solution.py:31
  230.3 34.7 %collective-permute-start.19 = (bf16[3,80,768]{2,1,0:T(8,128)(2,1)}, bf16[3,80,768]{2,1,0:T(8,128)(2,1)S(1)}, u32[]{:S(2)}, u32[]{:S(2)}) collective-permute-start(bf16[3,80,768]{2,1,0:T(8,128)(2,1)} %get-tuple-element.84), channel_id=1, source_target_pairs={{0,24},{1,25},{2,26},{3,27},{4,28},{5,29},{6,30},{7,31},{8,16},{9,... | collective-permute-start | bytes 1105928 | tf_op jit(solution)/shard_map/ppermute | solution.py:31
  241.6 35.1 %collective-permute-start.21 = (bf16[3,80,768]{2,1,0:T(8,128)(2,1)}, bf16[3,80,768]{2,1,0:T(8,128)(2,1)S(1)}, u32[]{:S(2)}, u32[]{:S(2)}) collective-permute-start(bf16[3,80,768]{2,1,0:T(8,128)(2,1)} %get-tuple-element.87), channel_id=1, source_target_pairs={{0,8},{1,9},{2,10},{3,11},{4,12},{5,13},{6,14},{7,15},{8,0},{9,1},... | collective-permute-start | bytes 1105928 | tf_op jit(solution)/shard_map/ppermute | solution.py:31
  244.7 32.0 %collective-permute-start.22 = (bf16[3,80,768]{2,1,0:T(8,128)(2,1)}, bf16[3,80,768]{2,1,0:T(8,128)(2,1)S(1)}, u32[]{:S(2)}, u32[]{:S(2)}) collective-permute-start(bf16[3,80,768]{2,1,0:T(8,128)(2,1)} %get-tuple-element.88), channel_id=1, source_target_pairs={{0,16},{1,17},{2,18},{3,19},{4,20},{5,21},{6,22},{7,23},{8,24},{9,... | collective-permute-start | bytes 1105928 | tf_op jit(solution)/shard_map/ppermute | solution.py:31
  249.9 26.8 %collective-permute-start.23 = (bf16[3,80,768]{2,1,0:T(8,128)(2,1)S(1)}, bf16[3,80,768]{2,1,0:T(8,128)(2,1)S(1)}, u32[]{:S(2)}, u32[]{:S(2)}) collective-permute-start(bf16[3,80,768]{2,1,0:T(8,128)(2,1)S(1)} %copy-done.29), channel_id=1, source_target_pairs={{0,24},{1,25},{2,26},{3,27},{4,28},{5,29},{6,30},{7,31},{8,16},{9,... | collective-permute-start | bytes 1105928 | tf_op jit(solution)/shard_map/ppermute | solution.py:31
  277.7 12.2 %collective-permute-start.25 = (bf16[2,4,2,24,3072]{4,3,2,1,0:T(8,128)(2,1)}, bf16[2,4,2,24,3072]{4,3,2,1,0:T(8,128)(2,1)S(1)}, u32[]{:S(2)}, u32[]{:S(2)}) collective-permute-start(bf16[2,4,2,24,3072]{4,3,2,1,0:T(8,128)(2,1)} %bitcast.60), channel_id=1, source_target_pairs={{0,8},{1,9},{2,10},{3,11},{4,12},{5,13},{6,14},{7,15},{8,0},{9,1},... | collective-permute-start | bytes 7077896 | tf_op jit(solution)/shard_map/ppermute | solution.py:31
  282.2 28.2 %all-to-all-start = ((bf16[32,24,128]{2,1,0:T(8,128)(2,1)}), bf16[32,24,128]{2,1,0:T(8,128)(2,1)}, u32[]{:S(2)}, u32[]{:S(2)}) async-start(bf16[32,24,128]{2,1,0:T(8,128)(2,1)} %bitcast.62), calls=%async_computation | async-start | bytes 393216 | tf_op jit(solution)/shard_map/all_to_all | solution.py:861
  296.0 18.2 %collective-permute-start.26 = (bf16[2,4,24,3072]{3,2,1,0:T(8,128)(2,1)}, bf16[2,4,24,3072]{3,2,1,0:T(8,128)(2,1)S(1)}, u32[]{:S(2)}, u32[]{:S(2)}) collective-permute-start(bf16[2,4,24,3072]{3,2,1,0:T(8,128)(2,1)} %shard_map.314), channel_id=1, source_target_pairs={{0,16},{1,17},{2,18},{3,19},{4,20},{5,21},{6,22},{7,23},{8,9},{9,8... | collective-permute-start | bytes 3538952 | tf_op jit(solution)/shard_map/ppermute | solution.py:31
  298.2 21.4 %collective-permute-start.31 = (bf16[24,6144]{1,0:T(8,128)(2,1)}, bf16[24,6144]{1,0:T(8,128)(2,1)S(1)}, u32[]{:S(2)}, u32[]{:S(2)}) collective-permute-start(bf16[24,6144]{1,0:T(8,128)(2,1)} %get-tuple-element.119), channel_id=1, source_target_pairs={{0,2},{1,3},{2,0},{3,1},{4,6},{5,7},{6,4},{7,5},{8,10},{9,11},{10,... | collective-permute-start | bytes 884744 | tf_op jit(solution)/shard_map/ppermute | solution.py:31
  299.7 23.5 %collective-permute-start.32 = (bf16[24,6144]{1,0:T(8,128)(2,1)S(1)}, bf16[24,6144]{1,0:T(8,128)(2,1)S(1)}, u32[]{:S(2)}, u32[]{:S(2)}) collective-permute-start(bf16[24,6144]{1,0:T(8,128)(2,1)S(1)} %get-tuple-element.121), channel_id=1, source_target_pairs={{0,4},{1,5},{2,6},{3,7},{4,0},{5,1},{6,2},{7,3},{8,12},{9,13},{10,... | collective-permute-start | bytes 884744 | tf_op jit(solution)/shard_map/ppermute | solution.py:31
  302.1 21.0 %collective-permute-start.33 = (bf16[24,6144]{1,0:T(8,128)(2,1)S(1)}, bf16[24,6144]{1,0:T(8,128)(2,1)}, u32[]{:S(2)}, u32[]{:S(2)}) collective-permute-start(bf16[24,6144]{1,0:T(8,128)(2,1)S(1)} %get-tuple-element.120), channel_id=1, source_target_pairs={{0,6},{1,7},{2,4},{3,5},{4,2},{5,3},{6,0},{7,1},{8,14},{9,15},{10,... | collective-permute-start | bytes 884744 | tf_op jit(solution)/shard_map/ppermute | solution.py:31
  318.1 10.1 %collective-permute-start.27 = (bf16[1,4,24,3072]{3,2,1,0:T(8,128)(2,1)}, bf16[1,4,24,3072]{3,2,1,0:T(8,128)(2,1)S(1)}, u32[]{:S(2)}, u32[]{:S(2)}) collective-permute-start(bf16[1,4,24,3072]{3,2,1,0:T(8,128)(2,1)} %shard_map.315), channel_id=1, source_target_pairs={{0,1},{1,0},{2,3},{3,2},{4,5},{5,4},{6,7},{7,6},{8,24},{9,25},{10,... | collective-permute-start | bytes 1769480 | tf_op jit(solution)/shard_map/ppermute | solution.py:31
  335.0 13.0 %collective-permute-start.29 = (bf16[24,3072]{1,0:T(8,128)(2,1)S(1)}, bf16[24,3072]{1,0:T(8,128)(2,1)S(1)}, u32[]{:S(2)}, u32[]{:S(2)}) collective-permute-start(bf16[24,3072]{1,0:T(8,128)(2,1)S(1)} %get-tuple-element.126), channel_id=1, source_target_pairs={{0,4},{1,5},{2,6},{3,7},{4,0},{5,1},{6,2},{7,3},{8,12},{9,13},{10,... | collective-permute-start | bytes 442376 | tf_op jit(solution)/shard_map/ppermute | solution.py:31
  337.2 10.8 %collective-permute-start.30 = (bf16[24,3072]{1,0:T(8,128)(2,1)S(1)}, bf16[24,3072]{1,0:T(8,128)(2,1)S(1)}, u32[]{:S(2)}, u32[]{:S(2)}) collective-permute-start(bf16[24,3072]{1,0:T(8,128)(2,1)S(1)} %get-tuple-element.125), channel_id=1, source_target_pairs={{0,6},{1,7},{2,4},{3,5},{4,2},{5,3},{6,0},{7,1},{8,14},{9,15},{10,... | collective-permute-start | bytes 442376 | tf_op jit(solution)/shard_map/ppermute | solution.py:31
  (37 other events, 134.4 us)
Sparse Core Ops, SparseCore 0:
  10.9 112.9 all-gather.1
where the time goes:
time: 359 us; the launch traced here: 357 us
  Pallas kernels  177 us (49%)
  waiting for transfers between devices  75.7 us (21%)
  starting transfers between devices  53.3 us (15%)
  local copies, waits for them, and re-layouts  27.5 us (8%)
  between operations  14.5 us (4%)
  other arithmetic  9.13 us (3%)
    pallas_call x5, Pallas kernels, call(): pl.pallas_call(run, grid=(slots,), in_specs=specs + [ANY] * len(extra), o...  74.5 us
    ppermute x34, waiting for transfers between devices, swap(): return lax.ppermute(value, AXES, pairs)  63.6 us
    pallas_call x1, Pallas kernels, mlp(): pl.pallas_call(body, grid_spec=pltpu.PrefetchScalarGridSpec(num_scalar_pr...  47.6 us
    ppermute x34, starting transfers between devices, swap(): return lax.ppermute(value, AXES, pairs)  45.5 us
    pallas_call x6, Pallas kernels, add(): pl.pallas_call(body, grid_spec=pltpu.PrefetchScalarGridSpec(num_scalar_pr...  23.6 us
    all_gather x1, waiting for transfers between devices, body(): lax.all_gather(side_by_side(w_out, w_up, w_down), AXES, axis=0, tiled=True)  12.1 us
    unnamed x66, local copies, waits for them, and re-layouts  11.9 us
    pallas_call x1, Pallas kernels, row_grad(): pl.pallas_call(body, grid_spec=pltpu.PrefetchScalarGridSpec(num_scalar_pr...  10.9 us
  transfers between devices with their start and end apart: 36, of which 14 were waited for; matrix products, arithmetic and copies ran while one was open for 6% of the time, Pallas kernels for 32%

commit v1 on v0

--- a/solution.py
+++ b/solution.py
@@ -335,7 +335,7 @@
     h2_ref[0] = (n * vec_ref[5:6] + vec_ref[6:7]).astype(jnp.bfloat16)
 
 
-def mlp(here, h2, cot, tags, rest, up_bias, shard):
+def mlp(here, h2, x2, cot, tags, rest, vec, up_bias, shard):
     slots, length, model = h2.shape
     rows = slots * length
     hidden = up_bias.shape[1]
@@ -344,11 +344,12 @@
     chunk = model // peers
     bf, f32 = jnp.bfloat16, jnp.float32
 
-    def body(here_ref, h2_ref, tag_ref, u_ref, b_ref, *refs):
+    def body(here_ref, h2_ref, x2_ref, tag_ref, vec_ref, u_ref, b_ref, *refs):
         cot_refs = refs[:peers]
         down_refs = refs[peers : peers + steps]
-        y_ref, gh_ref, gm_ref, sent_ref, kept_ref, gub_ref, gdb_ref, y_acc, gh_acc, ups, downs, sems = refs[
-            peers + steps :
+        out_refs = refs[peers + steps : 2 * peers + steps]
+        gh_ref, gm_ref, sent_ref, kept_ref, gub_ref, gdb_ref, y_acc, gh_acc, ups, downs, sems = refs[
+            2 * peers + steps :
         ]
         step = pl.program_id(0)
         core = here_ref[1]
@@ -430,7 +431,13 @@
 
         @pl.when(step == steps - 1)
         def _():
-            y_ref[...] = y_acc[...].reshape(y_ref.shape)
+            width = length // peers
+            for slot in range(slots):
+                y = y_acc[slot * length : (slot + 1) * length] + vec_ref[7:8]
+                keep = (tag_ref[slot] & 1).astype(f32)
+                result = (keep * (x2_ref[slot] + y)).astype(bf)
+                for index, ref in enumerate(out_refs):
+                    ref[slot] = result[index * width : (index + 1) * width]
             gh_ref[...] = gh_acc[...].reshape(gh_ref.shape)
             for copy in up_copies() + down_copies(kept_ref):
                 copy.wait()
@@ -442,14 +449,16 @@
     shape = (slots, length, model)
     side = jax.ShapeDtypeStruct((2, chunk, 2 * hidden), bf)
     line = jax.ShapeDtypeStruct((1, model), f32)
-    return pl.pallas_call(
+    results = pl.pallas_call(
         body,
         grid_spec=pltpu.PrefetchScalarGridSpec(
             num_scalar_prefetch=1,
             grid=(steps,),
             in_specs=[
                 full,
+                full,
                 pl.BlockSpec(tags.shape, lambda i, h: (0, 0, 0)),
+                pl.BlockSpec(vec.shape, lambda i, h: (0, 0)),
                 pl.BlockSpec((model, model), lambda i, h: (0, 1 + at(i, h))),
                 pl.BlockSpec((1, model), lambda i, h: (0, at(i, h))),
             ]
@@ -458,8 +467,8 @@
                 pl.BlockSpec((chunk, model), lambda i, h, c=1 + steps + step: (at(i, h), c))
                 for step in range(steps)
             ],
-            out_specs=[
-                full,
+            out_specs=[pl.BlockSpec(cot[0].shape, lambda i, h: (0, 0, 0))] * peers
+            + [
                 full,
                 full,
                 ANY,
@@ -475,8 +484,8 @@
                 pltpu.SemaphoreType.DMA((4 + steps,)),
             ],
         ),
-        out_shape=[
-            jax.ShapeDtypeStruct(shape, f32),
+        out_shape=[jax.ShapeDtypeStruct(cot[0].shape, bf)] * peers
+        + [
             jax.ShapeDtypeStruct(shape, f32),
             jax.ShapeDtypeStruct(shape, bf),
             side,
@@ -488,7 +497,8 @@
         cost_estimate=pl.CostEstimate(
             flops=12 * rows * model * hidden, bytes_accessed=30 * rows * model, transcendentals=rows * hidden
         ),
-    )(here, h2, tags, rest, up_bias, *cot, *([rest] * steps))
+    )(here, h2, x2, tags, vec, rest, up_bias, *cot, *([rest] * steps))
+    return [list(results[:peers])] + list(results[peers:])
 
 
 def norm_back(grad, n, scale, gain):
@@ -498,12 +508,9 @@
     return (gn - mean - n * cross) * scale
 
 
-def middle_kernel(y_ref, gh_ref, wo_ref, x2_ref, gm_ref, tag_ref, vec_ref, out_ref, gx_ref, ga_ref, go_ref, gg_ref, gb_ref, gob_ref):
-    x2 = x2_ref[0]
-    keep = (tag_ref[0] & 1).astype(jnp.float32)
-    spread(out_ref, (keep * (x2 + (y_ref[0] + vec_ref[7:8]))).astype(jnp.bfloat16))
+def middle_kernel(gh_ref, wo_ref, x2_ref, gm_ref, vec_ref, gx_ref, ga_ref, go_ref, gg_ref, gb_ref, gob_ref):
     gh = gh_ref[0]
-    n, scale = normalize(x2)
+    n, scale = normalize(x2_ref[0])
     add_rows(gg_ref, gh * n)
     add_rows(gb_ref, gh)
     gx = gm_ref[0].astype(jnp.float32) + norm_back(gh, n, scale, vec_ref[5:6])
@@ -769,7 +776,7 @@
         return choose
 
     def exchange(pieces):
-        return list(pieces[:1]) + [swap(sizes, pieces[bits], frame_peer(bits)) for bits in range(1, peers)]
+        return list(pieces[:1]) + [swap(sizes, pieces[bits], frame_peer(bits)) for bits in range(1, len(pieces))]
 
     def slots_for(value):
         own = value.shape[0] // peers
@@ -820,16 +827,18 @@
         slots,
         2 * here_rows * model * model,
     )
-    y, gh, gm, sent, kept, gub, gdb = mlp(here, h2, cot, tag_columns, rest, up_bias_row, rows)
+    out, gh, gm, sent, kept, gub, gdb = mlp(here, h2, x2, cot, tag_columns, rest, vec, up_bias_row, rows)
     put_rest = Scatter(sizes, here, sent, kept)
-    out, gx, ga, go, gmg, gmb, gob = call(
+    gx, ga, go, gmg, gmb, gob = call(
         middle_kernel,
-        [(y, "slot"), (gh, "slot"), (rest, 0), (x2, "slot"), (gm, "slot"), (tag_columns, "slot"), (vec, "whole")],
-        [framed, (full, f32), (full, bf), (full, bf)] + [((1, model), f32)] * 3,
+        [(gh, "slot"), (rest, 0), (x2, "slot"), (gm, "slot"), (vec, "whole")],
+        [(full, f32), (full, bf), (full, bf)] + [((1, model), f32)] * 3,
         slots,
         2 * here_rows * model * model,
     )
-    put_rest.hold([go])
+    late = out[3:]
+    out = exchange(out[:3])
+    put_rest.hold([go] + out[1:])
     put_rest.second()
     g_mix, gqb, gvb = call(
         attend_back_kernel,
@@ -841,28 +850,30 @@
     )
     put_rest.hold([g_mix])
     put_rest.third()
+    out += [swap(sizes, piece, frame_peer(3 + index)) for index, piece in enumerate(hold(late, [g_mix]))]
+    sent, kept = row_grad(here, [(h1, g_mix), (o, ga)], [put_rest.sent])
+    put_mixed = Scatter(sizes, here, sent, kept)
     in_grad, gag, gab = call(
         input_kernel,
         [(g_mix, "slot"), (mixed, "whole"), (x, "frames"), (gx, "slot"), (vec, "whole")],
         [framed] + [((1, model), f32)] * 2,
         slots,
         6 * here_rows * model * model,
-        after=[put_rest.sent],
+        after=[kept],
     )
-    out = exchange(hold(out, [g_mix]))
-    in_grad = exchange(in_grad)
-    put_rest.hold([gag])
+    put_mixed.hold([gag])
+    put_mixed.second()
+    put_rest.hold([put_mixed.sent])
     put_rest.fourth()
-    sent, kept = row_grad(here, [(h1, g_mix), (o, ga)], [gag, put_rest.sent] + out[1:])
-    put_mixed = Scatter(sizes, here, hold([sent], in_grad[1:])[0], kept)
-    put_mixed.second()
+    put_mixed.third()
+    in_grad = exchange(list(hold(in_grad, [put_mixed.sent])))
+    out = list(hold(out, [put_mixed.sent]))
+    put_mixed.fourth()
+    in_grad = list(hold(in_grad, [put_mixed.sent]))
     sums = [gag, gab, gqb, gvb, gob, gmg, gmb, gdb]
-    pack = turned(sums, gub.reshape(-1, ratio), [])
+    pack = turned(sums, gub.reshape(-1, ratio), [put_mixed.sent])
     pack = lax.all_to_all(pack.reshape(-1, rows, 128), AXES, 0, 0, tiled=True)
     last = jnp.sum(pack.astype(f32), axis=0)
-    put_mixed.third()
-    put_mixed.hold([pack])
-    put_mixed.fourth()
     rest_rows = put_rest.last()
     g_up = rest_rows[:, :hidden]
     g_down = rest_rows[:, hidden:].reshape(rows, ratio, model).transpose(1, 0, 2).reshape(ratio * rows, model)

time: 359 us -> 343 us (0.955)
  waiting for transfers between devices: 75.7 us -> 67.5 us
  starting transfers between devices: 53.3 us -> 48.5 us
    ppermute x34, waiting for transfers between devices: 63.6 us -> 55 us  [swap(): return lax.ppermute(value, AXES, pairs)]
    all_to_all x1, starting transfers between devices: 7.74 us -> 3.48 us  [body(): pack = lax.all_to_all(pack.reshape(-1, rows, 128), AXES, 0, 0, tiled=True)]
    unnamed x66 -> x64, local copies, waits for them, and re-layouts: 11.9 us -> 11.8 us
  transfers between devices with their start and end apart: 36 -> 36, of which waited for: 14 -> 12; matrix products, arithmetic and copies ran while one was open for 6% -> 6% of each run, Pallas kernels for 32% -> 31%
where the time goes in v1:
time: 343 us; the launch traced here: 341 us
  Pallas kernels  176 us (51%)
  waiting for transfers between devices  67.5 us (20%)
  starting transfers between devices  48.5 us (14%)
  local copies, waits for them, and re-layouts  27 us (8%)
  between operations  14.5 us (4%)
  other arithmetic  8.38 us (2%)
    pallas_call x5, Pallas kernels, call(): pl.pallas_call(run, grid=(slots,), in_specs=specs + [ANY] * len(extra), o...  72.4 us
    ppermute x34, waiting for transfers between devices, swap(): return lax.ppermute(value, AXES, pairs)  55 us
    pallas_call x1, Pallas kernels, mlp(): pl.pallas_call(body, grid_spec=pltpu.PrefetchScalarGridSpec(num_scalar_pr...  48.1 us
    ppermute x34, starting transfers between devices, swap(): return lax.ppermute(value, AXES, pairs)  44.9 us
    pallas_call x6, Pallas kernels, add(): pl.pallas_call(body, grid_spec=pltpu.PrefetchScalarGridSpec(num_scalar_pr...  23.5 us
    unnamed x64, local copies, waits for them, and re-layouts  11.8 us
    all_gather x1, waiting for transfers between devices, body(): lax.all_gather(side_by_side(w_out, w_up, w_down), AXES, axis=0, tiled=True)  11.3 us
    pallas_call x1, Pallas kernels, row_grad(): pl.pallas_call(body, grid_spec=pltpu.PrefetchScalarGridSpec(num_scalar_pr...  11.1 us
  transfers between devices with their start and end apart: 36, of which 12 were waited for; matrix products, arithmetic and copies ran while one was open for 6% of the time, Pallas kernels for 31%

profile of v1, /device:TPU:0, one launch (start us, length us, event | category | flops | bytes accessed | tf_op | source)
XLA Modules:
  0.0 341.5 jit_solution(17060126413218319977)
XLA Ops:
  21.2 2.6 collective-permute-start.4
  23.7 2.8 collective-permute-done.3.refs_0_
  26.5 5.9 %collective-permute-start.5 = (bf16[24,2432]{1,0:T(8,128)(2,1)S(1)}, bf16[24,2432]{1,0:T(8,128)(2,1)S(1)}, u32[]{:S(2)}, u32[]{:S(2)}) collective-permute-start(bf16[24,2432]{1,0:T(8,128)(2,1)S(1)} %get-tuple-element.142), channel_id=1, source_target_pairs={{0,6},{1,7},{2,4},{3,5},{4,2},{5,3},{6,0},{7,1},{8,14},{9,15},{10,... | collective-permute-start | bytes 350216 | tf_op jit(solution)/shard_map/ppermute | solution.py:31
  32.4 5.4 %collective-permute-done.4.refs_1_ = bf16[24,2432]{1,0:T(8,128)(2,1)S(1)} collective-permute-done((bf16[24,2432]{1,0:T(8,128)(2,1)S(1)}, bf16[24,2432]{1,0:T(8,128)(2,1)S(1)}, u32[]{:S(2)}, u32[]{:S(2)}) %collective-permute-start.4) | collective-permute-done | bytes 116768 | tf_op jit(solution)/shard_map/ppermute | solution.py:31
  43.9 14.4 %collective-permute-done.6.refs_1_ = bf16[4,24,2432]{2,1,0:T(8,128)(2,1)S(1)} collective-permute-done((bf16[4,24,2432]{2,1,0:T(8,128)(2,1)S(1)}, bf16[4,24,2432]{2,1,0:T(8,128)(2,1)S(1)}, u32[]{:S(2)}, u32[]{:S(2)}) %collective-permute-start.6) | collective-permute-done | bytes 466976 | tf_op jit(solution)/shard_map/ppermute | solution.py:31
  61.9 7.7 %collective-permute-done.8.refs_3_ = bf16[4,24,2432]{2,1,0:T(8,128)(2,1)S(1)} collective-permute-done((bf16[4,24,2432]{2,1,0:T(8,128)(2,1)}, bf16[4,24,2432]{2,1,0:T(8,128)(2,1)S(1)}, u32[]{:S(2)}, u32[]{:S(2)}) %collective-permute-start.8) | collective-permute-done | bytes 466976 | tf_op jit(solution)/shard_map/ppermute | solution.py:31
  72.3 4.9 %shard_map.292 = (bf16[2,2,4,2,24,2432]{5,4,3,2,1,0:T(8,128)(2,1)}, f32[16,768]{1,0:T(8,128)}) custom-call(s32[4]{0:T(128)} %pad_add_fusion.here_ref, bf16[4,24,2432]{2,1,0:T(8,128)(2,1)} %copy-done.9, bf16[4,24,2432]{2,1,0:T(8,128)(2,1)} %copy-done.10, bf16[4,24,2432]{2,1,0:T(8,128)(2,1)} %shard_map.291.refs_2_, bf16[4,24,2432]{2,1,0:T(8,128)(2,1)} %copy-done.21, ...), custom_call_target="tpu_custom_call" | custom-call | tf_op jit(solution)/shard_map/pallas_call | solution.py:156
  82.4 2.9 collective-permute-start.14
  85.3 25.1 %shard_map.293 = (bf16[3,320,768]{2,1,0:T(8,128)(2,1)}, bf16[3,320,2304]{2,1,0:T(8,128)(2,1)}, bf16[3,320,768]{2,1,0:T(8,128)(2,1)}, bf16[3,12,320,320]{3,2,1,0:T(8,128)(2,1)}, s32[3,320,1]{2,1,0:T(8,128)}) custom-call(bf16[3,88,768]{2,1,0:T(8,128)(2,1)} %get-tuple-element.128.refs_0_.refs_2_, bf16[3,88,768]{2,1,0:T(8,128)(2,1)} %copy-done.4, ...), custom_call_target="tpu_custom_call" | custom-call | flops 7172259840 | bytes 20156160 | tf_op jit(solution)/shard_map/pallas_call | solution.py:605
  112.2 11.3 %all-gather.2.cloned.1.call-done.refs_5_.u_ref.refs_4_.refs_6_.refs_7_.refs_1_ = bf16[768,6912]{1,0:T(8,128)(2,1)} async-done(((bf16[24,6912]{1,0:T(8,128)(2,1)}), bf16[768,6912]{1,0:T(8,128)(2,1)}) %all-gather.2.cloned.1.call-update) | async-done | bytes 10616848 | tf_op jit(solution)/shard_map/all_gather | solution.py:802
  123.5 6.0 %shard_map.295 = (f32[3,320,768]{2,1,0:T(8,128)}, bf16[3,320,768]{2,1,0:T(8,128)(2,1)}) custom-call(bf16[3,88,768]{2,1,0:T(8,128)(2,1)} %get-tuple-element.128.refs_0_.refs_2_, bf16[3,88,768]{2,1,0:T(8,128)(2,1)} %copy-done.4, bf16[3,88,768]{2,1,0:T(8,128)(2,1)} %copy-done.5, bf16[3,88,768]{2,1,0:T(8,128)(2,1)} %copy-done.6, ...), custom_call_target="tpu_custom_call" | custom-call | flops 1132462080 | bytes 18186240 | tf_op jit(solution)/shard_map/pallas_call | solution.py:605
  130.5 48.1 %shard_map.297 = (bf16[3,80,768]{2,1,0:T(8,128)(2,1)}, bf16[3,80,768]{2,1,0:T(8,128)(2,1)}, bf16[3,80,768]{2,1,0:T(8,128)(2,1)}, bf16[3,80,768]{2,1,0:T(8,128)(2...) custom-call(s32[4]{0:T(128)} %pad_add_fusion.here_ref, ...), custom_call_target="tpu_custom_call" | custom-call | flops 27179089920 | bytes 22118400 | tf_op jit(solution)/shard_map/pallas_call | solution.py:452
  179.2 7.9 %shard_map.298 = (f32[3,320,768]{2,1,0:T(8,128)}, bf16[3,320,768]{2,1,0:T(8,128)(2,1)}, bf16[3,320,768]{2,1,0:T(8,128)(2,1)}, f32[1,768]{1,0:T(1,128)}, f32[1,768]{1,0:T(1,128)}, /*index=5*/f32[1,768]{1,0:T(1,128)}) custom-call(f32[3,320,768]{2,1,0:T(8,128)} %get-tuple-element.80.refs_0_, ...), custom_call_target="tpu_custom_call" | custom-call | flops 1132462080 | bytes 23946240 | tf_op jit(solution)/shard_map/pallas_call | solution.py:605
  187.1 2.9 collective-permute-done.17.refs_3_.refs_2_
  190.7 5.2 %shard_map.300.refs_3_ = bf16[2,4,24,6144]{3,2,1,0:T(8,128)(2,1)} custom-call(s32[4]{0:T(128)} %pad_add_fusion.here_ref, bf16[2,4,2,24,6144]{4,3,2,1,0:T(8,128)(2,1)} %shard_map.299.refs_0_, bf16[2,4,2,24,6144]{4,3,2,1,0:T(8,128)(2,1)} %collective-permute-done.18.refs_1_), custom_call_target="tpu_custom_call" | custom-call | bytes 7077888 | tf_op jit(solution)/shard_map/pallas_call | solution.py:203
  196.2 24.0 %shard_map.301 = (bf16[3,320,2304]{2,1,0:T(8,128)(2,1)}, f32[1,768]{1,0:T(1,128)}, f32[1,768]{1,0:T(1,128)}) custom-call(bf16[3,320,2304]{2,1,0:T(8,128)(2,1)} %get-tuple-element.79.refs_0_, bf16[3,320,768]{2,1,0:T(8,128)(2,1)} %get-tuple-element.82.refs_1_, bf16[3,12,320,320]{3,2,1,0:T(8,128)(2,1)} %get-tuple-element.83.refs_2_, ...), custom_call_target="tpu_custom_call" | custom-call | flops 7549747200 | bytes 17700864 | tf_op jit(solution)/shard_map/pallas_call | solution.py:605
  220.2 4.8 %collective-permute-done.20.refs_2_ = bf16[2,4,24,6144]{3,2,1,0:T(8,128)(2,1)S(1)} collective-permute-done((bf16[2,4,24,6144]{3,2,1,0:T(8,128)(2,1)}, bf16[2,4,24,6144]{3,2,1,0:T(8,128)(2,1)S(1)}, u32[]{:S(2)}, u32[]{:S(2)}) %collective-permute-start.20) | collective-permute-done | bytes 2359328 | tf_op jit(solution)/shard_map/ppermute | solution.py:31
  226.4 3.7 %shard_map.304.refs_4_ = bf16[1,4,24,6144]{3,2,1,0:T(8,128)(2,1)} custom-call(s32[4]{0:T(128)} %pad_add_fusion.here_ref, bf16[2,4,2,24,6144]{4,3,2,1,0:T(8,128)(2,1)} %shard_map.303.refs_0_, bf16[2,4,2,24,6144]{4,3,2,1,0:T(8,128)(2,1)} %collective-permute-done.18.refs_1_, bf16[2,4,24,6144]{3,2,1,0:T(8,128)(2,1)} %copy-done.1), custom_call_target="tpu_custom_call" | custom-call | bytes 4718592 | tf_op jit(solution)/shard_map/pallas_call | solution.py:203
  230.1 11.1 %shard_map.305 = (bf16[2,192,3072]{2,1,0:T(8,128)(2,1)}, bf16[2,192,3072]{2,1,0:T(8,128)(2,1)}) custom-call(s32[4]{0:T(128)} %pad_add_fusion.here_ref, bf16[3,320,768]{2,1,0:T(8,128)(2,1)} %get-tuple-element.87.refs_0_, bf16[3,320,2304]{2,1,0:T(8,128)(2,1)} %get-tuple-element.86.refs_1_.refs_0_, bf16[3,320,768]{2,1,0:T(8,128)(2,1)} %get-tuple-element.71.refs_4_.refs_2_, ...), custom_call_target="tpu_custom_call" | custom-call | flops 4529848320 | bytes 5898240 | tf_op jit(solution)/shard_map/pallas_call | solution.py:661
  241.1 2.9 collective-permute-start.30
  244.0 9.4 %shard_map.306 = (bf16[3,80,768]{2,1,0:T(8,128)(2,1)}, bf16[3,80,768]{2,1,0:T(8,128)(2,1)}, bf16[3,80,768]{2,1,0:T(8,128)(2,1)}, bf16[3,80,768]{2,1,0:T(8,128)(2...) custom-call(bf16[3,320,2304]{2,1,0:T(8,128)(2,1)} %get-tuple-element.86.refs_1_.refs_0_, bf16[768,2432]{1,0:T(8,128)(2,1)} %bitcast.56, ...), custom_call_target="tpu_custom_call" | custom-call | flops 3397386240 | bytes 14260224 | tf_op jit(solution)/shard_map/pallas_call | solution.py:605
  254.9 4.4 %shard_map.308.refs_1_ = bf16[2,4,24,3072]{3,2,1,0:T(8,128)(2,1)} custom-call(s32[4]{0:T(128)} %pad_add_fusion.here_ref, bf16[2,4,2,24,3072]{4,3,2,1,0:T(8,128)(2,1)} %shard_map.307.refs_0_, bf16[2,4,2,24,3072]{4,3,2,1,0:T(8,128)(2,1)} %copy-done), custom_call_target="tpu_custom_call" | custom-call | bytes 3538944 | tf_op jit(solution)/shard_map/pallas_call | solution.py:203
  260.8 4.1 %shard_map.318 = bf16[1,4,24,6144]{3,2,1,0:T(8,128)(2,1)} custom-call(s32[4]{0:T(128)} %pad_add_fusion.here_ref, bf16[2,4,2,24,6144]{4,3,2,1,0:T(8,128)(2,1)} %shard_map.317.refs_0_, bf16[2,4,2,24,6144]{4,3,2,1,0:T(8,128)(2,1)} %collective-permute-done.18.refs_1_, bf16[2,4,24,6144]{3,2,1,0:T(8,128)(2,1)} %copy-done.1, ...), custom_call_target="tpu_custom_call" | custom-call | bytes 5898240 | tf_op jit(solution)/shard_map/pallas_call | solution.py:203
  267.0 6.6 %collective-permute-start.31 = (bf16[24,6144]{1,0:T(8,128)(2,1)}, bf16[24,6144]{1,0:T(8,128)(2,1)S(1)}, u32[]{:S(2)}, u32[]{:S(2)}) collective-permute-start(bf16[24,6144]{1,0:T(8,128)(2,1)} %get-tuple-element.133), channel_id=1, source_target_pairs={{0,2},{1,3},{2,0},{3,1},{4,6},{5,7},{6,4},{7,5},{8,10},{9,11},{10,... | collective-permute-start | bytes 884744 | tf_op jit(solution)/shard_map/ppermute | solution.py:31
  280.0 2.9 shard_map.309.refs_4_
  283.3 2.8 collective-permute-done.31
  286.1 11.2 %collective-permute-done.32 = bf16[24,6144]{1,0:T(8,128)(2,1)} collective-permute-done((bf16[24,6144]{1,0:T(8,128)(2,1)}, bf16[24,6144]{1,0:T(8,128)(2,1)}, u32[]{:S(2)}, u32[]{:S(2)}) %collective-permute-start.32) | collective-permute-done | bytes 294944 | tf_op jit(solution)/shard_map/ppermute | solution.py:31
  301.4 3.2 shard_map.313
  305.7 5.6 %collective-permute-start.27 = (bf16[24,3072]{1,0:T(8,128)(2,1)S(1)}, bf16[24,3072]{1,0:T(8,128)(2,1)S(1)}, u32[]{:S(2)}, u32[]{:S(2)}) collective-permute-start(bf16[24,3072]{1,0:T(8,128)(2,1)S(1)} %get-tuple-element.138), channel_id=1, source_target_pairs={{0,2},{1,3},{2,0},{3,1},{4,6},{5,7},{6,4},{7,5},{8,10},{9,11},{10,... | collective-permute-start | bytes 442376 | tf_op jit(solution)/shard_map/ppermute | solution.py:31
  315.4 3.7 %shard_map.311 = bf16[12,80,768]{2,1,0:T(8,128)(2,1)} custom-call(s32[4]{0:T(128)} %pad_add_fusion.here_ref, bf16[3,80,768]{2,1,0:T(8,128)(2,1)} %get-tuple-element.93.refs_0_, bf16[3,80,768]{2,1,0:T(8,128)(2,1)} %get-tuple-element.94.refs_1_, bf16[3,80,768]{2,1,0:T(8,128)(2,1)} %get-tuple-element.95.refs_2_, bf16[3,80,768]{2,1,0:T(8,128)(2,1)} %get-tuple-element.96.refs_3_), custom_call_target="tpu_custom_call" | custom-call | tf_op jit(solution)/shard_map/pallas_call | solution.py:712
  321.0 3.5 %all-to-all-start = ((bf16[32,24,128]{2,1,0:T(8,128)(2,1)}), bf16[32,24,128]{2,1,0:T(8,128)(2,1)S(1)}, u32[]{:S(2)}, u32[]{:S(2)}) async-start(bf16[32,24,128]{2,1,0:T(8,128)(2,1)} %bitcast.60), calls=%async_computation | async-start | bytes 393216 | tf_op jit(solution)/shard_map/all_to_all | solution.py:875
  325.4 4.1 %shard_map.315 = f32[12,80,768]{2,1,0:T(8,128)} custom-call(s32[4]{0:T(128)} %pad_add_fusion.here_ref, bf16[3,80,768]{2,1,0:T(8,128)(2,1)} %get-tuple-element.105.refs_0_, bf16[3,80,768]{2,1,0:T(8,128)(2,1)} %get-tuple-element.106.refs_1_, bf16[3,80,768]{2,1,0:T(8,128)(2,1)} %get-tuple-element.107.refs_2_, bf16[3,80,768]{2,1,0:T(8,128)(2,1)} %get-tuple-element.108.refs_3_), custom_call_target="tpu_custom_call" | custom-call | tf_op jit(solution)/shard_map/pallas_call | solution.py:712
  (168 shorter events, 65.9 us)
Async XLA Ops:
  7.2 116.3 %all-gather.2.cloned.1.call-start = ((), (), s32[]{:S(2)}) async-start(), calls=%async_computation.1 | async-start | bytes 10948608 | tf_op jit(solution)/shard_map/all_gather | solution.py:802
  13.3 24.6 %collective-permute-start = (bf16[3,88,768]{2,1,0:T(8,128)(2,1)S(1)}, bf16[3,88,768]{2,1,0:T(8,128)(2,1)S(1)}, u32[]{:S(2)}, u32[]{:S(2)}) collective-permute-start(bf16[3,88,768]{2,1,0:T(8,128)(2,1)S(1)} %get-tuple-element.127), channel_id=1, source_target_pairs={{0,8},{1,9},{2,10},{3,11},{4,12},{5,13},{6,14},{7,15},{8,0},{9,1},... | collective-permute-start | bytes 1216520 | tf_op jit(solution)/shard_map/ppermute | solution.py:31
  13.7 24.2 %collective-permute-start.1 = (bf16[3,88,768]{2,1,0:T(8,128)(2,1)S(1)}, bf16[3,88,768]{2,1,0:T(8,128)(2,1)S(1)}, u32[]{:S(2)}, u32[]{:S(2)}) collective-permute-start(bf16[3,88,768]{2,1,0:T(8,128)(2,1)S(1)} %get-tuple-element.126), channel_id=1, source_target_pairs={{0,16},{1,17},{2,18},{3,19},{4,20},{5,21},{6,22},{7,23},{8,24},{9,... | collective-permute-start | bytes 1216520 | tf_op jit(solution)/shard_map/ppermute | solution.py:31
  16.2 21.7 %collective-permute-start.2 = (bf16[3,88,768]{2,1,0:T(8,128)(2,1)S(1)}, bf16[3,88,768]{2,1,0:T(8,128)(2,1)S(1)}, u32[]{:S(2)}, u32[]{:S(2)}) collective-permute-start(bf16[3,88,768]{2,1,0:T(8,128)(2,1)S(1)} %get-tuple-element.125), channel_id=1, source_target_pairs={{0,24},{1,25},{2,26},{3,27},{4,28},{5,29},{6,30},{7,31},{8,16},{9,... | collective-permute-start | bytes 1216520 | tf_op jit(solution)/shard_map/ppermute | solution.py:31
  21.2 16.7 %collective-permute-start.4 = (bf16[24,2432]{1,0:T(8,128)(2,1)S(1)}, bf16[24,2432]{1,0:T(8,128)(2,1)S(1)}, u32[]{:S(2)}, u32[]{:S(2)}) collective-permute-start(bf16[24,2432]{1,0:T(8,128)(2,1)S(1)} %get-tuple-element.142), channel_id=1, source_target_pairs={{0,4},{1,5},{2,6},{3,7},{4,0},{5,1},{6,2},{7,3},{8,12},{9,13},{10,... | collective-permute-start | bytes 350216 | tf_op jit(solution)/shard_map/ppermute | solution.py:31
  26.5 11.3 %collective-permute-start.5 = (bf16[24,2432]{1,0:T(8,128)(2,1)S(1)}, bf16[24,2432]{1,0:T(8,128)(2,1)S(1)}, u32[]{:S(2)}, u32[]{:S(2)}) collective-permute-start(bf16[24,2432]{1,0:T(8,128)(2,1)S(1)} %get-tuple-element.142), channel_id=1, source_target_pairs={{0,6},{1,7},{2,4},{3,5},{4,2},{5,3},{6,0},{7,1},{8,14},{9,15},{10,... | collective-permute-start | bytes 350216 | tf_op jit(solution)/shard_map/ppermute | solution.py:31
  40.7 17.6 %collective-permute-start.6 = (bf16[4,24,2432]{2,1,0:T(8,128)(2,1)S(1)}, bf16[4,24,2432]{2,1,0:T(8,128)(2,1)S(1)}, u32[]{:S(2)}, u32[]{:S(2)}) collective-permute-start(bf16[4,24,2432]{2,1,0:T(8,128)(2,1)S(1)} %pad_maximum_fusion.refs_0_), channel_id=1, source_target_pairs={{0,1},{1,0},{2,3},{3,2},{4,5},{5,4},{6,7},{7,6},{8,24},{9,25},{10,... | collective-permute-start | bytes 1400840 | tf_op jit(solution)/shard_map/ppermute | solution.py:31
  42.2 17.9 %collective-permute-start.7 = (bf16[4,24,2432]{2,1,0:T(8,128)(2,1)S(1)}, bf16[4,24,2432]{2,1,0:T(8,128)(2,1)S(1)}, u32[]{:S(2)}, u32[]{:S(2)}) collective-permute-start(bf16[4,24,2432]{2,1,0:T(8,128)(2,1)S(1)} %pad_maximum_fusion.refs_0_), channel_id=1, source_target_pairs={{0,16},{1,17},{2,18},{3,19},{4,20},{5,21},{6,22},{7,23},{8,9},{9,8... | collective-permute-start | bytes 1400840 | tf_op jit(solution)/shard_map/ppermute | solution.py:31
  60.8 8.8 %collective-permute-start.8 = (bf16[4,24,2432]{2,1,0:T(8,128)(2,1)}, bf16[4,24,2432]{2,1,0:T(8,128)(2,1)S(1)}, u32[]{:S(2)}, u32[]{:S(2)}) collective-permute-start(bf16[4,24,2432]{2,1,0:T(8,128)(2,1)} %shard_map.291.refs_2_), channel_id=1, source_target_pairs={{0,1},{1,0},{2,3},{3,2},{4,5},{5,4},{6,7},{7,6},{8,24},{9,25},{10,... | collective-permute-start | bytes 1400840 | tf_op jit(solution)/shard_map/ppermute | solution.py:31
  61.4 8.9 %collective-permute-start.9 = (bf16[4,24,2432]{2,1,0:T(8,128)(2,1)S(1)}, bf16[4,24,2432]{2,1,0:T(8,128)(2,1)S(1)}, u32[]{:S(2)}, u32[]{:S(2)}) collective-permute-start(bf16[4,24,2432]{2,1,0:T(8,128)(2,1)S(1)} %pad_maximum_fusion.refs_0_), channel_id=1, source_target_pairs={{0,8},{1,9},{2,10},{3,11},{4,12},{5,13},{6,14},{7,15},{8,0},{9,1},... | collective-permute-start | bytes 1400840 | tf_op jit(solution)/shard_map/ppermute | solution.py:31
  61.4 8.9 %collective-permute-start.11 = (bf16[4,24,2432]{2,1,0:T(8,128)(2,1)}, bf16[4,24,2432]{2,1,0:T(8,128)(2,1)S(1)}, u32[]{:S(2)}, u32[]{:S(2)}) collective-permute-start(bf16[4,24,2432]{2,1,0:T(8,128)(2,1)} %shard_map.291.refs_2_), channel_id=1, source_target_pairs={{0,8},{1,9},{2,10},{3,11},{4,12},{5,13},{6,14},{7,15},{8,0},{9,1},... | collective-permute-start | bytes 1400840 | tf_op jit(solution)/shard_map/ppermute | solution.py:31
  82.1 47.4 %collective-permute-start.13 = (bf16[3,80,768]{2,1,0:T(8,128)(2,1)S(1)}, bf16[3,80,768]{2,1,0:T(8,128)(2,1)S(1)}, u32[]{:S(2)}, u32[]{:S(2)}) collective-permute-start(bf16[3,80,768]{2,1,0:T(8,128)(2,1)S(1)} %get-tuple-element.131), channel_id=1, source_target_pairs={{0,8},{1,9},{2,10},{3,11},{4,12},{5,13},{6,14},{7,15},{8,0},{9,1},... | collective-permute-start | bytes 1105928 | tf_op jit(solution)/shard_map/ppermute | solution.py:31
  82.4 47.1 %collective-permute-start.14 = (bf16[3,80,768]{2,1,0:T(8,128)(2,1)S(1)}, bf16[3,80,768]{2,1,0:T(8,128)(2,1)S(1)}, u32[]{:S(2)}, u32[]{:S(2)}) collective-permute-start(bf16[3,80,768]{2,1,0:T(8,128)(2,1)S(1)} %get-tuple-element.130), channel_id=1, source_target_pairs={{0,16},{1,17},{2,18},{3,19},{4,20},{5,21},{6,22},{7,23},{8,24},{9,... | collective-permute-start | bytes 1105928 | tf_op jit(solution)/shard_map/ppermute | solution.py:31
  85.3 44.3 %collective-permute-start.15 = (bf16[3,80,768]{2,1,0:T(8,128)(2,1)S(1)}, bf16[3,80,768]{2,1,0:T(8,128)(2,1)S(1)}, u32[]{:S(2)}, u32[]{:S(2)}) collective-permute-start(bf16[3,80,768]{2,1,0:T(8,128)(2,1)S(1)} %get-tuple-element.129), channel_id=1, source_target_pairs={{0,24},{1,25},{2,26},{3,27},{4,28},{5,29},{6,30},{7,31},{8,16},{9,... | collective-permute-start | bytes 1105928 | tf_op jit(solution)/shard_map/ppermute | solution.py:31
  178.6 12.1 %collective-permute-start.18 = (bf16[2,4,2,24,6144]{4,3,2,1,0:T(8,128)(2,1)}, bf16[2,4,2,24,6144]{4,3,2,1,0:T(8,128)(2,1)}, u32[]{:S(2)}, u32[]{:S(2)}) collective-permute-start(bf16[2,4,2,24,6144]{4,3,2,1,0:T(8,128)(2,1)} %bitcast.73), channel_id=1, source_target_pairs={{0,8},{1,9},{2,10},{3,11},{4,12},{5,13},{6,14},{7,15},{8,0},{9,1},... | collective-permute-start | bytes 14155784 | tf_op jit(solution)/shard_map/ppermute | solution.py:31
  179.2 10.8 %collective-permute-start.17 = (bf16[3,80,768]{2,1,0:T(8,128)(2,1)}, bf16[3,80,768]{2,1,0:T(8,128)(2,1)S(1)}, u32[]{:S(2)}, u32[]{:S(2)}) collective-permute-start(bf16[3,80,768]{2,1,0:T(8,128)(2,1)} %get-tuple-element.77), channel_id=1, source_target_pairs={{0,16},{1,17},{2,18},{3,19},{4,20},{5,21},{6,22},{7,23},{8,24},{9,... | collective-permute-start | bytes 1105928 | tf_op jit(solution)/shard_map/ppermute | solution.py:31
  195.9 29.1 %collective-permute-start.20 = (bf16[2,4,24,6144]{3,2,1,0:T(8,128)(2,1)}, bf16[2,4,24,6144]{3,2,1,0:T(8,128)(2,1)S(1)}, u32[]{:S(2)}, u32[]{:S(2)}) collective-permute-start(bf16[2,4,24,6144]{3,2,1,0:T(8,128)(2,1)} %shard_map.300.refs_3_), channel_id=1, source_target_pairs={{0,16},{1,17},{2,18},{3,19},{4,20},{5,21},{6,22},{7,23},{8,9},{9,8... | collective-permute-start | bytes 7077896 | tf_op jit(solution)/shard_map/ppermute | solution.py:31
  241.1 12.3 %collective-permute-start.21 = (bf16[2,4,2,24,3072]{4,3,2,1,0:T(8,128)(2,1)}, bf16[2,4,2,24,3072]{4,3,2,1,0:T(8,128)(2,1)S(1)}, u32[]{:S(2)}, u32[]{:S(2)}) collective-permute-start(bf16[2,4,2,24,3072]{4,3,2,1,0:T(8,128)(2,1)} %bitcast.74), channel_id=1, source_target_pairs={{0,8},{1,9},{2,10},{3,11},{4,12},{5,13},{6,14},{7,15},{8,0},{9,1},... | collective-permute-start | bytes 7077896 | tf_op jit(solution)/shard_map/ppermute | solution.py:31
  241.1 19.7 %collective-permute-start.30 = (bf16[1,4,24,6144]{3,2,1,0:T(8,128)(2,1)S(1)}, bf16[1,4,24,6144]{3,2,1,0:T(8,128)(2,1)}, u32[]{:S(2)}, u32[]{:S(2)}) collective-permute-start(bf16[1,4,24,6144]{3,2,1,0:T(8,128)(2,1)S(1)} %copy-done.16), channel_id=1, source_target_pairs={{0,1},{1,0},{2,3},{3,2},{4,5},{5,4},{6,7},{7,6},{8,24},{9,25},{10,... | collective-permute-start | bytes 3538952 | tf_op jit(solution)/shard_map/ppermute | solution.py:31
  260.6 18.4 %collective-permute-start.22 = (bf16[2,4,24,3072]{3,2,1,0:T(8,128)(2,1)S(1)}, bf16[2,4,24,3072]{3,2,1,0:T(8,128)(2,1)S(1)}, u32[]{:S(2)}, u32[]{:S(2)}) collective-permute-start(bf16[2,4,24,3072]{3,2,1,0:T(8,128)(2,1)S(1)} %copy-done.3), channel_id=1, source_target_pairs={{0,16},{1,17},{2,18},{3,19},{4,20},{5,21},{6,22},{7,23},{8,9},{9,8... | collective-permute-start | bytes 3538952 | tf_op jit(solution)/shard_map/ppermute | solution.py:31
  267.0 19.2 %collective-permute-start.31 = (bf16[24,6144]{1,0:T(8,128)(2,1)}, bf16[24,6144]{1,0:T(8,128)(2,1)S(1)}, u32[]{:S(2)}, u32[]{:S(2)}) collective-permute-start(bf16[24,6144]{1,0:T(8,128)(2,1)} %get-tuple-element.133), channel_id=1, source_target_pairs={{0,2},{1,3},{2,0},{3,1},{4,6},{5,7},{6,4},{7,5},{8,10},{9,11},{10,... | collective-permute-start | bytes 884744 | tf_op jit(solution)/shard_map/ppermute | solution.py:31
  273.6 23.8 %collective-permute-start.32 = (bf16[24,6144]{1,0:T(8,128)(2,1)}, bf16[24,6144]{1,0:T(8,128)(2,1)}, u32[]{:S(2)}, u32[]{:S(2)}) collective-permute-start(bf16[24,6144]{1,0:T(8,128)(2,1)} %get-tuple-element.135), channel_id=1, source_target_pairs={{0,4},{1,5},{2,6},{3,7},{4,0},{5,1},{6,2},{7,3},{8,12},{9,13},{10,... | collective-permute-start | bytes 884744 | tf_op jit(solution)/shard_map/ppermute | solution.py:31
  274.1 23.3 %collective-permute-start.33 = (bf16[24,6144]{1,0:T(8,128)(2,1)S(1)}, bf16[24,6144]{1,0:T(8,128)(2,1)}, u32[]{:S(2)}, u32[]{:S(2)}) collective-permute-start(bf16[24,6144]{1,0:T(8,128)(2,1)S(1)} %get-tuple-element.134), channel_id=1, source_target_pairs={{0,6},{1,7},{2,4},{3,5},{4,2},{5,3},{6,0},{7,1},{8,14},{9,15},{10,... | collective-permute-start | bytes 884744 | tf_op jit(solution)/shard_map/ppermute | solution.py:31
  278.3 33.0 %collective-permute-start.19 = (bf16[3,80,768]{2,1,0:T(8,128)(2,1)}, bf16[3,80,768]{2,1,0:T(8,128)(2,1)S(1)}, u32[]{:S(2)}, u32[]{:S(2)}) collective-permute-start(bf16[3,80,768]{2,1,0:T(8,128)(2,1)} %shard_map.302), channel_id=1, source_target_pairs={{0,24},{1,25},{2,26},{3,27},{4,28},{5,29},{6,30},{7,31},{8,16},{9,... | collective-permute-start | bytes 1105928 | tf_op jit(solution)/shard_map/ppermute | solution.py:31
  282.9 17.7 %collective-permute-start.26 = (bf16[1,4,24,3072]{3,2,1,0:T(8,128)(2,1)}, bf16[1,4,24,3072]{3,2,1,0:T(8,128)(2,1)S(1)}, u32[]{:S(2)}, u32[]{:S(2)}) collective-permute-start(bf16[1,4,24,3072]{3,2,1,0:T(8,128)(2,1)} %shard_map.309.refs_4_), channel_id=1, source_target_pairs={{0,1},{1,0},{2,3},{3,2},{4,5},{5,4},{6,7},{7,6},{8,24},{9,25},{10,... | collective-permute-start | bytes 1769480 | tf_op jit(solution)/shard_map/ppermute | solution.py:31
  298.6 13.2 %collective-permute-start.23 = (bf16[3,80,768]{2,1,0:T(8,128)(2,1)}, bf16[3,80,768]{2,1,0:T(8,128)(2,1)S(1)}, u32[]{:S(2)}, u32[]{:S(2)}) collective-permute-start(bf16[3,80,768]{2,1,0:T(8,128)(2,1)} %get-tuple-element.102), channel_id=1, source_target_pairs={{0,8},{1,9},{2,10},{3,11},{4,12},{5,13},{6,14},{7,15},{8,0},{9,1},... | collective-permute-start | bytes 1105928 | tf_op jit(solution)/shard_map/ppermute | solution.py:31
  298.7 25.8 %collective-permute-start.24 = (bf16[3,80,768]{2,1,0:T(8,128)(2,1)}, bf16[3,80,768]{2,1,0:T(8,128)(2,1)S(1)}, u32[]{:S(2)}, u32[]{:S(2)}) collective-permute-start(bf16[3,80,768]{2,1,0:T(8,128)(2,1)} %get-tuple-element.103), channel_id=1, source_target_pairs={{0,16},{1,17},{2,18},{3,19},{4,20},{5,21},{6,22},{7,23},{8,24},{9,... | collective-permute-start | bytes 1105928 | tf_op jit(solution)/shard_map/ppermute | solution.py:31
  300.5 24.0 %collective-permute-start.25 = (bf16[3,80,768]{2,1,0:T(8,128)(2,1)}, bf16[3,80,768]{2,1,0:T(8,128)(2,1)S(1)}, u32[]{:S(2)}, u32[]{:S(2)}) collective-permute-start(bf16[3,80,768]{2,1,0:T(8,128)(2,1)} %get-tuple-element.104), channel_id=1, source_target_pairs={{0,24},{1,25},{2,26},{3,27},{4,28},{5,29},{6,30},{7,31},{8,16},{9,... | collective-permute-start | bytes 1105928 | tf_op jit(solution)/shard_map/ppermute | solution.py:31
  305.7 23.8 %collective-permute-start.27 = (bf16[24,3072]{1,0:T(8,128)(2,1)S(1)}, bf16[24,3072]{1,0:T(8,128)(2,1)S(1)}, u32[]{:S(2)}, u32[]{:S(2)}) collective-permute-start(bf16[24,3072]{1,0:T(8,128)(2,1)S(1)} %get-tuple-element.138), channel_id=1, source_target_pairs={{0,2},{1,3},{2,0},{3,1},{4,6},{5,7},{6,4},{7,5},{8,10},{9,11},{10,... | collective-permute-start | bytes 442376 | tf_op jit(solution)/shard_map/ppermute | solution.py:31
  311.3 18.3 %collective-permute-start.28 = (bf16[24,3072]{1,0:T(8,128)(2,1)S(1)}, bf16[24,3072]{1,0:T(8,128)(2,1)S(1)}, u32[]{:S(2)}, u32[]{:S(2)}) collective-permute-start(bf16[24,3072]{1,0:T(8,128)(2,1)S(1)} %get-tuple-element.140), channel_id=1, source_target_pairs={{0,4},{1,5},{2,6},{3,7},{4,0},{5,1},{6,2},{7,3},{8,12},{9,13},{10,... | collective-permute-start | bytes 442376 | tf_op jit(solution)/shard_map/ppermute | solution.py:31
  311.9 17.7 %collective-permute-start.29 = (bf16[24,3072]{1,0:T(8,128)(2,1)S(1)}, bf16[24,3072]{1,0:T(8,128)(2,1)S(1)}, u32[]{:S(2)}, u32[]{:S(2)}) collective-permute-start(bf16[24,3072]{1,0:T(8,128)(2,1)S(1)} %get-tuple-element.139), channel_id=1, source_target_pairs={{0,6},{1,7},{2,4},{3,5},{4,2},{5,3},{6,0},{7,1},{8,14},{9,15},{10,... | collective-permute-start | bytes 442376 | tf_op jit(solution)/shard_map/ppermute | solution.py:31
  321.0 12.0 %all-to-all-start = ((bf16[32,24,128]{2,1,0:T(8,128)(2,1)}), bf16[32,24,128]{2,1,0:T(8,128)(2,1)S(1)}, u32[]{:S(2)}, u32[]{:S(2)}) async-start(bf16[32,24,128]{2,1,0:T(8,128)(2,1)} %bitcast.60), calls=%async_computation | async-start | bytes 393216 | tf_op jit(solution)/shard_map/all_to_all | solution.py:875
  (36 other events, 143.0 us)
Sparse Core Ops, SparseCore 0:
  10.9 112.5 all-gather.1

commit v2 on v1

--- a/solution.py
+++ b/solution.py
@@ -521,9 +521,11 @@
     go_ref[0] = dot(low, wo_ref[...], NT).astype(jnp.bfloat16)
 
 
-def attend_back_kernel(qkv_ref, go_ref, p_ref, g_ref, gqb_ref, gvb_ref):
+def attend_back_kernel(qkv_ref, go_ref, p_ref, o_ref, g_ref, gqb_ref, gvb_ref):
     model = go_ref.shape[-1]
     head = model // HEADS
+    turned_go = go_ref[0].T
+    turned_q = qkv_ref[0, :, :model].T
     for i in range(HEADS):
         at = slice(i * head, (i + 1) * head)
         k_at = slice(model + i * head, model + (i + 1) * head)
@@ -531,12 +533,11 @@
         go = go_ref[0, :, at]
         p = p_ref[0, i]
         dp = dot(go, qkv_ref[0, :, v_at], NT)
-        pf = p.astype(jnp.float32)
-        delta = jnp.sum(pf * dp, axis=-1, keepdims=True)
-        ds = (pf * (dp - delta)).astype(jnp.bfloat16)
+        delta = jnp.sum(go.astype(jnp.float32) * o_ref[0, :, at].astype(jnp.float32), axis=-1, keepdims=True)
+        ds = (p.astype(jnp.float32) * (dp - delta)).astype(jnp.bfloat16)
         g_ref[0, :, at] = (dot(ds, qkv_ref[0, :, k_at]) * head**-0.5).astype(jnp.bfloat16)
-        g_ref[0, :, k_at] = dot(ds, qkv_ref[0, :, at], TN).astype(jnp.bfloat16)
-        g_ref[0, :, v_at] = dot(p, go, TN).astype(jnp.bfloat16)
+        g_ref[0, :, k_at] = dot(turned_q[at], ds).T.astype(jnp.bfloat16)
+        g_ref[0, :, v_at] = dot(turned_go[at], p).T.astype(jnp.bfloat16)
     add_rows(gqb_ref, g_ref[0, :, :model].astype(jnp.float32))
     add_rows(gvb_ref, g_ref[0, :, 2 * model :].astype(jnp.float32))
 
@@ -842,38 +843,40 @@
     put_rest.second()
     g_mix, gqb, gvb = call(
         attend_back_kernel,
-        [(qkv, "slot"), (go, "slot"), (p, "slot")],
+        [(qkv, "slot"), (go, "slot"), (p, "slot"), (o, "slot")],
         [((slots, length, 3 * model), bf)] + [((1, model), f32)] * 2,
         slots,
         16 * scores,
         after=[put_rest.sent],
     )
-    put_rest.hold([g_mix])
+    out += [swap(sizes, piece, frame_peer(3 + index)) for index, piece in enumerate(hold(late, [g_mix]))]
+    sent, kept = row_grad(here, [(h1, g_mix), (o, ga)], [])
+    put_mixed = Scatter(sizes, here, sent, kept)
+    put_rest.hold([kept])
     put_rest.third()
-    out += [swap(sizes, piece, frame_peer(3 + index)) for index, piece in enumerate(hold(late, [g_mix]))]
-    sent, kept = row_grad(here, [(h1, g_mix), (o, ga)], [put_rest.sent])
-    put_mixed = Scatter(sizes, here, sent, kept)
     in_grad, gag, gab = call(
         input_kernel,
         [(g_mix, "slot"), (mixed, "whole"), (x, "frames"), (gx, "slot"), (vec, "whole")],
         [framed] + [((1, model), f32)] * 2,
         slots,
         6 * here_rows * model * model,
-        after=[kept],
+        after=[put_rest.sent],
     )
     put_mixed.hold([gag])
     put_mixed.second()
     put_rest.hold([put_mixed.sent])
     put_rest.fourth()
+    sums = [gag, gab, gqb, gvb, gob, gmg, gmb, gdb]
+    pack = turned(sums, gub.reshape(-1, ratio), [put_rest.sent])
+    pack = lax.all_to_all(pack.reshape(-1, rows, 128), AXES, 0, 0, tiled=True)
+    last = jnp.sum(pack.astype(f32), axis=0)
+    put_mixed.hold([put_rest.sent])
     put_mixed.third()
     in_grad = exchange(list(hold(in_grad, [put_mixed.sent])))
     out = list(hold(out, [put_mixed.sent]))
+    put_mixed.hold([pack])
     put_mixed.fourth()
     in_grad = list(hold(in_grad, [put_mixed.sent]))
-    sums = [gag, gab, gqb, gvb, gob, gmg, gmb, gdb]
-    pack = turned(sums, gub.reshape(-1, ratio), [put_mixed.sent])
-    pack = lax.all_to_all(pack.reshape(-1, rows, 128), AXES, 0, 0, tiled=True)
-    last = jnp.sum(pack.astype(f32), axis=0)
     rest_rows = put_rest.last()
     g_up = rest_rows[:, :hidden]
     g_down = rest_rows[:, hidden:].reshape(rows, ratio, model).transpose(1, 0, 2).reshape(ratio * rows, model)

time: 343 us -> 333 us (0.971)
  waiting for transfers between devices: 67.5 us -> 60 us
    ppermute x34, waiting for transfers between devices: 55 us -> 42.6 us  [swap(): return lax.ppermute(value, AXES, pairs)]
    all_to_all x1, waiting for transfers between devices: 1.19 us -> 6.09 us  [body(): pack = lax.all_to_all(pack.reshape(-1, rows, 128), AXES, 0, 0, tiled=True)]
    unnamed x64 -> x66, local copies, waits for them, and re-layouts: 11.8 us -> 11.9 us
  transfers between devices with their start and end apart: 36 -> 36, of which waited for: 12 -> 11; matrix products, arithmetic and copies ran while one was open for 6% -> 7% of each run, Pallas kernels for 31% -> 36%
where the time goes in v2:
time: 333 us; the launch traced here: 332 us
  Pallas kernels  175 us (53%)
  waiting for transfers between devices  60 us (18%)
  starting transfers between devices  46.7 us (14%)
  local copies, waits for them, and re-layouts  27.2 us (8%)
  between operations  14.5 us (4%)
  other arithmetic  8.52 us (3%)
    pallas_call x5, Pallas kernels, call(): pl.pallas_call(run, grid=(slots,), in_specs=specs + [ANY] * len(extra), o...  71.5 us
    pallas_call x1, Pallas kernels, mlp(): pl.pallas_call(body, grid_spec=pltpu.PrefetchScalarGridSpec(num_scalar_pr...  48 us
    ppermute x34, starting transfers between devices, swap(): return lax.ppermute(value, AXES, pairs)  42.8 us
    ppermute x34, waiting for transfers between devices, swap(): return lax.ppermute(value, AXES, pairs)  42.6 us
    pallas_call x6, Pallas kernels, add(): pl.pallas_call(body, grid_spec=pltpu.PrefetchScalarGridSpec(num_scalar_pr...  23.5 us
    unnamed x66, local copies, waits for them, and re-layouts  11.9 us
    all_gather x1, waiting for transfers between devices, body(): lax.all_gather(side_by_side(w_out, w_up, w_down), AXES, axis=0, tiled=True)  11.3 us
    pallas_call x1, Pallas kernels, row_grad(): pl.pallas_call(body, grid_spec=pltpu.PrefetchScalarGridSpec(num_scalar_pr...  11.2 us
  transfers between devices with their start and end apart: 36, of which 11 were waited for; matrix products, arithmetic and copies ran while one was open for 7% of the time, Pallas kernels for 36%

profile of v2, /device:TPU:0, one launch (start us, length us, event | category | flops | bytes accessed | tf_op | source)
XLA Modules:
  0.0 331.7 jit_solution(15738134135170533965)
XLA Ops:
  21.1 2.6 collective-permute-start.4
  23.7 2.8 collective-permute-done.3.refs_0_
  26.5 5.9 %collective-permute-start.5 = (bf16[24,2432]{1,0:T(8,128)(2,1)S(1)}, bf16[24,2432]{1,0:T(8,128)(2,1)S(1)}, u32[]{:S(2)}, u32[]{:S(2)}) collective-permute-start(bf16[24,2432]{1,0:T(8,128)(2,1)S(1)} %get-tuple-element.142), channel_id=1, source_target_pairs={{0,6},{1,7},{2,4},{3,5},{4,2},{5,3},{6,0},{7,1},{8,14},{9,15},{10,... | collective-permute-start | bytes 350216 | tf_op jit(solution)/shard_map/ppermute | solution.py:31
  32.4 5.4 %collective-permute-done.4.refs_1_ = bf16[24,2432]{1,0:T(8,128)(2,1)S(1)} collective-permute-done((bf16[24,2432]{1,0:T(8,128)(2,1)S(1)}, bf16[24,2432]{1,0:T(8,128)(2,1)S(1)}, u32[]{:S(2)}, u32[]{:S(2)}) %collective-permute-start.4) | collective-permute-done | bytes 116768 | tf_op jit(solution)/shard_map/ppermute | solution.py:31
  43.8 14.5 %collective-permute-done.6.refs_1_ = bf16[4,24,2432]{2,1,0:T(8,128)(2,1)S(1)} collective-permute-done((bf16[4,24,2432]{2,1,0:T(8,128)(2,1)S(1)}, bf16[4,24,2432]{2,1,0:T(8,128)(2,1)S(1)}, u32[]{:S(2)}, u32[]{:S(2)}) %collective-permute-start.6) | collective-permute-done | bytes 466976 | tf_op jit(solution)/shard_map/ppermute | solution.py:31
  61.9 7.7 %collective-permute-done.8.refs_3_ = bf16[4,24,2432]{2,1,0:T(8,128)(2,1)S(1)} collective-permute-done((bf16[4,24,2432]{2,1,0:T(8,128)(2,1)}, bf16[4,24,2432]{2,1,0:T(8,128)(2,1)S(1)}, u32[]{:S(2)}, u32[]{:S(2)}) %collective-permute-start.8) | collective-permute-done | bytes 466976 | tf_op jit(solution)/shard_map/ppermute | solution.py:31
  72.2 4.9 %shard_map.292 = (bf16[2,2,4,2,24,2432]{5,4,3,2,1,0:T(8,128)(2,1)}, f32[16,768]{1,0:T(8,128)}) custom-call(s32[4]{0:T(128)} %pad_add_fusion.here_ref, bf16[4,24,2432]{2,1,0:T(8,128)(2,1)} %copy-done.8, bf16[4,24,2432]{2,1,0:T(8,128)(2,1)} %copy-done.9, bf16[4,24,2432]{2,1,0:T(8,128)(2,1)} %shard_map.291.refs_2_, bf16[4,24,2432]{2,1,0:T(8,128)(2,1)} %copy-done.21, ...), custom_call_target="tpu_custom_call" | custom-call | tf_op jit(solution)/shard_map/pallas_call | solution.py:156
  77.1 2.6 shard_map.296
  82.4 2.9 collective-permute-start.14
  85.3 25.1 %shard_map.293 = (bf16[3,320,768]{2,1,0:T(8,128)(2,1)}, bf16[3,320,2304]{2,1,0:T(8,128)(2,1)}, bf16[3,320,768]{2,1,0:T(8,128)(2,1)}, bf16[3,12,320,320]{3,2,1,0:T(8,128)(2,1)}, s32[3,320,1]{2,1,0:T(8,128)}) custom-call(bf16[3,88,768]{2,1,0:T(8,128)(2,1)} %get-tuple-element.128.refs_0_.refs_2_, bf16[3,88,768]{2,1,0:T(8,128)(2,1)} %copy-done.3, ...), custom_call_target="tpu_custom_call" | custom-call | flops 7172259840 | bytes 20156160 | tf_op jit(solution)/shard_map/pallas_call | solution.py:606
  112.2 11.3 %all-gather.2.cloned.1.call-done.refs_5_.u_ref.refs_4_.refs_6_.refs_7_.refs_1_ = bf16[768,6912]{1,0:T(8,128)(2,1)} async-done(((bf16[24,6912]{1,0:T(8,128)(2,1)}), bf16[768,6912]{1,0:T(8,128)(2,1)}) %all-gather.2.cloned.1.call-update) | async-done | bytes 10616848 | tf_op jit(solution)/shard_map/all_gather | solution.py:803
  123.5 6.0 %shard_map.295 = (f32[3,320,768]{2,1,0:T(8,128)}, bf16[3,320,768]{2,1,0:T(8,128)(2,1)}) custom-call(bf16[3,88,768]{2,1,0:T(8,128)(2,1)} %get-tuple-element.128.refs_0_.refs_2_, bf16[3,88,768]{2,1,0:T(8,128)(2,1)} %copy-done.3, bf16[3,88,768]{2,1,0:T(8,128)(2,1)} %copy-done.4, bf16[3,88,768]{2,1,0:T(8,128)(2,1)} %copy-done.5, ...), custom_call_target="tpu_custom_call" | custom-call | flops 1132462080 | bytes 18186240 | tf_op jit(solution)/shard_map/pallas_call | solution.py:606
  130.5 48.0 %shard_map.297 = (bf16[3,80,768]{2,1,0:T(8,128)(2,1)}, bf16[3,80,768]{2,1,0:T(8,128)(2,1)}, bf16[3,80,768]{2,1,0:T(8,128)(2,1)}, bf16[3,80,768]{2,1,0:T(8,128)(2...) custom-call(s32[4]{0:T(128)} %pad_add_fusion.here_ref, ...), custom_call_target="tpu_custom_call" | custom-call | flops 27179089920 | bytes 22118400 | tf_op jit(solution)/shard_map/pallas_call | solution.py:452
  179.1 7.9 %shard_map.298 = (f32[3,320,768]{2,1,0:T(8,128)}, bf16[3,320,768]{2,1,0:T(8,128)(2,1)}, bf16[3,320,768]{2,1,0:T(8,128)(2,1)}, f32[1,768]{1,0:T(1,128)}, f32[1,768]{1,0:T(1,128)}, /*index=5*/f32[1,768]{1,0:T(1,128)}) custom-call(f32[3,320,768]{2,1,0:T(8,128)} %get-tuple-element.80.refs_0_, ...), custom_call_target="tpu_custom_call" | custom-call | flops 1132462080 | bytes 23946240 | tf_op jit(solution)/shard_map/pallas_call | solution.py:606
  186.9 2.9 collective-permute-done.17.refs_3_.refs_2_
  190.6 5.2 %shard_map.300.refs_4_ = bf16[2,4,24,6144]{3,2,1,0:T(8,128)(2,1)} custom-call(s32[4]{0:T(128)} %pad_add_fusion.here_ref, bf16[2,4,2,24,6144]{4,3,2,1,0:T(8,128)(2,1)} %shard_map.299.refs_0_, bf16[2,4,2,24,6144]{4,3,2,1,0:T(8,128)(2,1)} %collective-permute-done.18.refs_1_), custom_call_target="tpu_custom_call" | custom-call | bytes 7077888 | tf_op jit(solution)/shard_map/pallas_call | solution.py:203
  196.0 23.1 %shard_map.301 = (bf16[3,320,2304]{2,1,0:T(8,128)(2,1)}, f32[1,768]{1,0:T(1,128)}, f32[1,768]{1,0:T(1,128)}) custom-call(bf16[3,320,2304]{2,1,0:T(8,128)(2,1)} %get-tuple-element.79.refs_0_, bf16[3,320,768]{2,1,0:T(8,128)(2,1)} %get-tuple-element.82.refs_1_, bf16[3,12,320,320]{3,2,1,0:T(8,128)(2,1)} %get-tuple-element.83.refs_2_, ...), custom_call_target="tpu_custom_call" | custom-call | flops 7549747200 | bytes 19175424 | tf_op jit(solution)/shard_map/pallas_call | solution.py:606
  219.1 11.2 %shard_map.303 = (bf16[2,192,3072]{2,1,0:T(8,128)(2,1)}, bf16[2,192,3072]{2,1,0:T(8,128)(2,1)}) custom-call(s32[4]{0:T(128)} %pad_add_fusion.here_ref, bf16[3,320,768]{2,1,0:T(8,128)(2,1)} %get-tuple-element.87.refs_0_, bf16[3,320,2304]{2,1,0:T(8,128)(2,1)} %get-tuple-element.86.refs_1_.refs_0_, ...), custom_call_target="tpu_custom_call" | custom-call | flops 4529848320 | bytes 5898240 | tf_op jit(solution)/shard_map/pallas_call | solution.py:662
  231.8 3.7 %shard_map.305.refs_8_ = bf16[1,4,24,6144]{3,2,1,0:T(8,128)(2,1)} custom-call(s32[4]{0:T(128)} %pad_add_fusion.here_ref, bf16[2,4,2,24,6144]{4,3,2,1,0:T(8,128)(2,1)} %shard_map.304.refs_0_, bf16[2,4,2,24,6144]{4,3,2,1,0:T(8,128)(2,1)} %collective-permute-done.18.refs_1_, bf16[2,4,24,6144]{3,2,1,0:T(8,128)(2,1)} %collective-permute-done.20.refs_2_), custom_call_target="tpu_custom_call" | custom-call | bytes 4718592 | tf_op jit(solution)/shard_map/pallas_call | solution.py:203
  236.9 9.4 %shard_map.306 = (bf16[3,80,768]{2,1,0:T(8,128)(2,1)}, bf16[3,80,768]{2,1,0:T(8,128)(2,1)}, bf16[3,80,768]{2,1,0:T(8,128)(2,1)}, bf16[3,80,768]{2,1,0:T(8,128)(2...) custom-call(bf16[3,320,2304]{2,1,0:T(8,128)(2,1)} %get-tuple-element.86.refs_1_.refs_0_, bf16[768,2432]{1,0:T(8,128)(2,1)} %bitcast.59, ...), custom_call_target="tpu_custom_call" | custom-call | flops 3397386240 | bytes 14260224 | tf_op jit(solution)/shard_map/pallas_call | solution.py:606
  247.7 4.4 %shard_map.308.refs_1_ = bf16[2,4,24,3072]{3,2,1,0:T(8,128)(2,1)} custom-call(s32[4]{0:T(128)} %pad_add_fusion.here_ref, bf16[2,4,2,24,3072]{4,3,2,1,0:T(8,128)(2,1)} %shard_map.307.refs_0_, bf16[2,4,2,24,3072]{4,3,2,1,0:T(8,128)(2,1)} %copy-done), custom_call_target="tpu_custom_call" | custom-call | bytes 3538944 | tf_op jit(solution)/shard_map/pallas_call | solution.py:203
  255.2 4.2 %shard_map.310 = bf16[1,4,24,6144]{3,2,1,0:T(8,128)(2,1)} custom-call(s32[4]{0:T(128)} %pad_add_fusion.here_ref, bf16[2,4,2,24,6144]{4,3,2,1,0:T(8,128)(2,1)} %shard_map.309.refs_0_, bf16[2,4,2,24,6144]{4,3,2,1,0:T(8,128)(2,1)} %collective-permute-done.18.refs_1_, bf16[2,4,24,6144]{3,2,1,0:T(8,128)(2,1)} %collective-permute-done.20.refs_2_, ...), custom_call_target="tpu_custom_call" | custom-call | bytes 5898240 | tf_op jit(solution)/shard_map/pallas_call | solution.py:203
  261.4 6.5 %collective-permute-start.31 = (bf16[24,6144]{1,0:T(8,128)(2,1)}, bf16[24,6144]{1,0:T(8,128)(2,1)}, u32[]{:S(2)}, u32[]{:S(2)}) collective-permute-start(bf16[24,6144]{1,0:T(8,128)(2,1)} %get-tuple-element.133), channel_id=1, source_target_pairs={{0,2},{1,3},{2,0},{3,1},{4,6},{5,7},{6,4},{7,5},{8,10},{9,11},{10,... | collective-permute-start | bytes 884744 | tf_op jit(solution)/shard_map/ppermute | solution.py:31
  274.6 3.9 %all-to-all-start = ((bf16[32,24,128]{2,1,0:T(8,128)(2,1)}), bf16[32,24,128]{2,1,0:T(8,128)(2,1)S(1)}, u32[]{:S(2)}, u32[]{:S(2)}) async-start(bf16[32,24,128]{2,1,0:T(8,128)(2,1)} %bitcast.62), calls=%async_computation | async-start | bytes 393216 | tf_op jit(solution)/shard_map/all_to_all | solution.py:871
  279.5 2.9 shard_map.312.refs_4_
  284.7 3.8 %shard_map.314 = bf16[12,80,768]{2,1,0:T(8,128)(2,1)} custom-call(s32[4]{0:T(128)} %pad_add_fusion.here_ref, bf16[3,80,768]{2,1,0:T(8,128)(2,1)} %get-tuple-element.93.refs_0_, bf16[3,80,768]{2,1,0:T(8,128)(2,1)} %get-tuple-element.94.refs_1_, bf16[3,80,768]{2,1,0:T(8,128)(2,1)} %get-tuple-element.95.refs_2_, bf16[3,80,768]{2,1,0:T(8,128)(2,1)} %get-tuple-element.96.refs_3_), custom_call_target="tpu_custom_call" | custom-call | tf_op jit(solution)/shard_map/pallas_call | solution.py:713
  290.1 3.7 %collective-permute-done.32 = bf16[24,6144]{1,0:T(8,128)(2,1)} collective-permute-done((bf16[24,6144]{1,0:T(8,128)(2,1)}, bf16[24,6144]{1,0:T(8,128)(2,1)}, u32[]{:S(2)}, u32[]{:S(2)}) %collective-permute-start.32) | collective-permute-done | bytes 294944 | tf_op jit(solution)/shard_map/ppermute | solution.py:31
  296.8 6.1 %all-to-all-done.refs_1_ = bf16[32,24,128]{2,1,0:T(8,128)(2,1)S(1)} async-done(((bf16[32,24,128]{2,1,0:T(8,128)(2,1)}), bf16[32,24,128]{2,1,0:T(8,128)(2,1)S(1)}, u32[]{:S(2)}, u32[]{:S(2)}) %all-to-all-start) | async-done | bytes 196640 | tf_op jit(solution)/shard_map/all_to_all | solution.py:871
  304.4 3.1 shard_map.318
  310.5 2.6 collective-permute-start.30
  315.5 4.1 %shard_map.320 = f32[12,80,768]{2,1,0:T(8,128)} custom-call(s32[4]{0:T(128)} %pad_add_fusion.here_ref, bf16[3,80,768]{2,1,0:T(8,128)(2,1)} %get-tuple-element.113.refs_0_, bf16[3,80,768]{2,1,0:T(8,128)(2,1)} %get-tuple-element.114.refs_1_, bf16[3,80,768]{2,1,0:T(8,128)(2,1)} %get-tuple-element.115.refs_2_, bf16[3,80,768]{2,1,0:T(8,128)(2,1)} %get-tuple-element.116.refs_3_), custom_call_target="tpu_custom_call" | custom-call | tf_op jit(solution)/shard_map/pallas_call | solution.py:713
  319.6 2.9 collective-permute-done.29
  (172 shorter events, 66.2 us)
Async XLA Ops:
  7.2 116.3 %all-gather.2.cloned.1.call-start = ((), (), s32[]{:S(2)}) async-start(), calls=%async_computation.1 | async-start | bytes 10948608 | tf_op jit(solution)/shard_map/all_gather | solution.py:803
  13.3 24.6 %collective-permute-start = (bf16[3,88,768]{2,1,0:T(8,128)(2,1)S(1)}, bf16[3,88,768]{2,1,0:T(8,128)(2,1)S(1)}, u32[]{:S(2)}, u32[]{:S(2)}) collective-permute-start(bf16[3,88,768]{2,1,0:T(8,128)(2,1)S(1)} %get-tuple-element.127), channel_id=1, source_target_pairs={{0,8},{1,9},{2,10},{3,11},{4,12},{5,13},{6,14},{7,15},{8,0},{9,1},... | collective-permute-start | bytes 1216520 | tf_op jit(solution)/shard_map/ppermute | solution.py:31
  13.7 24.2 %collective-permute-start.1 = (bf16[3,88,768]{2,1,0:T(8,128)(2,1)S(1)}, bf16[3,88,768]{2,1,0:T(8,128)(2,1)S(1)}, u32[]{:S(2)}, u32[]{:S(2)}) collective-permute-start(bf16[3,88,768]{2,1,0:T(8,128)(2,1)S(1)} %get-tuple-element.126), channel_id=1, source_target_pairs={{0,16},{1,17},{2,18},{3,19},{4,20},{5,21},{6,22},{7,23},{8,24},{9,... | collective-permute-start | bytes 1216520 | tf_op jit(solution)/shard_map/ppermute | solution.py:31
  16.2 21.7 %collective-permute-start.2 = (bf16[3,88,768]{2,1,0:T(8,128)(2,1)S(1)}, bf16[3,88,768]{2,1,0:T(8,128)(2,1)S(1)}, u32[]{:S(2)}, u32[]{:S(2)}) collective-permute-start(bf16[3,88,768]{2,1,0:T(8,128)(2,1)S(1)} %get-tuple-element.125), channel_id=1, source_target_pairs={{0,24},{1,25},{2,26},{3,27},{4,28},{5,29},{6,30},{7,31},{8,16},{9,... | collective-permute-start | bytes 1216520 | tf_op jit(solution)/shard_map/ppermute | solution.py:31
  21.1 16.7 %collective-permute-start.4 = (bf16[24,2432]{1,0:T(8,128)(2,1)S(1)}, bf16[24,2432]{1,0:T(8,128)(2,1)S(1)}, u32[]{:S(2)}, u32[]{:S(2)}) collective-permute-start(bf16[24,2432]{1,0:T(8,128)(2,1)S(1)} %get-tuple-element.142), channel_id=1, source_target_pairs={{0,4},{1,5},{2,6},{3,7},{4,0},{5,1},{6,2},{7,3},{8,12},{9,13},{10,... | collective-permute-start | bytes 350216 | tf_op jit(solution)/shard_map/ppermute | solution.py:31
  26.5 11.3 %collective-permute-start.5 = (bf16[24,2432]{1,0:T(8,128)(2,1)S(1)}, bf16[24,2432]{1,0:T(8,128)(2,1)S(1)}, u32[]{:S(2)}, u32[]{:S(2)}) collective-permute-start(bf16[24,2432]{1,0:T(8,128)(2,1)S(1)} %get-tuple-element.142), channel_id=1, source_target_pairs={{0,6},{1,7},{2,4},{3,5},{4,2},{5,3},{6,0},{7,1},{8,14},{9,15},{10,... | collective-permute-start | bytes 350216 | tf_op jit(solution)/shard_map/ppermute | solution.py:31
  40.7 17.6 %collective-permute-start.6 = (bf16[4,24,2432]{2,1,0:T(8,128)(2,1)S(1)}, bf16[4,24,2432]{2,1,0:T(8,128)(2,1)S(1)}, u32[]{:S(2)}, u32[]{:S(2)}) collective-permute-start(bf16[4,24,2432]{2,1,0:T(8,128)(2,1)S(1)} %pad_maximum_fusion.refs_0_), channel_id=1, source_target_pairs={{0,1},{1,0},{2,3},{3,2},{4,5},{5,4},{6,7},{7,6},{8,24},{9,25},{10,... | collective-permute-start | bytes 1400840 | tf_op jit(solution)/shard_map/ppermute | solution.py:31
  42.3 17.7 %collective-permute-start.7 = (bf16[4,24,2432]{2,1,0:T(8,128)(2,1)S(1)}, bf16[4,24,2432]{2,1,0:T(8,128)(2,1)S(1)}, u32[]{:S(2)}, u32[]{:S(2)}) collective-permute-start(bf16[4,24,2432]{2,1,0:T(8,128)(2,1)S(1)} %pad_maximum_fusion.refs_0_), channel_id=1, source_target_pairs={{0,16},{1,17},{2,18},{3,19},{4,20},{5,21},{6,22},{7,23},{8,9},{9,8... | collective-permute-start | bytes 1400840 | tf_op jit(solution)/shard_map/ppermute | solution.py:31
  60.8 8.8 %collective-permute-start.8 = (bf16[4,24,2432]{2,1,0:T(8,128)(2,1)}, bf16[4,24,2432]{2,1,0:T(8,128)(2,1)S(1)}, u32[]{:S(2)}, u32[]{:S(2)}) collective-permute-start(bf16[4,24,2432]{2,1,0:T(8,128)(2,1)} %shard_map.291.refs_2_), channel_id=1, source_target_pairs={{0,1},{1,0},{2,3},{3,2},{4,5},{5,4},{6,7},{7,6},{8,24},{9,25},{10,... | collective-permute-start | bytes 1400840 | tf_op jit(solution)/shard_map/ppermute | solution.py:31
  61.4 8.9 %collective-permute-start.9 = (bf16[4,24,2432]{2,1,0:T(8,128)(2,1)S(1)}, bf16[4,24,2432]{2,1,0:T(8,128)(2,1)S(1)}, u32[]{:S(2)}, u32[]{:S(2)}) collective-permute-start(bf16[4,24,2432]{2,1,0:T(8,128)(2,1)S(1)} %pad_maximum_fusion.refs_0_), channel_id=1, source_target_pairs={{0,8},{1,9},{2,10},{3,11},{4,12},{5,13},{6,14},{7,15},{8,0},{9,1},... | collective-permute-start | bytes 1400840 | tf_op jit(solution)/shard_map/ppermute | solution.py:31
  61.4 8.9 %collective-permute-start.11 = (bf16[4,24,2432]{2,1,0:T(8,128)(2,1)}, bf16[4,24,2432]{2,1,0:T(8,128)(2,1)S(1)}, u32[]{:S(2)}, u32[]{:S(2)}) collective-permute-start(bf16[4,24,2432]{2,1,0:T(8,128)(2,1)} %shard_map.291.refs_2_), channel_id=1, source_target_pairs={{0,8},{1,9},{2,10},{3,11},{4,12},{5,13},{6,14},{7,15},{8,0},{9,1},... | collective-permute-start | bytes 1400840 | tf_op jit(solution)/shard_map/ppermute | solution.py:31
  82.1 47.4 %collective-permute-start.13 = (bf16[3,80,768]{2,1,0:T(8,128)(2,1)S(1)}, bf16[3,80,768]{2,1,0:T(8,128)(2,1)S(1)}, u32[]{:S(2)}, u32[]{:S(2)}) collective-permute-start(bf16[3,80,768]{2,1,0:T(8,128)(2,1)S(1)} %get-tuple-element.131), channel_id=1, source_target_pairs={{0,8},{1,9},{2,10},{3,11},{4,12},{5,13},{6,14},{7,15},{8,0},{9,1},... | collective-permute-start | bytes 1105928 | tf_op jit(solution)/shard_map/ppermute | solution.py:31
  82.4 47.1 %collective-permute-start.14 = (bf16[3,80,768]{2,1,0:T(8,128)(2,1)S(1)}, bf16[3,80,768]{2,1,0:T(8,128)(2,1)S(1)}, u32[]{:S(2)}, u32[]{:S(2)}) collective-permute-start(bf16[3,80,768]{2,1,0:T(8,128)(2,1)S(1)} %get-tuple-element.130), channel_id=1, source_target_pairs={{0,16},{1,17},{2,18},{3,19},{4,20},{5,21},{6,22},{7,23},{8,24},{9,... | collective-permute-start | bytes 1105928 | tf_op jit(solution)/shard_map/ppermute | solution.py:31
  85.2 44.3 %collective-permute-start.15 = (bf16[3,80,768]{2,1,0:T(8,128)(2,1)S(1)}, bf16[3,80,768]{2,1,0:T(8,128)(2,1)S(1)}, u32[]{:S(2)}, u32[]{:S(2)}) collective-permute-start(bf16[3,80,768]{2,1,0:T(8,128)(2,1)S(1)} %get-tuple-element.129), channel_id=1, source_target_pairs={{0,24},{1,25},{2,26},{3,27},{4,28},{5,29},{6,30},{7,31},{8,16},{9,... | collective-permute-start | bytes 1105928 | tf_op jit(solution)/shard_map/ppermute | solution.py:31
  178.5 12.1 %collective-permute-start.18 = (bf16[2,4,2,24,6144]{4,3,2,1,0:T(8,128)(2,1)}, bf16[2,4,2,24,6144]{4,3,2,1,0:T(8,128)(2,1)}, u32[]{:S(2)}, u32[]{:S(2)}) collective-permute-start(bf16[2,4,2,24,6144]{4,3,2,1,0:T(8,128)(2,1)} %bitcast.75), channel_id=1, source_target_pairs={{0,8},{1,9},{2,10},{3,11},{4,12},{5,13},{6,14},{7,15},{8,0},{9,1},... | collective-permute-start | bytes 14155784 | tf_op jit(solution)/shard_map/ppermute | solution.py:31
  179.1 10.8 %collective-permute-start.17 = (bf16[3,80,768]{2,1,0:T(8,128)(2,1)}, bf16[3,80,768]{2,1,0:T(8,128)(2,1)S(1)}, u32[]{:S(2)}, u32[]{:S(2)}) collective-permute-start(bf16[3,80,768]{2,1,0:T(8,128)(2,1)} %get-tuple-element.77), channel_id=1, source_target_pairs={{0,16},{1,17},{2,18},{3,19},{4,20},{5,21},{6,22},{7,23},{8,24},{9,... | collective-permute-start | bytes 1105928 | tf_op jit(solution)/shard_map/ppermute | solution.py:31
  195.8 36.1 %collective-permute-start.20 = (bf16[2,4,24,6144]{3,2,1,0:T(8,128)(2,1)}, bf16[2,4,24,6144]{3,2,1,0:T(8,128)(2,1)}, u32[]{:S(2)}, u32[]{:S(2)}) collective-permute-start(bf16[2,4,24,6144]{3,2,1,0:T(8,128)(2,1)} %shard_map.300.refs_4_), channel_id=1, source_target_pairs={{0,16},{1,17},{2,18},{3,19},{4,20},{5,21},{6,22},{7,23},{8,9},{9,8... | collective-permute-start | bytes 7077896 | tf_op jit(solution)/shard_map/ppermute | solution.py:31
  230.3 16.0 %collective-permute-start.21 = (bf16[2,4,2,24,3072]{4,3,2,1,0:T(8,128)(2,1)}, bf16[2,4,2,24,3072]{4,3,2,1,0:T(8,128)(2,1)S(1)}, u32[]{:S(2)}, u32[]{:S(2)}) collective-permute-start(bf16[2,4,2,24,3072]{4,3,2,1,0:T(8,128)(2,1)} %bitcast.76), channel_id=1, source_target_pairs={{0,8},{1,9},{2,10},{3,11},{4,12},{5,13},{6,14},{7,15},{8,0},{9,1},... | collective-permute-start | bytes 7077896 | tf_op jit(solution)/shard_map/ppermute | solution.py:31
  235.5 19.6 %collective-permute-start.22 = (bf16[1,4,24,6144]{3,2,1,0:T(8,128)(2,1)}, bf16[1,4,24,6144]{3,2,1,0:T(8,128)(2,1)}, u32[]{:S(2)}, u32[]{:S(2)}) collective-permute-start(bf16[1,4,24,6144]{3,2,1,0:T(8,128)(2,1)} %shard_map.305.refs_8_), channel_id=1, source_target_pairs={{0,1},{1,0},{2,3},{3,2},{4,5},{5,4},{6,7},{7,6},{8,24},{9,25},{10,... | collective-permute-start | bytes 3538952 | tf_op jit(solution)/shard_map/ppermute | solution.py:31
  236.9 47.1 %collective-permute-start.19 = (bf16[3,80,768]{2,1,0:T(8,128)(2,1)}, bf16[3,80,768]{2,1,0:T(8,128)(2,1)S(1)}, u32[]{:S(2)}, u32[]{:S(2)}) collective-permute-start(bf16[3,80,768]{2,1,0:T(8,128)(2,1)} %shard_map.302), channel_id=1, source_target_pairs={{0,24},{1,25},{2,26},{3,27},{4,28},{5,29},{6,30},{7,31},{8,16},{9,... | collective-permute-start | bytes 1105928 | tf_op jit(solution)/shard_map/ppermute | solution.py:31
  253.4 25.0 %collective-permute-start.23 = (bf16[2,4,24,3072]{3,2,1,0:T(8,128)(2,1)S(1)}, bf16[2,4,24,3072]{3,2,1,0:T(8,128)(2,1)S(1)}, u32[]{:S(2)}, u32[]{:S(2)}) collective-permute-start(bf16[2,4,24,3072]{3,2,1,0:T(8,128)(2,1)S(1)} %copy-done.2), channel_id=1, source_target_pairs={{0,16},{1,17},{2,18},{3,19},{4,20},{5,21},{6,22},{7,23},{8,9},{9,8... | collective-permute-start | bytes 3538952 | tf_op jit(solution)/shard_map/ppermute | solution.py:31
  261.4 27.2 %collective-permute-start.31 = (bf16[24,6144]{1,0:T(8,128)(2,1)}, bf16[24,6144]{1,0:T(8,128)(2,1)}, u32[]{:S(2)}, u32[]{:S(2)}) collective-permute-start(bf16[24,6144]{1,0:T(8,128)(2,1)} %get-tuple-element.133), channel_id=1, source_target_pairs={{0,2},{1,3},{2,0},{3,1},{4,6},{5,7},{6,4},{7,5},{8,10},{9,11},{10,... | collective-permute-start | bytes 884744 | tf_op jit(solution)/shard_map/ppermute | solution.py:31
  267.9 25.8 %collective-permute-start.32 = (bf16[24,6144]{1,0:T(8,128)(2,1)}, bf16[24,6144]{1,0:T(8,128)(2,1)}, u32[]{:S(2)}, u32[]{:S(2)}) collective-permute-start(bf16[24,6144]{1,0:T(8,128)(2,1)} %get-tuple-element.135), channel_id=1, source_target_pairs={{0,4},{1,5},{2,6},{3,7},{4,0},{5,1},{6,2},{7,3},{8,12},{9,13},{10,... | collective-permute-start | bytes 884744 | tf_op jit(solution)/shard_map/ppermute | solution.py:31
  268.4 25.3 %collective-permute-start.33 = (bf16[24,6144]{1,0:T(8,128)(2,1)}, bf16[24,6144]{1,0:T(8,128)(2,1)}, u32[]{:S(2)}, u32[]{:S(2)}) collective-permute-start(bf16[24,6144]{1,0:T(8,128)(2,1)} %get-tuple-element.134), channel_id=1, source_target_pairs={{0,6},{1,7},{2,4},{3,5},{4,2},{5,3},{6,0},{7,1},{8,14},{9,15},{10,... | collective-permute-start | bytes 884744 | tf_op jit(solution)/shard_map/ppermute | solution.py:31
  274.6 28.3 %all-to-all-start = ((bf16[32,24,128]{2,1,0:T(8,128)(2,1)}), bf16[32,24,128]{2,1,0:T(8,128)(2,1)S(1)}, u32[]{:S(2)}, u32[]{:S(2)}) async-start(bf16[32,24,128]{2,1,0:T(8,128)(2,1)} %bitcast.62), calls=%async_computation | async-start | bytes 393216 | tf_op jit(solution)/shard_map/all_to_all | solution.py:871
  282.4 21.1 %collective-permute-start.27 = (bf16[1,4,24,3072]{3,2,1,0:T(8,128)(2,1)}, bf16[1,4,24,3072]{3,2,1,0:T(8,128)(2,1)S(1)}, u32[]{:S(2)}, u32[]{:S(2)}) collective-permute-start(bf16[1,4,24,3072]{3,2,1,0:T(8,128)(2,1)} %shard_map.312.refs_4_), channel_id=1, source_target_pairs={{0,1},{1,0},{2,3},{3,2},{4,5},{5,4},{6,7},{7,6},{8,24},{9,25},{10,... | collective-permute-start | bytes 1769480 | tf_op jit(solution)/shard_map/ppermute | solution.py:31
  284.0 26.5 %collective-permute-start.24 = (bf16[3,80,768]{2,1,0:T(8,128)(2,1)}, bf16[3,80,768]{2,1,0:T(8,128)(2,1)S(1)}, u32[]{:S(2)}, u32[]{:S(2)}) collective-permute-start(bf16[3,80,768]{2,1,0:T(8,128)(2,1)} %get-tuple-element.102), channel_id=1, source_target_pairs={{0,8},{1,9},{2,10},{3,11},{4,12},{5,13},{6,14},{7,15},{8,0},{9,1},... | collective-permute-start | bytes 1105928 | tf_op jit(solution)/shard_map/ppermute | solution.py:31
  288.6 26.1 %collective-permute-start.25 = (bf16[3,80,768]{2,1,0:T(8,128)(2,1)S(1)}, bf16[3,80,768]{2,1,0:T(8,128)(2,1)S(1)}, u32[]{:S(2)}, u32[]{:S(2)}) collective-permute-start(bf16[3,80,768]{2,1,0:T(8,128)(2,1)S(1)} %copy-done.26), channel_id=1, source_target_pairs={{0,16},{1,17},{2,18},{3,19},{4,20},{5,21},{6,22},{7,23},{8,24},{9,... | collective-permute-start | bytes 1105928 | tf_op jit(solution)/shard_map/ppermute | solution.py:31
  293.7 20.9 %collective-permute-start.26 = (bf16[3,80,768]{2,1,0:T(8,128)(2,1)}, bf16[3,80,768]{2,1,0:T(8,128)(2,1)S(1)}, u32[]{:S(2)}, u32[]{:S(2)}) collective-permute-start(bf16[3,80,768]{2,1,0:T(8,128)(2,1)} %get-tuple-element.104), channel_id=1, source_target_pairs={{0,24},{1,25},{2,26},{3,27},{4,28},{5,29},{6,30},{7,31},{8,16},{9,... | collective-permute-start | bytes 1105928 | tf_op jit(solution)/shard_map/ppermute | solution.py:31
  308.6 11.0 %collective-permute-start.28 = (bf16[24,3072]{1,0:T(8,128)(2,1)S(1)}, bf16[24,3072]{1,0:T(8,128)(2,1)S(1)}, u32[]{:S(2)}, u32[]{:S(2)}) collective-permute-start(bf16[24,3072]{1,0:T(8,128)(2,1)S(1)} %get-tuple-element.138), channel_id=1, source_target_pairs={{0,2},{1,3},{2,0},{3,1},{4,6},{5,7},{6,4},{7,5},{8,10},{9,11},{10,... | collective-permute-start | bytes 442376 | tf_op jit(solution)/shard_map/ppermute | solution.py:31
  309.5 13.0 %collective-permute-start.29 = (bf16[24,3072]{1,0:T(8,128)(2,1)S(1)}, bf16[24,3072]{1,0:T(8,128)(2,1)S(1)}, u32[]{:S(2)}, u32[]{:S(2)}) collective-permute-start(bf16[24,3072]{1,0:T(8,128)(2,1)S(1)} %get-tuple-element.140), channel_id=1, source_target_pairs={{0,4},{1,5},{2,6},{3,7},{4,0},{5,1},{6,2},{7,3},{8,12},{9,13},{10,... | collective-permute-start | bytes 442376 | tf_op jit(solution)/shard_map/ppermute | solution.py:31
  310.5 12.0 %collective-permute-start.30 = (bf16[24,3072]{1,0:T(8,128)(2,1)S(1)}, bf16[24,3072]{1,0:T(8,128)(2,1)S(1)}, u32[]{:S(2)}, u32[]{:S(2)}) collective-permute-start(bf16[24,3072]{1,0:T(8,128)(2,1)S(1)} %get-tuple-element.139), channel_id=1, source_target_pairs={{0,6},{1,7},{2,4},{3,5},{4,2},{5,3},{6,0},{7,1},{8,14},{9,15},{10,... | collective-permute-start | bytes 442376 | tf_op jit(solution)/shard_map/ppermute | solution.py:31
  (37 other events, 139.3 us)
Sparse Core Ops, SparseCore 0:
  10.9 112.5 all-gather.1

commit v3 on v2

--- a/solution.py
+++ b/solution.py
@@ -874,7 +874,6 @@
     put_mixed.third()
     in_grad = exchange(list(hold(in_grad, [put_mixed.sent])))
     out = list(hold(out, [put_mixed.sent]))
-    put_mixed.hold([pack])
     put_mixed.fourth()
     in_grad = list(hold(in_grad, [put_mixed.sent]))
     rest_rows = put_rest.last()

time: 333 us -> 332 us (level)
  waiting for transfers between devices: 60 us -> 50.8 us
  starting transfers between devices: 46.7 us -> 55.4 us
    all_to_all x1, waiting for transfers between devices: 6.09 us -> 0.01 us  [body(): pack = lax.all_to_all(pack.reshape(-1, rows, 128), AXES, 0, 0, tiled=True)]
    ppermute x34, starting transfers between devices: 42.8 us -> 47.9 us  [swap(): return lax.ppermute(value, AXES, pairs)]
    all_to_all x1, starting transfers between devices: 3.88 us -> 7.49 us  [body(): pack = lax.all_to_all(pack.reshape(-1, rows, 128), AXES, 0, 0, tiled=True)]
    unnamed x66 -> x62, local copies, waits for them, and re-layouts: 11.9 us -> 10.9 us
  transfers between devices with their start and end apart: 36 -> 36, of which waited for: 11 -> 9; matrix products, arithmetic and copies ran while one was open for 7% -> 7% of each run, Pallas kernels for 36% -> 36%
where the time goes in v3:
time: 332 us; the launch traced here: 330 us
  Pallas kernels  175 us (53%)
  starting transfers between devices  55.4 us (17%)
  waiting for transfers between devices  50.8 us (15%)
  local copies, waits for them, and re-layouts  26.2 us (8%)
  between operations  14.5 us (4%)
  other arithmetic  8.5 us (3%)
    pallas_call x5, Pallas kernels, call(): pl.pallas_call(run, grid=(slots,), in_specs=specs + [ANY] * len(extra), o...  71.5 us
    pallas_call x1, Pallas kernels, mlp(): pl.pallas_call(body, grid_spec=pltpu.PrefetchScalarGridSpec(num_scalar_pr...  48.1 us
    ppermute x34, starting transfers between devices, swap(): return lax.ppermute(value, AXES, pairs)  47.9 us
    ppermute x34, waiting for transfers between devices, swap(): return lax.ppermute(value, AXES, pairs)  39.5 us
    pallas_call x6, Pallas kernels, add(): pl.pallas_call(body, grid_spec=pltpu.PrefetchScalarGridSpec(num_scalar_pr...  23.5 us
    all_gather x1, waiting for transfers between devices, body(): lax.all_gather(side_by_side(w_out, w_up, w_down), AXES, axis=0, tiled=True)  11.3 us
    pallas_call x1, Pallas kernels, row_grad(): pl.pallas_call(body, grid_spec=pltpu.PrefetchScalarGridSpec(num_scalar_pr...  10.9 us
    unnamed x62, local copies, waits for them, and re-layouts  10.9 us
  transfers between devices with their start and end apart: 36, of which 9 were waited for; matrix products, arithmetic and copies ran while one was open for 7% of the time, Pallas kernels for 36%

profile of v3, /device:TPU:0, one launch (start us, length us, event | category | flops | bytes accessed | tf_op | source)
XLA Modules:
  0.0 330.1 jit_solution(11086312200780441165)
XLA Ops:
  13.7 2.6 collective-permute-start.1
  21.1 2.6 collective-permute-start.4
  23.7 2.8 collective-permute-done.3.refs_0_
  26.5 5.9 %collective-permute-start.5 = (bf16[24,2432]{1,0:T(8,128)(2,1)S(1)}, bf16[24,2432]{1,0:T(8,128)(2,1)S(1)}, u32[]{:S(2)}, u32[]{:S(2)}) collective-permute-start(bf16[24,2432]{1,0:T(8,128)(2,1)S(1)} %get-tuple-element.142), channel_id=1, source_target_pairs={{0,6},{1,7},{2,4},{3,5},{4,2},{5,3},{6,0},{7,1},{8,14},{9,15},{10,... | collective-permute-start | bytes 350216 | tf_op jit(solution)/shard_map/ppermute | solution.py:31
  32.4 5.4 %collective-permute-done.4.refs_1_ = bf16[24,2432]{1,0:T(8,128)(2,1)S(1)} collective-permute-done((bf16[24,2432]{1,0:T(8,128)(2,1)S(1)}, bf16[24,2432]{1,0:T(8,128)(2,1)S(1)}, u32[]{:S(2)}, u32[]{:S(2)}) %collective-permute-start.4) | collective-permute-done | bytes 116768 | tf_op jit(solution)/shard_map/ppermute | solution.py:31
  43.8 14.5 %collective-permute-done.6.refs_1_ = bf16[4,24,2432]{2,1,0:T(8,128)(2,1)S(1)} collective-permute-done((bf16[4,24,2432]{2,1,0:T(8,128)(2,1)S(1)}, bf16[4,24,2432]{2,1,0:T(8,128)(2,1)S(1)}, u32[]{:S(2)}, u32[]{:S(2)}) %collective-permute-start.6) | collective-permute-done | bytes 466976 | tf_op jit(solution)/shard_map/ppermute | solution.py:31
  61.9 7.7 %collective-permute-done.8.refs_3_ = bf16[4,24,2432]{2,1,0:T(8,128)(2,1)S(1)} collective-permute-done((bf16[4,24,2432]{2,1,0:T(8,128)(2,1)}, bf16[4,24,2432]{2,1,0:T(8,128)(2,1)S(1)}, u32[]{:S(2)}, u32[]{:S(2)}) %collective-permute-start.8) | collective-permute-done | bytes 466976 | tf_op jit(solution)/shard_map/ppermute | solution.py:31
  72.2 4.9 %shard_map.292 = (bf16[2,2,4,2,24,2432]{5,4,3,2,1,0:T(8,128)(2,1)}, f32[16,768]{1,0:T(8,128)}) custom-call(s32[4]{0:T(128)} %pad_add_fusion.here_ref, bf16[4,24,2432]{2,1,0:T(8,128)(2,1)} %copy-done.8, bf16[4,24,2432]{2,1,0:T(8,128)(2,1)} %copy-done.9, bf16[4,24,2432]{2,1,0:T(8,128)(2,1)} %shard_map.291.refs_2_, bf16[4,24,2432]{2,1,0:T(8,128)(2,1)} %copy-done.19, ...), custom_call_target="tpu_custom_call" | custom-call | tf_op jit(solution)/shard_map/pallas_call | solution.py:156
  77.2 2.6 shard_map.296
  79.7 2.3 constant_dynamic-slice_fusion
  82.4 2.9 collective-permute-start.14
  85.2 25.1 %shard_map.293 = (bf16[3,320,768]{2,1,0:T(8,128)(2,1)}, bf16[3,320,2304]{2,1,0:T(8,128)(2,1)}, bf16[3,320,768]{2,1,0:T(8,128)(2,1)}, bf16[3,12,320,320]{3,2,1,0:T(8,128)(2,1)}, s32[3,320,1]{2,1,0:T(8,128)}) custom-call(bf16[3,88,768]{2,1,0:T(8,128)(2,1)} %get-tuple-element.128.refs_0_.refs_2_, bf16[3,88,768]{2,1,0:T(8,128)(2,1)} %copy-done.3, ...), custom_call_target="tpu_custom_call" | custom-call | flops 7172259840 | bytes 20156160 | tf_op jit(solution)/shard_map/pallas_call | solution.py:606
  112.2 11.3 %all-gather.2.cloned.1.call-done.refs_5_.u_ref.refs_4_.refs_6_.refs_7_.refs_1_ = bf16[768,6912]{1,0:T(8,128)(2,1)} async-done(((bf16[24,6912]{1,0:T(8,128)(2,1)}), bf16[768,6912]{1,0:T(8,128)(2,1)}) %all-gather.2.cloned.1.call-update) | async-done | bytes 10616848 | tf_op jit(solution)/shard_map/all_gather | solution.py:803
  123.5 6.0 %shard_map.295 = (f32[3,320,768]{2,1,0:T(8,128)}, bf16[3,320,768]{2,1,0:T(8,128)(2,1)}) custom-call(bf16[3,88,768]{2,1,0:T(8,128)(2,1)} %get-tuple-element.128.refs_0_.refs_2_, bf16[3,88,768]{2,1,0:T(8,128)(2,1)} %copy-done.3, bf16[3,88,768]{2,1,0:T(8,128)(2,1)} %copy-done.4, bf16[3,88,768]{2,1,0:T(8,128)(2,1)} %copy-done.5, ...), custom_call_target="tpu_custom_call" | custom-call | flops 1132462080 | bytes 18186240 | tf_op jit(solution)/shard_map/pallas_call | solution.py:606
  130.5 48.1 %shard_map.297 = (bf16[3,80,768]{2,1,0:T(8,128)(2,1)}, bf16[3,80,768]{2,1,0:T(8,128)(2,1)}, bf16[3,80,768]{2,1,0:T(8,128)(2,1)}, bf16[3,80,768]{2,1,0:T(8,128)(2...) custom-call(s32[4]{0:T(128)} %pad_add_fusion.here_ref, ...), custom_call_target="tpu_custom_call" | custom-call | flops 27179089920 | bytes 22118400 | tf_op jit(solution)/shard_map/pallas_call | solution.py:452
  179.2 7.8 %shard_map.298 = (f32[3,320,768]{2,1,0:T(8,128)}, bf16[3,320,768]{2,1,0:T(8,128)(2,1)}, bf16[3,320,768]{2,1,0:T(8,128)(2,1)}, f32[1,768]{1,0:T(1,128)}, f32[1,768]{1,0:T(1,128)}, /*index=5*/f32[1,768]{1,0:T(1,128)}) custom-call(f32[3,320,768]{2,1,0:T(8,128)} %get-tuple-element.80.refs_0_, ...), custom_call_target="tpu_custom_call" | custom-call | flops 1132462080 | bytes 23946240 | tf_op jit(solution)/shard_map/pallas_call | solution.py:606
  187.1 2.9 collective-permute-done.17.refs_3_.refs_2_
  190.8 5.2 %shard_map.300.refs_4_ = bf16[2,4,24,6144]{3,2,1,0:T(8,128)(2,1)} custom-call(s32[4]{0:T(128)} %pad_add_fusion.here_ref, bf16[2,4,2,24,6144]{4,3,2,1,0:T(8,128)(2,1)} %shard_map.299.refs_0_, bf16[2,4,2,24,6144]{4,3,2,1,0:T(8,128)(2,1)} %collective-permute-done.18.refs_1_), custom_call_target="tpu_custom_call" | custom-call | bytes 7077888 | tf_op jit(solution)/shard_map/pallas_call | solution.py:203
  196.2 23.1 %shard_map.301 = (bf16[3,320,2304]{2,1,0:T(8,128)(2,1)}, f32[1,768]{1,0:T(1,128)}, f32[1,768]{1,0:T(1,128)}) custom-call(bf16[3,320,2304]{2,1,0:T(8,128)(2,1)} %get-tuple-element.79.refs_0_, bf16[3,320,768]{2,1,0:T(8,128)(2,1)} %get-tuple-element.82.refs_1_, bf16[3,12,320,320]{3,2,1,0:T(8,128)(2,1)} %get-tuple-element.83.refs_2_, ...), custom_call_target="tpu_custom_call" | custom-call | flops 7549747200 | bytes 19175424 | tf_op jit(solution)/shard_map/pallas_call | solution.py:606
  219.3 10.9 %shard_map.303 = (bf16[2,192,3072]{2,1,0:T(8,128)(2,1)}, bf16[2,192,3072]{2,1,0:T(8,128)(2,1)}) custom-call(s32[4]{0:T(128)} %pad_add_fusion.here_ref, bf16[3,320,768]{2,1,0:T(8,128)(2,1)} %get-tuple-element.87.refs_0_, bf16[3,320,2304]{2,1,0:T(8,128)(2,1)} %get-tuple-element.86.refs_1_.refs_0_, ...), custom_call_target="tpu_custom_call" | custom-call | flops 4529848320 | bytes 5898240 | tf_op jit(solution)/shard_map/pallas_call | solution.py:662
  231.8 3.7 %shard_map.305.refs_8_ = bf16[1,4,24,6144]{3,2,1,0:T(8,128)(2,1)} custom-call(s32[4]{0:T(128)} %pad_add_fusion.here_ref, bf16[2,4,2,24,6144]{4,3,2,1,0:T(8,128)(2,1)} %shard_map.304.refs_0_, bf16[2,4,2,24,6144]{4,3,2,1,0:T(8,128)(2,1)} %collective-permute-done.18.refs_1_, bf16[2,4,24,6144]{3,2,1,0:T(8,128)(2,1)} %collective-permute-done.20.refs_2_), custom_call_target="tpu_custom_call" | custom-call | bytes 4718592 | tf_op jit(solution)/shard_map/pallas_call | solution.py:203
  236.8 9.4 %shard_map.306 = (bf16[3,80,768]{2,1,0:T(8,128)(2,1)}, bf16[3,80,768]{2,1,0:T(8,128)(2,1)}, bf16[3,80,768]{2,1,0:T(8,128)(2,1)}, bf16[3,80,768]{2,1,0:T(8,128)(2...) custom-call(bf16[3,320,2304]{2,1,0:T(8,128)(2,1)} %get-tuple-element.86.refs_1_.refs_0_, bf16[768,2432]{1,0:T(8,128)(2,1)} %bitcast.59, ...), custom_call_target="tpu_custom_call" | custom-call | flops 3397386240 | bytes 14260224 | tf_op jit(solution)/shard_map/pallas_call | solution.py:606
  247.7 4.4 %shard_map.308.refs_1_ = bf16[2,4,24,3072]{3,2,1,0:T(8,128)(2,1)} custom-call(s32[4]{0:T(128)} %pad_add_fusion.here_ref, bf16[2,4,2,24,3072]{4,3,2,1,0:T(8,128)(2,1)} %shard_map.307.refs_0_, bf16[2,4,2,24,3072]{4,3,2,1,0:T(8,128)(2,1)} %copy-done), custom_call_target="tpu_custom_call" | custom-call | bytes 3538944 | tf_op jit(solution)/shard_map/pallas_call | solution.py:203
  255.1 4.2 %shard_map.310 = bf16[1,4,24,6144]{3,2,1,0:T(8,128)(2,1)} custom-call(s32[4]{0:T(128)} %pad_add_fusion.here_ref, bf16[2,4,2,24,6144]{4,3,2,1,0:T(8,128)(2,1)} %shard_map.309.refs_0_, bf16[2,4,2,24,6144]{4,3,2,1,0:T(8,128)(2,1)} %collective-permute-done.18.refs_1_, bf16[2,4,24,6144]{3,2,1,0:T(8,128)(2,1)} %collective-permute-done.20.refs_2_, ...), custom_call_target="tpu_custom_call" | custom-call | bytes 5898240 | tf_op jit(solution)/shard_map/pallas_call | solution.py:203
  261.3 6.3 %collective-permute-start.31 = (bf16[24,6144]{1,0:T(8,128)(2,1)}, bf16[24,6144]{1,0:T(8,128)(2,1)}, u32[]{:S(2)}, u32[]{:S(2)}) collective-permute-start(bf16[24,6144]{1,0:T(8,128)(2,1)} %get-tuple-element.133), channel_id=1, source_target_pairs={{0,2},{1,3},{2,0},{3,1},{4,6},{5,7},{6,4},{7,5},{8,10},{9,11},{10,... | collective-permute-start | bytes 884744 | tf_op jit(solution)/shard_map/ppermute | solution.py:31
  273.4 2.9 shard_map.312.refs_4_
  280.2 7.5 %all-to-all-start = ((bf16[32,24,128]{2,1,0:T(8,128)(2,1)}), bf16[32,24,128]{2,1,0:T(8,128)(2,1)S(1)}, u32[]{:S(2)}, u32[]{:S(2)}) async-start(bf16[32,24,128]{2,1,0:T(8,128)(2,1)} %bitcast.62), calls=%async_computation | async-start | bytes 393216 | tf_op jit(solution)/shard_map/all_to_all | solution.py:871
  288.4 3.8 %shard_map.314 = bf16[12,80,768]{2,1,0:T(8,128)(2,1)} custom-call(s32[4]{0:T(128)} %pad_add_fusion.here_ref, bf16[3,80,768]{2,1,0:T(8,128)(2,1)} %get-tuple-element.93.refs_0_, bf16[3,80,768]{2,1,0:T(8,128)(2,1)} %get-tuple-element.94.refs_1_, bf16[3,80,768]{2,1,0:T(8,128)(2,1)} %get-tuple-element.95.refs_2_, bf16[3,80,768]{2,1,0:T(8,128)(2,1)} %get-tuple-element.96.refs_3_), custom_call_target="tpu_custom_call" | custom-call | tf_op jit(solution)/shard_map/pallas_call | solution.py:713
  298.0 3.2 shard_map.316
  302.2 6.4 %collective-permute-start.28 = (bf16[24,3072]{1,0:T(8,128)(2,1)S(1)}, bf16[24,3072]{1,0:T(8,128)(2,1)S(1)}, u32[]{:S(2)}, u32[]{:S(2)}) collective-permute-start(bf16[24,3072]{1,0:T(8,128)(2,1)S(1)} %get-tuple-element.138), channel_id=1, source_target_pairs={{0,2},{1,3},{2,0},{3,1},{4,6},{5,7},{6,4},{7,5},{8,10},{9,11},{10,... | collective-permute-start | bytes 442376 | tf_op jit(solution)/shard_map/ppermute | solution.py:31
  313.5 4.1 %shard_map.318 = f32[12,80,768]{2,1,0:T(8,128)} custom-call(s32[4]{0:T(128)} %pad_add_fusion.here_ref, bf16[3,80,768]{2,1,0:T(8,128)(2,1)} %get-tuple-element.105.refs_0_, bf16[3,80,768]{2,1,0:T(8,128)(2,1)} %get-tuple-element.106.refs_1_, bf16[3,80,768]{2,1,0:T(8,128)(2,1)} %get-tuple-element.107.refs_2_, bf16[3,80,768]{2,1,0:T(8,128)(2,1)} %get-tuple-element.108.refs_3_), custom_call_target="tpu_custom_call" | custom-call | tf_op jit(solution)/shard_map/pallas_call | solution.py:713
  317.6 3.3 %collective-permute-done.29 = bf16[24,3072]{1,0:T(8,128)(2,1)S(1)} collective-permute-done((bf16[24,3072]{1,0:T(8,128)(2,1)S(1)}, bf16[24,3072]{1,0:T(8,128)(2,1)S(1)}, u32[]{:S(2)}, u32[]{:S(2)}) %collective-permute-start.29) | collective-permute-done | bytes 147488 | tf_op jit(solution)/shard_map/ppermute | solution.py:31
  (167 shorter events, 61.8 us)
Async XLA Ops:
  7.2 116.3 %all-gather.2.cloned.1.call-start = ((), (), s32[]{:S(2)}) async-start(), calls=%async_computation.1 | async-start | bytes 10948608 | tf_op jit(solution)/shard_map/all_gather | solution.py:803
  13.3 24.6 %collective-permute-start = (bf16[3,88,768]{2,1,0:T(8,128)(2,1)S(1)}, bf16[3,88,768]{2,1,0:T(8,128)(2,1)S(1)}, u32[]{:S(2)}, u32[]{:S(2)}) collective-permute-start(bf16[3,88,768]{2,1,0:T(8,128)(2,1)S(1)} %get-tuple-element.127), channel_id=1, source_target_pairs={{0,8},{1,9},{2,10},{3,11},{4,12},{5,13},{6,14},{7,15},{8,0},{9,1},... | collective-permute-start | bytes 1216520 | tf_op jit(solution)/shard_map/ppermute | solution.py:31
  13.7 24.2 %collective-permute-start.1 = (bf16[3,88,768]{2,1,0:T(8,128)(2,1)S(1)}, bf16[3,88,768]{2,1,0:T(8,128)(2,1)S(1)}, u32[]{:S(2)}, u32[]{:S(2)}) collective-permute-start(bf16[3,88,768]{2,1,0:T(8,128)(2,1)S(1)} %get-tuple-element.126), channel_id=1, source_target_pairs={{0,16},{1,17},{2,18},{3,19},{4,20},{5,21},{6,22},{7,23},{8,24},{9,... | collective-permute-start | bytes 1216520 | tf_op jit(solution)/shard_map/ppermute | solution.py:31
  16.2 21.7 %collective-permute-start.2 = (bf16[3,88,768]{2,1,0:T(8,128)(2,1)S(1)}, bf16[3,88,768]{2,1,0:T(8,128)(2,1)S(1)}, u32[]{:S(2)}, u32[]{:S(2)}) collective-permute-start(bf16[3,88,768]{2,1,0:T(8,128)(2,1)S(1)} %get-tuple-element.125), channel_id=1, source_target_pairs={{0,24},{1,25},{2,26},{3,27},{4,28},{5,29},{6,30},{7,31},{8,16},{9,... | collective-permute-start | bytes 1216520 | tf_op jit(solution)/shard_map/ppermute | solution.py:31
  21.1 16.7 %collective-permute-start.4 = (bf16[24,2432]{1,0:T(8,128)(2,1)S(1)}, bf16[24,2432]{1,0:T(8,128)(2,1)S(1)}, u32[]{:S(2)}, u32[]{:S(2)}) collective-permute-start(bf16[24,2432]{1,0:T(8,128)(2,1)S(1)} %get-tuple-element.142), channel_id=1, source_target_pairs={{0,4},{1,5},{2,6},{3,7},{4,0},{5,1},{6,2},{7,3},{8,12},{9,13},{10,... | collective-permute-start | bytes 350216 | tf_op jit(solution)/shard_map/ppermute | solution.py:31
  26.5 11.3 %collective-permute-start.5 = (bf16[24,2432]{1,0:T(8,128)(2,1)S(1)}, bf16[24,2432]{1,0:T(8,128)(2,1)S(1)}, u32[]{:S(2)}, u32[]{:S(2)}) collective-permute-start(bf16[24,2432]{1,0:T(8,128)(2,1)S(1)} %get-tuple-element.142), channel_id=1, source_target_pairs={{0,6},{1,7},{2,4},{3,5},{4,2},{5,3},{6,0},{7,1},{8,14},{9,15},{10,... | collective-permute-start | bytes 350216 | tf_op jit(solution)/shard_map/ppermute | solution.py:31
  40.7 17.6 %collective-permute-start.6 = (bf16[4,24,2432]{2,1,0:T(8,128)(2,1)S(1)}, bf16[4,24,2432]{2,1,0:T(8,128)(2,1)S(1)}, u32[]{:S(2)}, u32[]{:S(2)}) collective-permute-start(bf16[4,24,2432]{2,1,0:T(8,128)(2,1)S(1)} %pad_maximum_fusion.refs_0_), channel_id=1, source_target_pairs={{0,1},{1,0},{2,3},{3,2},{4,5},{5,4},{6,7},{7,6},{8,24},{9,25},{10,... | collective-permute-start | bytes 1400840 | tf_op jit(solution)/shard_map/ppermute | solution.py:31
  42.3 17.7 %collective-permute-start.7 = (bf16[4,24,2432]{2,1,0:T(8,128)(2,1)S(1)}, bf16[4,24,2432]{2,1,0:T(8,128)(2,1)S(1)}, u32[]{:S(2)}, u32[]{:S(2)}) collective-permute-start(bf16[4,24,2432]{2,1,0:T(8,128)(2,1)S(1)} %pad_maximum_fusion.refs_0_), channel_id=1, source_target_pairs={{0,16},{1,17},{2,18},{3,19},{4,20},{5,21},{6,22},{7,23},{8,9},{9,8... | collective-permute-start | bytes 1400840 | tf_op jit(solution)/shard_map/ppermute | solution.py:31
  60.8 8.8 %collective-permute-start.8 = (bf16[4,24,2432]{2,1,0:T(8,128)(2,1)}, bf16[4,24,2432]{2,1,0:T(8,128)(2,1)S(1)}, u32[]{:S(2)}, u32[]{:S(2)}) collective-permute-start(bf16[4,24,2432]{2,1,0:T(8,128)(2,1)} %shard_map.291.refs_2_), channel_id=1, source_target_pairs={{0,1},{1,0},{2,3},{3,2},{4,5},{5,4},{6,7},{7,6},{8,24},{9,25},{10,... | collective-permute-start | bytes 1400840 | tf_op jit(solution)/shard_map/ppermute | solution.py:31
  61.4 8.9 %collective-permute-start.9 = (bf16[4,24,2432]{2,1,0:T(8,128)(2,1)S(1)}, bf16[4,24,2432]{2,1,0:T(8,128)(2,1)S(1)}, u32[]{:S(2)}, u32[]{:S(2)}) collective-permute-start(bf16[4,24,2432]{2,1,0:T(8,128)(2,1)S(1)} %pad_maximum_fusion.refs_0_), channel_id=1, source_target_pairs={{0,8},{1,9},{2,10},{3,11},{4,12},{5,13},{6,14},{7,15},{8,0},{9,1},... | collective-permute-start | bytes 1400840 | tf_op jit(solution)/shard_map/ppermute | solution.py:31
  61.4 8.9 %collective-permute-start.11 = (bf16[4,24,2432]{2,1,0:T(8,128)(2,1)}, bf16[4,24,2432]{2,1,0:T(8,128)(2,1)S(1)}, u32[]{:S(2)}, u32[]{:S(2)}) collective-permute-start(bf16[4,24,2432]{2,1,0:T(8,128)(2,1)} %shard_map.291.refs_2_), channel_id=1, source_target_pairs={{0,8},{1,9},{2,10},{3,11},{4,12},{5,13},{6,14},{7,15},{8,0},{9,1},... | collective-permute-start | bytes 1400840 | tf_op jit(solution)/shard_map/ppermute | solution.py:31
  82.0 47.5 %collective-permute-start.13 = (bf16[3,80,768]{2,1,0:T(8,128)(2,1)S(1)}, bf16[3,80,768]{2,1,0:T(8,128)(2,1)S(1)}, u32[]{:S(2)}, u32[]{:S(2)}) collective-permute-start(bf16[3,80,768]{2,1,0:T(8,128)(2,1)S(1)} %get-tuple-element.131), channel_id=1, source_target_pairs={{0,8},{1,9},{2,10},{3,11},{4,12},{5,13},{6,14},{7,15},{8,0},{9,1},... | collective-permute-start | bytes 1105928 | tf_op jit(solution)/shard_map/ppermute | solution.py:31
  82.4 47.1 %collective-permute-start.14 = (bf16[3,80,768]{2,1,0:T(8,128)(2,1)S(1)}, bf16[3,80,768]{2,1,0:T(8,128)(2,1)S(1)}, u32[]{:S(2)}, u32[]{:S(2)}) collective-permute-start(bf16[3,80,768]{2,1,0:T(8,128)(2,1)S(1)} %get-tuple-element.130), channel_id=1, source_target_pairs={{0,16},{1,17},{2,18},{3,19},{4,20},{5,21},{6,22},{7,23},{8,24},{9,... | collective-permute-start | bytes 1105928 | tf_op jit(solution)/shard_map/ppermute | solution.py:31
  85.2 44.3 %collective-permute-start.15 = (bf16[3,80,768]{2,1,0:T(8,128)(2,1)S(1)}, bf16[3,80,768]{2,1,0:T(8,128)(2,1)S(1)}, u32[]{:S(2)}, u32[]{:S(2)}) collective-permute-start(bf16[3,80,768]{2,1,0:T(8,128)(2,1)S(1)} %get-tuple-element.129), channel_id=1, source_target_pairs={{0,24},{1,25},{2,26},{3,27},{4,28},{5,29},{6,30},{7,31},{8,16},{9,... | collective-permute-start | bytes 1105928 | tf_op jit(solution)/shard_map/ppermute | solution.py:31
  178.7 12.1 %collective-permute-start.18 = (bf16[2,4,2,24,6144]{4,3,2,1,0:T(8,128)(2,1)}, bf16[2,4,2,24,6144]{4,3,2,1,0:T(8,128)(2,1)}, u32[]{:S(2)}, u32[]{:S(2)}) collective-permute-start(bf16[2,4,2,24,6144]{4,3,2,1,0:T(8,128)(2,1)} %bitcast.75), channel_id=1, source_target_pairs={{0,8},{1,9},{2,10},{3,11},{4,12},{5,13},{6,14},{7,15},{8,0},{9,1},... | collective-permute-start | bytes 14155784 | tf_op jit(solution)/shard_map/ppermute | solution.py:31
  179.2 10.8 %collective-permute-start.17 = (bf16[3,80,768]{2,1,0:T(8,128)(2,1)}, bf16[3,80,768]{2,1,0:T(8,128)(2,1)S(1)}, u32[]{:S(2)}, u32[]{:S(2)}) collective-permute-start(bf16[3,80,768]{2,1,0:T(8,128)(2,1)} %get-tuple-element.77), channel_id=1, source_target_pairs={{0,16},{1,17},{2,18},{3,19},{4,20},{5,21},{6,22},{7,23},{8,24},{9,... | collective-permute-start | bytes 1105928 | tf_op jit(solution)/shard_map/ppermute | solution.py:31
  195.9 35.9 %collective-permute-start.20 = (bf16[2,4,24,6144]{3,2,1,0:T(8,128)(2,1)}, bf16[2,4,24,6144]{3,2,1,0:T(8,128)(2,1)}, u32[]{:S(2)}, u32[]{:S(2)}) collective-permute-start(bf16[2,4,24,6144]{3,2,1,0:T(8,128)(2,1)} %shard_map.300.refs_4_), channel_id=1, source_target_pairs={{0,16},{1,17},{2,18},{3,19},{4,20},{5,21},{6,22},{7,23},{8,9},{9,8... | collective-permute-start | bytes 7077896 | tf_op jit(solution)/shard_map/ppermute | solution.py:31
  230.2 16.1 %collective-permute-start.21 = (bf16[2,4,2,24,3072]{4,3,2,1,0:T(8,128)(2,1)}, bf16[2,4,2,24,3072]{4,3,2,1,0:T(8,128)(2,1)S(1)}, u32[]{:S(2)}, u32[]{:S(2)}) collective-permute-start(bf16[2,4,2,24,3072]{4,3,2,1,0:T(8,128)(2,1)} %bitcast.76), channel_id=1, source_target_pairs={{0,8},{1,9},{2,10},{3,11},{4,12},{5,13},{6,14},{7,15},{8,0},{9,1},... | collective-permute-start | bytes 7077896 | tf_op jit(solution)/shard_map/ppermute | solution.py:31
  235.5 19.6 %collective-permute-start.22 = (bf16[1,4,24,6144]{3,2,1,0:T(8,128)(2,1)}, bf16[1,4,24,6144]{3,2,1,0:T(8,128)(2,1)}, u32[]{:S(2)}, u32[]{:S(2)}) collective-permute-start(bf16[1,4,24,6144]{3,2,1,0:T(8,128)(2,1)} %shard_map.305.refs_8_), channel_id=1, source_target_pairs={{0,1},{1,0},{2,3},{3,2},{4,5},{5,4},{6,7},{7,6},{8,24},{9,25},{10,... | collective-permute-start | bytes 3538952 | tf_op jit(solution)/shard_map/ppermute | solution.py:31
  236.8 50.9 %collective-permute-start.19 = (bf16[3,80,768]{2,1,0:T(8,128)(2,1)}, bf16[3,80,768]{2,1,0:T(8,128)(2,1)S(1)}, u32[]{:S(2)}, u32[]{:S(2)}) collective-permute-start(bf16[3,80,768]{2,1,0:T(8,128)(2,1)} %shard_map.302), channel_id=1, source_target_pairs={{0,24},{1,25},{2,26},{3,27},{4,28},{5,29},{6,30},{7,31},{8,16},{9,... | collective-permute-start | bytes 1105928 | tf_op jit(solution)/shard_map/ppermute | solution.py:31
  253.3 19.0 %collective-permute-start.23 = (bf16[2,4,24,3072]{3,2,1,0:T(8,128)(2,1)S(1)}, bf16[2,4,24,3072]{3,2,1,0:T(8,128)(2,1)S(1)}, u32[]{:S(2)}, u32[]{:S(2)}) collective-permute-start(bf16[2,4,24,3072]{3,2,1,0:T(8,128)(2,1)S(1)} %copy-done.2), channel_id=1, source_target_pairs={{0,16},{1,17},{2,18},{3,19},{4,20},{5,21},{6,22},{7,23},{8,9},{9,8... | collective-permute-start | bytes 3538952 | tf_op jit(solution)/shard_map/ppermute | solution.py:31
  261.3 30.9 %collective-permute-start.31 = (bf16[24,6144]{1,0:T(8,128)(2,1)}, bf16[24,6144]{1,0:T(8,128)(2,1)}, u32[]{:S(2)}, u32[]{:S(2)}) collective-permute-start(bf16[24,6144]{1,0:T(8,128)(2,1)} %get-tuple-element.133), channel_id=1, source_target_pairs={{0,2},{1,3},{2,0},{3,1},{4,6},{5,7},{6,4},{7,5},{8,10},{9,11},{10,... | collective-permute-start | bytes 884744 | tf_op jit(solution)/shard_map/ppermute | solution.py:31
  267.7 26.4 %collective-permute-start.32 = (bf16[24,6144]{1,0:T(8,128)(2,1)}, bf16[24,6144]{1,0:T(8,128)(2,1)}, u32[]{:S(2)}, u32[]{:S(2)}) collective-permute-start(bf16[24,6144]{1,0:T(8,128)(2,1)} %get-tuple-element.135), channel_id=1, source_target_pairs={{0,4},{1,5},{2,6},{3,7},{4,0},{5,1},{6,2},{7,3},{8,12},{9,13},{10,... | collective-permute-start | bytes 884744 | tf_op jit(solution)/shard_map/ppermute | solution.py:31
  268.2 25.9 %collective-permute-start.33 = (bf16[24,6144]{1,0:T(8,128)(2,1)}, bf16[24,6144]{1,0:T(8,128)(2,1)}, u32[]{:S(2)}, u32[]{:S(2)}) collective-permute-start(bf16[24,6144]{1,0:T(8,128)(2,1)} %get-tuple-element.134), channel_id=1, source_target_pairs={{0,6},{1,7},{2,4},{3,5},{4,2},{5,3},{6,0},{7,1},{8,14},{9,15},{10,... | collective-permute-start | bytes 884744 | tf_op jit(solution)/shard_map/ppermute | solution.py:31
  276.4 20.8 %collective-permute-start.27 = (bf16[1,4,24,3072]{3,2,1,0:T(8,128)(2,1)}, bf16[1,4,24,3072]{3,2,1,0:T(8,128)(2,1)S(1)}, u32[]{:S(2)}, u32[]{:S(2)}) collective-permute-start(bf16[1,4,24,3072]{3,2,1,0:T(8,128)(2,1)} %shard_map.312.refs_4_), channel_id=1, source_target_pairs={{0,1},{1,0},{2,3},{3,2},{4,5},{5,4},{6,7},{7,6},{8,24},{9,25},{10,... | collective-permute-start | bytes 1769480 | tf_op jit(solution)/shard_map/ppermute | solution.py:31
  280.2 30.9 %all-to-all-start = ((bf16[32,24,128]{2,1,0:T(8,128)(2,1)}), bf16[32,24,128]{2,1,0:T(8,128)(2,1)S(1)}, u32[]{:S(2)}, u32[]{:S(2)}) async-start(bf16[32,24,128]{2,1,0:T(8,128)(2,1)} %bitcast.62), calls=%async_computation | async-start | bytes 393216 | tf_op jit(solution)/shard_map/all_to_all | solution.py:871
  287.7 21.5 %collective-permute-start.24 = (bf16[3,80,768]{2,1,0:T(8,128)(2,1)}, bf16[3,80,768]{2,1,0:T(8,128)(2,1)S(1)}, u32[]{:S(2)}, u32[]{:S(2)}) collective-permute-start(bf16[3,80,768]{2,1,0:T(8,128)(2,1)} %get-tuple-element.102), channel_id=1, source_target_pairs={{0,8},{1,9},{2,10},{3,11},{4,12},{5,13},{6,14},{7,15},{8,0},{9,1},... | collective-permute-start | bytes 1105928 | tf_op jit(solution)/shard_map/ppermute | solution.py:31
  292.3 20.3 %collective-permute-start.25 = (bf16[3,80,768]{2,1,0:T(8,128)(2,1)S(1)}, bf16[3,80,768]{2,1,0:T(8,128)(2,1)S(1)}, u32[]{:S(2)}, u32[]{:S(2)}) collective-permute-start(bf16[3,80,768]{2,1,0:T(8,128)(2,1)S(1)} %copy-done.24), channel_id=1, source_target_pairs={{0,16},{1,17},{2,18},{3,19},{4,20},{5,21},{6,22},{7,23},{8,24},{9,... | collective-permute-start | bytes 1105928 | tf_op jit(solution)/shard_map/ppermute | solution.py:31
  294.1 18.5 %collective-permute-start.26 = (bf16[3,80,768]{2,1,0:T(8,128)(2,1)}, bf16[3,80,768]{2,1,0:T(8,128)(2,1)S(1)}, u32[]{:S(2)}, u32[]{:S(2)}) collective-permute-start(bf16[3,80,768]{2,1,0:T(8,128)(2,1)} %get-tuple-element.104), channel_id=1, source_target_pairs={{0,24},{1,25},{2,26},{3,27},{4,28},{5,29},{6,30},{7,31},{8,16},{9,... | collective-permute-start | bytes 1105928 | tf_op jit(solution)/shard_map/ppermute | solution.py:31
  302.2 15.4 %collective-permute-start.28 = (bf16[24,3072]{1,0:T(8,128)(2,1)S(1)}, bf16[24,3072]{1,0:T(8,128)(2,1)S(1)}, u32[]{:S(2)}, u32[]{:S(2)}) collective-permute-start(bf16[24,3072]{1,0:T(8,128)(2,1)S(1)} %get-tuple-element.138), channel_id=1, source_target_pairs={{0,2},{1,3},{2,0},{3,1},{4,6},{5,7},{6,4},{7,5},{8,10},{9,11},{10,... | collective-permute-start | bytes 442376 | tf_op jit(solution)/shard_map/ppermute | solution.py:31
  308.6 12.4 %collective-permute-start.29 = (bf16[24,3072]{1,0:T(8,128)(2,1)S(1)}, bf16[24,3072]{1,0:T(8,128)(2,1)S(1)}, u32[]{:S(2)}, u32[]{:S(2)}) collective-permute-start(bf16[24,3072]{1,0:T(8,128)(2,1)S(1)} %get-tuple-element.140), channel_id=1, source_target_pairs={{0,4},{1,5},{2,6},{3,7},{4,0},{5,1},{6,2},{7,3},{8,12},{9,13},{10,... | collective-permute-start | bytes 442376 | tf_op jit(solution)/shard_map/ppermute | solution.py:31
  309.2 11.7 %collective-permute-start.30 = (bf16[24,3072]{1,0:T(8,128)(2,1)S(1)}, bf16[24,3072]{1,0:T(8,128)(2,1)S(1)}, u32[]{:S(2)}, u32[]{:S(2)}) collective-permute-start(bf16[24,3072]{1,0:T(8,128)(2,1)S(1)} %get-tuple-element.139), channel_id=1, source_target_pairs={{0,6},{1,7},{2,4},{3,5},{4,2},{5,3},{6,0},{7,1},{8,14},{9,15},{10,... | collective-permute-start | bytes 442376 | tf_op jit(solution)/shard_map/ppermute | solution.py:31
  (35 other events, 128.3 us)
Sparse Core Ops, SparseCore 0:
  10.9 112.5 all-gather.1
